TPU v7x, 32 devices: a whole 2x2x4 slice. The times are simulated.
32 devices in a mesh: replica: 4 (over x, core), fsdp: 4 (over z), tensor: 2 (over y).
Axes of the slice: x: 2, y: 2, z: 4, core: 2. Of those that a mesh axis runs over, the one named last changes fastest.
Arguments:
- images: bfloat16 [96, 729, 1152], P(('replica', 'fsdp')), may hold values from -6 to 6
- live: int32 [96], P(('replica', 'fsdp')), may hold values 0 or 1
- cotangent: bfloat16 [96, 729, 1152], P(('replica', 'fsdp')), may hold values from -6 to 6
- ln1_gain: float32 [1152], replicated, may hold values from 0.1 to 1.9
- ln1_bias: float32 [1152], replicated, may hold values from -3 to 3
- q_weight: float32 [1152, 1152], P('fsdp', 'tensor'), may hold values from -0.25 to 0.25
- q_bias: float32 [1152], replicated, may hold values from -3 to 3
- k_weight: float32 [1152, 1152], P('fsdp', 'tensor'), may hold values from -0.25 to 0.25
- v_weight: float32 [1152, 1152], P('fsdp', 'tensor'), may hold values from -0.1875 to 0.1875
- v_bias: float32 [1152], replicated, may hold values from -3 to 3
- o_weight: float32 [1152, 1152], P('tensor', 'fsdp'), may hold values from -0.75 to 0.75
- o_bias: float32 [1152], replicated, may hold values from -3 to 3
- ln2_gain: float32 [1152], replicated, may hold values from 0.1 to 1.9
- ln2_bias: float32 [1152], replicated, may hold values from -3 to 3
- fc1_weight: float32 [1152, 4304], P('fsdp', 'tensor'), may hold values from -1 to 1
- fc1_bias: float32 [4304], replicated, may hold values from -3 to 3
- fc2_weight: float32 [4304, 1152], P('tensor', 'fsdp'), may hold values from -0.09375 to 0.09375
- fc2_bias: float32 [1152], replicated, may hold values from -3 to 3
Outputs:
- output: bfloat16 [96, 729, 1152], P(('replica', 'fsdp'))
- input_grad: bfloat16 [96, 729, 1152], P(('replica', 'fsdp'))
- ln1_gain_grad: float32 [1152], P('tensor')
- ln1_bias_grad: float32 [1152], P('tensor')
- q_weight_grad: float32 [1152, 1152], P('fsdp', 'tensor')
- q_bias_grad: float32 [1152], P('tensor')
- k_weight_grad: float32 [1152, 1152], P('fsdp', 'tensor')
- v_weight_grad: float32 [1152, 1152], P('fsdp', 'tensor')
- v_bias_grad: float32 [1152], P('tensor')
- o_weight_grad: float32 [1152, 1152], P('tensor', 'fsdp')
- o_bias_grad: float32 [1152], P('tensor')
- ln2_gain_grad: float32 [1152], P('tensor')
- ln2_bias_grad: float32 [1152], P('tensor')
- fc1_weight_grad: float32 [1152, 4304], P('fsdp', 'tensor')
- fc1_bias_grad: float32 [4304], P('tensor')
- fc2_weight_grad: float32 [4304, 1152], P('tensor', 'fsdp')
- fc2_bias_grad: float32 [1152], P('tensor')
Inputs may be any that keep to these rules, and one draw needn't show every extreme that they name: `live`: 1 marks a slot that holds an image, 0 an empty slot.
All inputs are finite; a program needn't handle non-finite values. No bound on the sum of `live` on one device may be relied on, other than what follows from the above.
Results may differ from a plain program's by a relative error of at most 0.018.
Values may be sent and summed in bfloat16 or wider, within the bound.
No kernel may reach another device: no remote copies, remote signals or barrier semaphores. Data moves between devices by JAX's collectives and lax.ppermute only.
A program may use at most 640 MiB of HBM per device.

v0:
```python
import jax
import jax.numpy as jnp
from jax import lax
from jax.sharding import PartitionSpec as P

HEAD = 72
MB = 2
SLOTS = 3


EPSILON = 1e-06


def matmul(first_op, second_op):
    return jnp.dot(first_op, second_op, preferred_element_type=jnp.float32)


def matmul_tn(first_op, second_op):
    return lax.dot_general(
        first_op, second_op, (((0,), (0,)), ((), ())), preferred_element_type=jnp.float32
    )


def matmul_nt(first_op, second_op):
    return lax.dot_general(
        first_op, second_op, (((1,), (1,)), ((), ())), preferred_element_type=jnp.float32
    )


def gelu_tanh(values):
    return jax.nn.gelu(values, approximate=True)


def row_totals(first_sum, second_sum):
    return lax.psum((first_sum, second_sum), "tensor")


def spread_whole(rounded):
    return lax.all_gather(rounded, "tensor", axis=1, tiled=True)


def combine_parts(partial_value):
    return lax.psum_scatter(partial_value, "tensor", scatter_dimension=1, tiled=True)


def normalize(stream, gain_vec, shift_vec):
    full_width = stream.shape[1] * lax.axis_size("tensor")
    totals = row_totals(
        jnp.sum(stream, axis=1, keepdims=True), jnp.sum(stream * stream, axis=1, keepdims=True)
    )
    center = totals[0] / full_width
    spread = totals[1] / full_width - center * center
    scale_inv = lax.rsqrt(spread + EPSILON)
    normed = (stream - center) * scale_inv
    rounded = (normed * gain_vec + shift_vec).astype(jnp.bfloat16)
    return (spread_whole(rounded), normed, scale_inv)


def norm_back(grad_part, normed, scale_inv, gain_vec):
    scaled = grad_part * gain_vec
    full_width = grad_part.shape[1] * lax.axis_size("tensor")
    totals = row_totals(
        jnp.sum(scaled, axis=1, keepdims=True), jnp.sum(scaled * normed, axis=1, keepdims=True)
    )
    mean_one = totals[0] / full_width
    mean_two = totals[1] / full_width
    return scale_inv * (scaled - mean_one - normed * mean_two)


def score_block(queries, key_rows):
    return jnp.einsum("bqhd,bkhd->bhqk", queries, key_rows, preferred_element_type=jnp.float32)


def forward_pass(stream, row_mask, weights, vectors, sizes_info):
    q_full, k_full, v_full, o_full, up_full, down_full = weights
    gain_one, shift_one, q_shift, v_shift, o_shift, gain_two, shift_two, up_shift, down_shift = (
        vectors
    )
    blocks, length, row_count, padded_rows = sizes_info
    head_count = q_shift.shape[0] // HEAD
    shape_four = (blocks, length, head_count, HEAD)
    first, normed_one, inv_one = normalize(stream, gain_one, shift_one)
    queries = (
        ((matmul(first, q_full) + q_shift) * HEAD ** (-0.5))
        .astype(jnp.bfloat16)
        .reshape(shape_four)
    )
    key_rows = matmul(first, k_full).astype(jnp.bfloat16).reshape(shape_four)
    value_rows = (matmul(first, v_full) + v_shift).astype(jnp.bfloat16).reshape(shape_four)
    scores = score_block(queries, key_rows)
    top_score = jnp.max(scores, axis=-1, keepdims=True)
    log_total = top_score + jnp.log(jnp.sum(jnp.exp(scores - top_score), axis=-1, keepdims=True))
    probs_bf = jnp.exp(scores - log_total).astype(jnp.bfloat16)
    attended = jnp.einsum(
        "bhqk,bkhd->bqhd", probs_bf, value_rows, preferred_element_type=jnp.float32
    )
    attended_bf = attended.reshape(row_count, head_count * HEAD).astype(jnp.bfloat16)
    middle = stream + combine_parts(matmul(attended_bf, o_full)) + o_shift
    second, normed_two, inv_two = normalize(middle, gain_two, shift_two)
    upper_pre = matmul(second, up_full) + up_shift
    hidden = gelu_tanh(upper_pre).astype(jnp.bfloat16)
    result = middle + combine_parts(matmul(hidden, down_full)) + down_shift
    output = (result * row_mask).astype(jnp.bfloat16)
    kept_state = (
        first,
        normed_one,
        inv_one,
        queries,
        key_rows,
        value_rows,
        log_total,
        attended_bf,
        normed_two,
        inv_two,
        second,
        upper_pre,
        hidden,
    )
    return (output, kept_state)


def backward_pass(cot_stream, row_mask, weights, vectors, kept_state, sizes_info):
    q_full, k_full, v_full, o_full, up_full, down_full = weights
    gain_one, shift_one, q_shift, v_shift, o_shift, gain_two, shift_two, up_shift, down_shift = (
        vectors
    )
    (
        first,
        normed_one,
        inv_one,
        queries,
        key_rows,
        value_rows,
        log_total,
        attended_bf,
        normed_two,
        inv_two,
        second,
        upper_pre,
        hidden,
    ) = kept_state
    blocks, length, row_count, padded_rows = sizes_info
    shape_four = queries.shape
    out_grad = cot_stream.astype(jnp.float32) * row_mask
    out_whole = spread_whole(out_grad.astype(jnp.bfloat16))
    down_grad = matmul_tn(hidden, out_whole)
    hidden_grad = matmul_nt(out_whole, down_full)
    upper_grad = jax.vjp(gelu_tanh, upper_pre)[1](hidden_grad)[0].astype(jnp.bfloat16)
    up_grad = matmul_tn(second, upper_grad)
    second_grad = combine_parts(matmul_nt(upper_grad, up_full))
    middle_grad = out_grad + norm_back(second_grad, normed_two, inv_two, gain_two)
    middle_bf = middle_grad.astype(jnp.bfloat16)
    middle_whole = spread_whole(middle_bf)
    o_grad = matmul_tn(attended_bf, middle_whole)
    attended_grad = matmul_nt(middle_whole, o_full).astype(jnp.bfloat16).reshape(shape_four)
    scores = score_block(queries, key_rows)
    probs = jnp.exp(scores - log_total)
    probs_bf = probs.astype(jnp.bfloat16)
    prob_grad = jnp.einsum(
        "bqhd,bkhd->bhqk", attended_grad, value_rows, preferred_element_type=jnp.float32
    )
    value_grad = jnp.einsum(
        "bhqk,bqhd->bkhd", probs_bf, attended_grad, preferred_element_type=jnp.float32
    )
    value_grad = value_grad.reshape(row_count, -1).astype(jnp.bfloat16)
    row_dot = jnp.sum(prob_grad * probs, axis=-1, keepdims=True)
    score_grad = (probs * (prob_grad - row_dot)).astype(jnp.bfloat16)
    query_grad = jnp.einsum(
        "bhqk,bkhd->bqhd", score_grad, key_rows, preferred_element_type=jnp.float32
    )
    query_grad = (query_grad.reshape(row_count, -1) * HEAD ** (-0.5)).astype(jnp.bfloat16)
    key_grad = jnp.einsum(
        "bhqk,bqhd->bkhd", score_grad, queries, preferred_element_type=jnp.float32
    )
    key_grad = key_grad.reshape(row_count, -1).astype(jnp.bfloat16)
    first_grad = combine_parts(
        matmul_nt(query_grad, q_full) + matmul_nt(key_grad, k_full) + matmul_nt(value_grad, v_full)
    )
    input_grad = middle_grad + norm_back(first_grad, normed_one, inv_one, gain_one)
    matrices = (
        matmul_tn(first, query_grad),
        matmul_tn(first, key_grad),
        matmul_tn(first, value_grad),
        o_grad,
        up_grad,
        down_grad,
    )
    vector_grads = (
        jnp.sum(first_grad * normed_one, axis=0),
        jnp.sum(first_grad, axis=0),
        jnp.sum(query_grad, axis=0, dtype=jnp.float32),
        jnp.sum(value_grad, axis=0, dtype=jnp.float32),
        jnp.sum(middle_bf, axis=0, dtype=jnp.float32),
        jnp.sum(second_grad * normed_two, axis=0),
        jnp.sum(second_grad, axis=0),
        jnp.sum(upper_grad, axis=0, dtype=jnp.float32),
        jnp.sum(out_grad, axis=0),
    )
    return (input_grad.astype(jnp.bfloat16), matrices, vector_grads)


def body(
    images,
    live,
    cotangent,
    ln1_gain,
    ln1_bias,
    q_weight,
    q_bias,
    k_weight,
    v_weight,
    v_bias,
    o_weight,
    o_bias,
    ln2_gain,
    ln2_bias,
    fc1_weight,
    fc1_bias,
    fc2_weight,
    fc2_bias,
):
    tensor_count = lax.axis_size("tensor")
    tensor_rank = lax.axis_index("tensor")
    length = images.shape[1]
    full_width = images.shape[2]
    part_width = full_width // tensor_count
    feature_start = tensor_rank * part_width
    head_width = q_bias.shape[0] // tensor_count
    head_start = tensor_rank * head_width
    unit_width = fc1_bias.shape[0] // tensor_count
    unit_start = tensor_rank * unit_width
    row_count = SLOTS * length
    row_share = (row_count + tensor_count - 1) // tensor_count
    padded_rows = row_share * tensor_count
    sizes_info = (SLOTS, length, row_count, padded_rows)
    q_shift = lax.dynamic_slice_in_dim(q_bias, head_start, head_width, 0)
    v_shift = lax.dynamic_slice_in_dim(v_bias, head_start, head_width, 0)
    up_shift = lax.dynamic_slice_in_dim(fc1_bias, unit_start, unit_width, 0)
    gain_one, shift_one, o_shift, gain_two, shift_two, down_shift = tuple(
        (
            lax.dynamic_slice_in_dim(vector, feature_start, part_width, 0)
            for vector in (ln1_gain, ln1_bias, o_bias, ln2_gain, ln2_bias, fc2_bias)
        )
    )
    vectors = (
        gain_one,
        shift_one,
        q_shift,
        v_shift,
        o_shift,
        gain_two,
        shift_two,
        up_shift,
        down_shift,
    )
    q_low = q_weight.astype(jnp.bfloat16)
    k_low = k_weight.astype(jnp.bfloat16)
    v_low = v_weight.astype(jnp.bfloat16)
    o_low = o_weight.astype(jnp.bfloat16)
    up_low = fc1_weight.astype(jnp.bfloat16)
    down_low = fc2_weight.astype(jnp.bfloat16)
    slot_mask = live.astype(jnp.float32)
    outputs = []
    input_grads = []
    matrix_sums = None
    vector_sums = None
    for micro_batch in range(MB):
        slot_start = micro_batch * SLOTS
        batch_tokens = images[slot_start : slot_start + SLOTS].reshape(row_count, full_width)
        batch_cot = cotangent[slot_start : slot_start + SLOTS].reshape(row_count, full_width)
        mask_rows = jnp.broadcast_to(
            slot_mask[slot_start : slot_start + SLOTS, None], (SLOTS, length)
        ).reshape(-1, 1)
        stream = lax.dynamic_slice_in_dim(batch_tokens, feature_start, part_width, 1).astype(
            jnp.float32
        )
        cot_stream = lax.dynamic_slice_in_dim(batch_cot, feature_start, part_width, 1)
        forward_weights = (
            lax.all_gather(q_low, "fsdp", axis=0, tiled=True),
            lax.all_gather(k_low, "fsdp", axis=0, tiled=True),
            lax.all_gather(v_low, "fsdp", axis=0, tiled=True),
            lax.all_gather(o_low, "fsdp", axis=1, tiled=True),
            lax.all_gather(up_low, "fsdp", axis=0, tiled=True),
            lax.all_gather(down_low, "fsdp", axis=1, tiled=True),
        )
        output, kept_state = forward_pass(stream, mask_rows, forward_weights, vectors, sizes_info)
        backward_weights = (
            lax.all_gather(q_low, "fsdp", axis=0, tiled=True),
            lax.all_gather(k_low, "fsdp", axis=0, tiled=True),
            lax.all_gather(v_low, "fsdp", axis=0, tiled=True),
            lax.all_gather(o_low, "fsdp", axis=1, tiled=True),
            lax.all_gather(up_low, "fsdp", axis=0, tiled=True),
            lax.all_gather(down_low, "fsdp", axis=1, tiled=True),
        )
        grad_in, matrices, vector_grads = backward_pass(
            cot_stream, mask_rows, backward_weights, vectors, kept_state, sizes_info
        )
        whole_out, whole_grad = (
            lax.all_gather(output, "tensor", axis=1, tiled=True),
            lax.all_gather(grad_in, "tensor", axis=1, tiled=True),
        )
        outputs.append(whole_out.reshape(SLOTS, length, full_width))
        input_grads.append(whole_grad.reshape(SLOTS, length, full_width))
        vector_sums = (
            vector_grads
            if vector_sums is None
            else jax.tree.map(jnp.add, vector_sums, vector_grads)
        )
        matrix_sums = (
            matrices if matrix_sums is None else jax.tree.map(jnp.add, matrix_sums, matrices)
        )
    total_wq, total_wk, total_wv, total_wo, total_up, total_down = matrix_sums
    shard_wq, shard_wk, shard_wv, shard_wo, shard_up, shard_down = (
        lax.psum_scatter(
            total_wq.astype(jnp.bfloat16), "fsdp", scatter_dimension=0, tiled=True
        ).astype(jnp.float32),
        lax.psum_scatter(
            total_wk.astype(jnp.bfloat16), "fsdp", scatter_dimension=0, tiled=True
        ).astype(jnp.float32),
        lax.psum_scatter(
            total_wv.astype(jnp.bfloat16), "fsdp", scatter_dimension=0, tiled=True
        ).astype(jnp.float32),
        lax.psum_scatter(
            total_wo.astype(jnp.bfloat16), "fsdp", scatter_dimension=1, tiled=True
        ).astype(jnp.float32),
        lax.psum_scatter(
            total_up.astype(jnp.bfloat16), "fsdp", scatter_dimension=0, tiled=True
        ).astype(jnp.float32),
        lax.psum_scatter(
            total_down.astype(jnp.bfloat16), "fsdp", scatter_dimension=1, tiled=True
        ).astype(jnp.float32),
    )
    final_wq, final_wk, final_wv, final_wo, final_up, final_down = (
        lax.psum(shard_wq.astype(jnp.bfloat16), "replica").astype(jnp.float32),
        lax.psum(shard_wk.astype(jnp.bfloat16), "replica").astype(jnp.float32),
        lax.psum(shard_wv.astype(jnp.bfloat16), "replica").astype(jnp.float32),
        lax.psum(shard_wo.astype(jnp.bfloat16), "replica").astype(jnp.float32),
        lax.psum(shard_up.astype(jnp.bfloat16), "replica").astype(jnp.float32),
        lax.psum(shard_down.astype(jnp.bfloat16), "replica").astype(jnp.float32),
    )
    (
        sum_gain_one,
        sum_shift_one,
        sum_q_shift,
        sum_v_shift,
        sum_o_shift,
        sum_gain_two,
        sum_shift_two,
        sum_up_shift,
        sum_down_shift,
    ) = vector_sums
    summed = lax.psum(
        (
            sum_gain_one,
            sum_shift_one,
            sum_q_shift,
            sum_v_shift,
            sum_o_shift,
            sum_gain_two,
            sum_shift_two,
            sum_up_shift,
            sum_down_shift,
        ),
        ("replica", "fsdp"),
    )
    (
        grad_gain_one,
        grad_shift_one,
        grad_q_shift,
        grad_v_shift,
        grad_o_shift,
        grad_gain_two,
        grad_shift_two,
        grad_up_shift,
        grad_down_shift,
    ) = summed
    return (
        jnp.concatenate(outputs, axis=0),
        jnp.concatenate(input_grads, axis=0),
        grad_gain_one,
        grad_shift_one,
        final_wq,
        grad_q_shift,
        final_wk,
        final_wv,
        grad_v_shift,
        final_wo,
        grad_o_shift,
        grad_gain_two,
        grad_shift_two,
        final_up,
        grad_up_shift,
        final_down,
        grad_down_shift,
    )


def solution(mesh):
    in_specs = (
        P(("replica", "fsdp"), None, None),
        P(("replica", "fsdp")),
        P(("replica", "fsdp"), None, None),
        P(),
        P(),
        P("fsdp", "tensor"),
        P(),
        P("fsdp", "tensor"),
        P("fsdp", "tensor"),
        P(),
        P("tensor", "fsdp"),
        P(),
        P(),
        P(),
        P("fsdp", "tensor"),
        P(),
        P("tensor", "fsdp"),
        P(),
    )
    out_specs = (
        P(("replica", "fsdp"), None, None),
        P(("replica", "fsdp"), None, None),
        P("tensor"),
        P("tensor"),
        P("fsdp", "tensor"),
        P("tensor"),
        P("fsdp", "tensor"),
        P("fsdp", "tensor"),
        P("tensor"),
        P("tensor", "fsdp"),
        P("tensor"),
        P("tensor"),
        P("tensor"),
        P("fsdp", "tensor"),
        P("tensor"),
        P("tensor", "fsdp"),
        P("tensor"),
    )
    return jax.shard_map(body, mesh=mesh, in_specs=in_specs, out_specs=out_specs, check_vma=False)
```

profile of v0, /device:TPU:0, one launch (start us, length us, event | category | flops | bytes accessed | tf_op | source)
XLA Modules:
  0.0 2773.0 jit_solution(4197665589286498630)
XLA Ops:
  81.4 54.7 %all-gather.19.cloned.1.call-done = bf16[2187,1152]{0,1:T(8,128)(2,1)} async-done(((bf16[2187,576]{0,1:T(8,128)(2,1)}), bf16[2187,1152]{0,1:T(8,128)(2,1)}) %all-gather.19.cloned.1.call-update) | async-done | bytes 5038864 | tf_op jit(solution)/shard_map/all_gather | solution.py:39
  148.5 25.2 all-gather.21.cloned.1.call-done
  226.4 22.4 fusion.110
  248.8 22.3 exponential_reduce_fusion.1
  271.7 21.6 convert_bitcast_fusion.3
  356.8 24.4 fusion.111
  403.0 22.3 convert_bitcast_fusion.2
  478.0 90.3 %reduce-scatter.19.cloned.1.call-done = f32[2187,576]{0,1:T(8,128)} async-done(((f32[2187,1152]{0,1:T(8,128)}), f32[2187,576]{0,1:T(8,128)}) %reduce-scatter.19.cloned.1.call-update) | async-done | bytes 5038864 | tf_op jit(solution)/shard_map/reduce_scatter | solution.py:43
  608.5 31.0 %all-gather.43.cloned.1.call-done = bf16[2187,1152]{0,1:T(8,128)(2,1)} async-done(((bf16[2187,576]{0,1:T(8,128)(2,1)}), bf16[2187,1152]{0,1:T(8,128)(2,1)}) %all-gather.43.cloned.1.call-update) | async-done | bytes 5038864 | tf_op jit(solution)/shard_map/all_gather | solution.py:39
  639.5 96.4 %all-gather.33.cloned.1.call-done = bf16[2152,1152]{0,1:T(8,128)(2,1)} async-done(((bf16[2152,288]{0,1:T(8,128)(2,1)}), bf16[2152,1152]{0,1:T(8,128)(2,1)}) %all-gather.33.cloned.1.call-update) | async-done | bytes 4958224 | tf_op jit(solution)/shard_map/all_gather | solution.py:284
  755.4 75.4 %all-gather.31.cloned.1.call-done = bf16[1152,2152]{1,0:T(8,128)(2,1)} async-done(((bf16[288,2152]{1,0:T(8,128)(2,1)}), bf16[1152,2152]{1,0:T(8,128)(2,1)}) %all-gather.31.cloned.1.call-update) | async-done | bytes 4958224 | tf_op jit(solution)/shard_map/all_gather | solution.py:283
  830.8 69.1 %all-gather.29.cloned.1.call-done = bf16[2187,1152]{0,1:T(8,128)(2,1)} async-done(((bf16[2187,576]{0,1:T(8,128)(2,1)}), bf16[2187,1152]{0,1:T(8,128)(2,1)}) %all-gather.29.cloned.1.call-update) | async-done | bytes 5038864 | tf_op jit(solution)/shard_map/all_gather | solution.py:39
  899.9 36.6 %convert_reduce_fusion.1 = (f32[2152]{0:T(1024)}, bf16[2187,2152]{1,0:T(8,128)(2,1)}, f32[2187,2152]{1,0:T(8,128)}) fusion(f32[2187,2152]{1,0:T(8,128)} %fusion.114, f32[2152]{0:T(1024)S(1)} %dynamic_slice.47, bf16[2187,1152]{0,1:T(8,128)(2,1)} %all-gather.29.cloned.1.call-done, bf16[1152,2152]{1,0:T(8,128)(2,1)} %all-gather.31.cloned.1.call-done), kind=kOutput, calls=%fused_computation.31 | convolution fusion | flops 10951843840 | bytes 57078512 | tf_op jit(solution)/shard_map/dot_general | solution.py:15
  991.0 51.1 %all-gather.39.cloned.1.call-done = bf16[2187,1152]{0,1:T(8,128)(2,1)} async-done(((bf16[2187,576]{0,1:T(8,128)(2,1)}), bf16[2187,1152]{0,1:T(8,128)(2,1)}) %all-gather.39.cloned.1.call-update) | async-done | bytes 5038864 | tf_op jit(solution)/shard_map/all_gather | solution.py:39
  1042.1 35.9 %convert_reduce_fusion = (f32[2152]{0:T(1024)}, bf16[2187,2152]{1,0:T(8,128)(2,1)S(1)}, f32[2187,2152]{1,0:T(8,128)}) fusion(f32[2187,2152]{1,0:T(8,128)} %fusion.117, f32[2152]{0:T(1024)S(1)} %dynamic_slice.47, bf16[2187,1152]{0,1:T(8,128)(2,1)} %all-gather.39.cloned.1.call-done, bf16[1152,2152]{1,0:T(8,128)(2,1)} %all-gather.31.cloned.1.call-done), kind=kOutput, calls=%fused_computation.30 | convolution fusion | flops 10951843840 | bytes 57078512 | tf_op jit(solution)/shard_map/dot_general | solution.py:15
  1098.3 69.2 %reduce-scatter.23.cloned.1.call-done = f32[2187,576]{0,1:T(8,128)} async-done(((f32[2187,1152]{0,1:T(8,128)}), f32[2187,576]{0,1:T(8,128)}) %reduce-scatter.23.cloned.1.call-update) | async-done | bytes 5038864 | tf_op jit(solution)/shard_map/reduce_scatter | solution.py:43
  1167.5 125.6 %reduce-scatter.27.cloned.1.call-done = f32[2187,576]{0,1:T(8,128)} async-done(((f32[2187,1152]{0,1:T(8,128)}), f32[2187,576]{0,1:T(8,128)}) %reduce-scatter.27.cloned.1.call-update) | async-done | bytes 5038864 | tf_op jit(solution)/shard_map/reduce_scatter | solution.py:43
  1412.5 22.7 convert_reduce_fusion.7
  1435.2 40.5 %multiply_reduce_fusion.1 = (f32[3,8,729]{2,1,0:T(8,128)}, f32[3,8,729,729]{2,3,1,0:T(8,128)}) fusion(f32[3,8,729,729]{2,3,1,0:T(8,128)} %get-tuple-element.120, f32[3,8,729]{2,1,0:T(8,128)} %log_add_fusion.1, bf16[3,729,8,72]{1,0,3,2:T(4,128)(2,1)S(1)} %copy-done.7, bf16[3,729,8,72]{1,0,3,2:T(4,128)(2,1)} %reshape.154), kind=kOutput, calls=%fused_computation.3 | convolution fusion | flops 1874906368 | bytes 107215488 | tf_op jit(solution)/shard_map/bqhd,bkhd->bhqk/dot_general | solution.py:159
  1475.7 44.6 %multiply_convert_fusion.1 = bf16[3,8,729,729]{2,3,1,0:T(8,128)(2,1)} fusion(f32[3,8,729,729]{2,3,1,0:T(8,128)} %get-tuple-element.128, f32[3,8,729,729]{2,3,1,0:T(8,128)} %get-tuple-element.120, f32[3,8,729]{2,1,0:T(8,128)} %get-tuple-element.127, f32[3,8,729]{2,1,0:T(8,128)} %log_add_fusion.1), kind=kLoop, calls=%fused_computation.2 | loop fusion | flops 51018336 | bytes 127685808 | tf_op jit(solution)/shard_map/convert_element_type | solution.py:167
  1576.5 22.9 convert_reduce_fusion.6
  1599.3 40.3 %multiply_reduce_fusion = (f32[3,8,729]{2,1,0:T(8,128)}, f32[3,8,729,729]{2,3,1,0:T(8,128)}) fusion(f32[3,8,729,729]{2,3,1,0:T(8,128)} %get-tuple-element.122, f32[3,8,729]{2,1,0:T(8,128)} %log_add_fusion, bf16[3,729,8,72]{1,0,3,2:T(4,128)(2,1)S(1)} %copy-done.9, bf16[3,729,8,72]{1,0,3,2:T(4,128)(2,1)} %reshape.157), kind=kOutput, calls=%fused_computation.1 | convolution fusion | flops 1874906368 | bytes 107215488 | tf_op jit(solution)/shard_map/bqhd,bkhd->bhqk/dot_general | solution.py:159
  1639.7 45.4 %multiply_convert_fusion = bf16[3,8,729,729]{2,3,1,0:T(8,128)(2,1)} fusion(f32[3,8,729,729]{2,3,1,0:T(8,128)} %get-tuple-element.126, f32[3,8,729,729]{2,3,1,0:T(8,128)} %get-tuple-element.122, f32[3,8,729]{2,1,0:T(8,128)} %get-tuple-element.125, f32[3,8,729]{2,1,0:T(8,128)} %log_add_fusion), kind=kLoop, calls=%fused_computation | loop fusion | flops 51018336 | bytes 127685808 | tf_op jit(solution)/shard_map/convert_element_type | solution.py:167
  1914.7 71.2 %reduce-scatter.25.cloned.1.call-done = f32[2187,576]{0,1:T(8,128)} async-done(((f32[2187,1152]{0,1:T(8,128)}), f32[2187,576]{0,1:T(8,128)}) %reduce-scatter.25.cloned.1.call-update) | async-done | bytes 5038864 | tf_op jit(solution)/shard_map/reduce_scatter | solution.py:43
  1986.0 125.6 %reduce-scatter.29.cloned.1.call-done = f32[2187,576]{0,1:T(8,128)} async-done(((f32[2187,1152]{0,1:T(8,128)}), f32[2187,576]{0,1:T(8,128)}) %reduce-scatter.29.cloned.1.call-update) | async-done | bytes 5038864 | tf_op jit(solution)/shard_map/reduce_scatter | solution.py:43
  2127.1 110.7 %reduce-scatter.17.cloned.1.call-done = f32[2187,576]{0,1:T(8,128)} async-done(((f32[2187,1152]{0,1:T(8,128)}), f32[2187,576]{0,1:T(8,128)}) %reduce-scatter.17.cloned.1.call-update) | async-done | bytes 5038864 | tf_op jit(solution)/shard_map/reduce_scatter | solution.py:43
  2252.5 111.1 %reduce-scatter.21.cloned.1.call-done = f32[2187,576]{0,1:T(8,128)} async-done(((f32[2187,1152]{0,1:T(8,128)}), f32[2187,576]{0,1:T(8,128)}) %reduce-scatter.21.cloned.1.call-update) | async-done | bytes 5038864 | tf_op jit(solution)/shard_map/reduce_scatter | solution.py:43
  2377.5 72.0 %all-reduce.8.cloned.1.call-done = (bf16[288,576]{1,0:T(8,128)(2,1)}, bf16[288,576]{1,0:T(8,128)(2,1)}, bf16[288,576]{1,0:T(8,128)(2,1)}, bf16[576,288]{0,1:T(8,...) async-done(((bf16[288,576]{1,0:T(8,128)(2,1)}, bf16[288,576]{1,0:T(8,128)(2,1)}, bf16[288,576]{1,0:T(8,128)(2,1)}, bf16[576,288]{0,1:T(8,128)(2,1)}, ...) | async-done | bytes 3806224 | tf_op jit(solution)/shard_map/psum | solution.py:334
  2462.0 61.4 %all-reduce = (f32[576]{0:T(1024)}, f32[576]{0:T(1024)}, f32[576]{0:T(1024)}, f32[576]{0:T(1024)}, f32[576]{0:T(1024)}, /*index=5*/f32[576]{0:T(1024)}, f32[576]{0:T(1024)}, f32[2152]{0:T(1024)}, f32[576]{0:T(1024)}) all-reduce(f32[576]{0:T(1024)S(1)} %add.383, ...), channel_id=1, replica_groups=mesh['replica'=4,'fsdp'=4,'tensor'=2] {'replica','fsdp'}, use_global_device_ids=true, to_apply=%region_48.0 | all-reduce | flops 6760 | bytes 54080 | tf_op jit(solution)/shard_map/psum | solution.py:352
  2538.3 53.6 %all-gather.47.cloned.1.call-done = bf16[2187,1152]{0,1:T(8,128)(2,1)} async-done(((bf16[2187,576]{0,1:T(8,128)(2,1)}), bf16[2187,1152]{0,1:T(8,128)(2,1)}) %all-gather.47.cloned.1.call-update) | async-done | bytes 5038864 | tf_op jit(solution)/shard_map/all_gather | solution.py:300
  2607.0 56.5 %all-gather.41.cloned.1.call-done = bf16[2187,1152]{0,1:T(8,128)(2,1)} async-done(((bf16[2187,576]{0,1:T(8,128)(2,1)}), bf16[2187,1152]{0,1:T(8,128)(2,1)}) %all-gather.41.cloned.1.call-update) | async-done | bytes 5038864 | tf_op jit(solution)/shard_map/all_gather | solution.py:299
  2678.8 55.5 %all-gather.53.cloned.1.call-done = bf16[2187,1152]{0,1:T(8,128)(2,1)} async-done(((bf16[2187,576]{0,1:T(8,128)(2,1)}), bf16[2187,1152]{0,1:T(8,128)(2,1)}) %all-gather.53.cloned.1.call-update) | async-done | bytes 5038864 | tf_op jit(solution)/shard_map/all_gather | solution.py:300
  (449 shorter events, 949.3 us)
Async XLA Ops:
  9.2 126.9 %all-gather.19.cloned.1.call-start = ((), (), s32[]{:S(2)}) async-start(), calls=%async_computation.14 | async-start | bytes 7962624 | tf_op jit(solution)/shard_map/all_gather | solution.py:39
  66.1 107.6 %all-gather.21.cloned.1.call-start = ((), (), s32[]{:S(2)}) async-start(), calls=%async_computation.15 | async-start | bytes 1843200 | tf_op jit(solution)/shard_map/all_gather | solution.py:281
  67.0 143.1 %all-gather.25.cloned.1.call-start = ((), (), s32[]{:S(2)}) async-start(), calls=%async_computation.17 | async-start | bytes 1843200 | tf_op jit(solution)/shard_map/all_gather | solution.py:280
  69.0 233.4 %all-gather.27.cloned.1.call-start = ((), (), s32[]{:S(2)}) async-start(), calls=%async_computation.18 | async-start | bytes 1843200 | tf_op jit(solution)/shard_map/all_gather | solution.py:282
  69.8 246.9 %all-gather.37.cloned.1.call-start = ((), (), s32[]{:S(2)}) async-start(), calls=%async_computation.25 | async-start | bytes 7962624 | tf_op jit(solution)/shard_map/all_gather | solution.py:39
  70.4 407.6 %reduce-scatter.15.cloned.1.call-start = ((), (), s32[]{:S(2)}) async-start(), calls=%async_computation.19 | async-start | bytes 15925248 | tf_op jit(solution)/shard_map/reduce_scatter | solution.py:43
  312.7 255.6 %reduce-scatter.19.cloned.1.call-start = ((), (), s32[]{:S(2)}) async-start(), calls=%async_computation.26 | async-start | bytes 15925248 | tf_op jit(solution)/shard_map/reduce_scatter | solution.py:43
  444.8 194.7 %all-gather.43.cloned.1.call-start = ((), (), s32[]{:S(2)}) async-start(), calls=%async_computation.30 | async-start | bytes 7962624 | tf_op jit(solution)/shard_map/all_gather | solution.py:39
  471.5 264.4 %all-gather.33.cloned.1.call-start = ((), (), s32[]{:S(2)}) async-start(), calls=%async_computation.22 | async-start | bytes 6266880 | tf_op jit(solution)/shard_map/all_gather | solution.py:284
  474.6 356.2 %all-gather.31.cloned.1.call-start = ((), (), s32[]{:S(2)}) async-start(), calls=%async_computation.21 | async-start | bytes 6266880 | tf_op jit(solution)/shard_map/all_gather | solution.py:283
  477.7 422.2 %all-gather.29.cloned.1.call-start = ((), (), s32[]{:S(2)}) async-start(), calls=%async_computation.20 | async-start | bytes 7962624 | tf_op jit(solution)/shard_map/all_gather | solution.py:39
  591.3 380.1 %all-gather.49.cloned.1.call-start = ((), (), s32[]{:S(2)}) async-start(), calls=%async_computation.35 | async-start | bytes 7962624 | tf_op jit(solution)/shard_map/all_gather | solution.py:39
  608.2 433.9 %all-gather.39.cloned.1.call-start = ((), (), s32[]{:S(2)}) async-start(), calls=%async_computation.27 | async-start | bytes 7962624 | tf_op jit(solution)/shard_map/all_gather | solution.py:39
  755.3 412.2 %reduce-scatter.23.cloned.1.call-start = ((), (), s32[]{:S(2)}) async-start(), calls=%async_computation.31 | async-start | bytes 15925248 | tf_op jit(solution)/shard_map/reduce_scatter | solution.py:43
  953.5 339.6 %reduce-scatter.27.cloned.1.call-start = ((), (), s32[]{:S(2)}) async-start(), calls=%async_computation.36 | async-start | bytes 15925248 | tf_op jit(solution)/shard_map/reduce_scatter | solution.py:43
  1098.3 301.3 %all-gather.45.cloned.1.call-start = ((), (), s32[]{:S(2)}) async-start(), calls=%async_computation.32 | async-start | bytes 7962624 | tf_op jit(solution)/shard_map/all_gather | solution.py:39
  1323.2 221.9 %all-gather.51.cloned.1.call-start = ((), (), s32[]{:S(2)}) async-start(), calls=%async_computation.37 | async-start | bytes 7962624 | tf_op jit(solution)/shard_map/all_gather | solution.py:39
  1323.8 590.7 %reduce-scatter.39.cloned.1.call-start = ((), (), s32[]{:S(2)}) async-start(), calls=%async_computation.44 | async-start | bytes 6266880 | tf_op jit(solution)/shard_map/reduce_scatter | solution.py:326
  1359.7 554.8 %reduce-scatter.41.cloned.1.call-start = ((), (), s32[]{:S(2)}) async-start(), calls=%async_computation.45 | async-start | bytes 6266880 | tf_op jit(solution)/shard_map/reduce_scatter | solution.py:329
  1399.0 515.5 %reduce-scatter.37.cloned.1.call-start = ((), (), s32[]{:S(2)}) async-start(), calls=%async_computation.43 | async-start | bytes 1843200 | tf_op jit(solution)/shard_map/reduce_scatter | solution.py:323
  1639.7 274.8 %reduce-scatter.35.cloned.1.call-start = ((), (), s32[]{:S(2)}) async-start(), calls=%async_computation.42 | async-start | bytes 1843200 | tf_op jit(solution)/shard_map/reduce_scatter | solution.py:320
  1735.3 179.2 %reduce-scatter.31.cloned.1.call-start = ((), (), s32[]{:S(2)}) async-start(), calls=%async_computation.40 | async-start | bytes 1843200 | tf_op jit(solution)/shard_map/reduce_scatter | solution.py:314
  1777.0 137.6 %reduce-scatter.33.cloned.1.call-start = ((), (), s32[]{:S(2)}) async-start(), calls=%async_computation.41 | async-start | bytes 1843200 | tf_op jit(solution)/shard_map/reduce_scatter | solution.py:317
  1826.5 159.5 %reduce-scatter.25.cloned.1.call-start = ((), (), s32[]{:S(2)}) async-start(), calls=%async_computation.33 | async-start | bytes 15925248 | tf_op jit(solution)/shard_map/reduce_scatter | solution.py:43
  1849.3 262.3 %reduce-scatter.29.cloned.1.call-start = ((), (), s32[]{:S(2)}) async-start(), calls=%async_computation.38 | async-start | bytes 15925248 | tf_op jit(solution)/shard_map/reduce_scatter | solution.py:43
  1874.1 363.8 %reduce-scatter.17.cloned.1.call-start = ((), (), s32[]{:S(2)}) async-start(), calls=%async_computation.23 | async-start | bytes 15925248 | tf_op jit(solution)/shard_map/reduce_scatter | solution.py:43
  1893.7 469.9 %reduce-scatter.21.cloned.1.call-start = ((), (), s32[]{:S(2)}) async-start(), calls=%async_computation.28 | async-start | bytes 15925248 | tf_op jit(solution)/shard_map/reduce_scatter | solution.py:43
  1913.8 535.8 %all-reduce.8.cloned.1.call-start = ((), (), s32[]{:S(2)}) async-start(), calls=%async_computation.46 | async-start | bytes 7962624 | tf_op jit(solution)/shard_map/psum | solution.py:334
  1914.7 608.7 %all-gather.35.cloned.1.call-start = ((), (), s32[]{:S(2)}) async-start(), calls=%async_computation.24 | async-start | bytes 7962624 | tf_op jit(solution)/shard_map/all_gather | solution.py:299
  2251.7 340.3 %all-gather.47.cloned.1.call-start = ((), (), s32[]{:S(2)}) async-start(), calls=%async_computation.34 | async-start | bytes 7962624 | tf_op jit(solution)/shard_map/all_gather | solution.py:300
  2252.4 411.1 %all-gather.41.cloned.1.call-start = ((), (), s32[]{:S(2)}) async-start(), calls=%async_computation.29 | async-start | bytes 7962624 | tf_op jit(solution)/shard_map/all_gather | solution.py:299
  2376.6 357.7 %all-gather.53.cloned.1.call-start = ((), (), s32[]{:S(2)}) async-start(), calls=%async_computation.39 | async-start | bytes 7962624 | tf_op jit(solution)/shard_map/all_gather | solution.py:300
  (99 other events, 6528.9 us)
Sparse Core Ops, SparseCore 0:
  10.2 38.1 all-gather.22
  66.2 69.7 all-gather.18
  138.2 35.4 all-gather.20
  175.7 34.3 all-gather.24
  212.1 34.3 all-gather.26
  248.5 68.1 all-gather.36
  319.0 123.2 reduce-scatter.14
  445.0 123.2 reduce-scatter.18
  569.8 69.6 all-gather.42
  641.5 94.3 all-gather.32
  738.1 92.6 all-gather.30
  832.2 67.6 all-gather.28
  902.0 69.2 all-gather.48
  972.8 69.2 all-gather.38
  1044.3 123.2 reduce-scatter.22
  1169.8 123.2 reduce-scatter.26
  1323.4 70.4 all-gather.44
  1395.2 69.2 all-gather.50
  1466.9 90.0 reduce-scatter.38
  1559.7 90.5 reduce-scatter.40
  1735.4 34.8 reduce-scatter.34
  1777.1 34.8 reduce-scatter.30
  1826.6 34.7 reduce-scatter.32
  1863.7 122.1 reduce-scatter.24
  1988.2 123.2 reduce-scatter.28
  2113.7 124.1 reduce-scatter.16
  2240.3 123.2 reduce-scatter.20
  2366.4 83.0 all-reduce.7
  2451.6 69.3 all-gather.34
  2522.6 69.2 all-gather.46
  2594.1 69.2 all-gather.40
  2664.9 69.2 all-gather.52
  (1 shorter events, 34.2 us)
where the time goes:
time: 2780 us; the launch traced here: 2770 us
  waiting for transfers between devices  1390 us (50%)
  matrix products  735 us (26%)
  local copies, waits for them, and re-layouts  263 us (9%)
  other arithmetic  261 us (9%)
  blocking collectives  94.2 us (3%)
    reduce_scatter x8, waiting for transfers between devices, combine_parts(): lax.psum_scatter(partial_value, 'tensor', scatter_dimension=1, tiled=True)  704 us
    all_gather x8, waiting for transfers between devices, spread_whole(): return lax.all_gather(rounded, 'tensor', axis=1, tiled=True)  228 us
    dot_general x12, matrix products, matmul(): return jnp.dot(first_op, second_op, preferred_element_type=jnp.float32)  177 us
    dot_general x12, matrix products, matmul_tn(): lax.dot_general(first_op, second_op, (((0,), (0,)), ((), ())), preferred_...  147 us
    dot_general x12, matrix products, matmul_nt(): lax.dot_general(first_op, second_op, (((1,), (1,)), ((), ())), preferred_...  132 us
    all_gather x2, waiting for transfers between devices, body(): lax.all_gather(grad_in, 'tensor', axis=1, tiled=True)  109 us
    all_gather x1, waiting for transfers between devices, body(): lax.all_gather(down_low, 'fsdp', axis=1, tiled=True)  96.4 us
    convert_element_type x2, other arithmetic, backward_pass(): score_grad = (probs * (prob_grad - row_dot)).astype(jnp.bfloat16)  90 us
  transfers between devices with their start and end apart: 33, of which 21 were waited for; matrix products, arithmetic and copies ran while one was open for 43% of the time, Pallas kernels for 0%

commit v1 on v0

--- a/solution.py
+++ b/solution.py
@@ -1,6 +1,10 @@
+import functools
+
 import jax
 import jax.numpy as jnp
 from jax import lax
+from jax.experimental import pallas as pl
+from jax.experimental.pallas import tpu as pltpu
 from jax.sharding import PartitionSpec as P
 
 HEAD = 72
@@ -199,7 +203,7 @@
     return (input_grad.astype(jnp.bfloat16), matrices, vector_grads)
 
 
-def body(
+def split_heads_body(
     images,
     live,
     cotangent,
@@ -395,6 +399,770 @@
     )
 
 
+WINDOW = 256
+LANES = 128
+SHIFT = 64
+VMEM = 60 * 2**20
+GELU = 0.7978845608
+EVERY = ("tensor", "fsdp", "replica")
+
+
+def ceil_to(value, step):
+    return -(-value // step) * step
+
+
+def call(kernel, name, grid, scalars, ins, outs, flops=0, scratch=(), aliases=None):
+    total = sum(array.size * array.dtype.itemsize for array, _ in ins)
+    return pl.pallas_call(
+        kernel,
+        grid_spec=pltpu.PrefetchScalarGridSpec(
+            num_scalar_prefetch=1,
+            grid=grid,
+            in_specs=[spec for _, spec in ins],
+            out_specs=[spec for _, _, spec in outs],
+            scratch_shapes=list(scratch),
+        ),
+        out_shape=[jax.ShapeDtypeStruct(shape, dtype) for shape, dtype, _ in outs],
+        input_output_aliases=aliases or {},
+        compiler_params=pltpu.CompilerParams(vmem_limit_bytes=VMEM),
+        cost_estimate=pl.CostEstimate(flops=flops, bytes_accessed=total, transcendentals=0),
+        name=name,
+    )(scalars, *(array for array, _ in ins))
+
+
+def fixed(shape, index):
+    return pl.BlockSpec(shape, index, pipeline_mode=pl.Buffered(1))
+
+
+def head_window(offset, base, rows):
+    start = (offset + base) // LANES * LANES
+    lane = lax.broadcasted_iota(jnp.int32, (rows, WINDOW), 1) + start
+    inside = (lane >= offset + base) & (lane < offset + base + HEAD)
+    return pl.ds(pl.multiple_of(start, LANES), WINDOW), inside
+
+
+def attention(qvk, length, rows, width, group):
+    heads = width // HEAD
+    count = qvk.shape[0] // rows
+    steps = heads // group
+    out_width = ceil_to(width + SHIFT, WINDOW)
+
+    def kernel(none_ref, qvk_ref, mixed_ref, probs_ref):
+        @pl.when(pl.program_id(1) == 0)
+        def _():
+            mixed_ref[...] = jnp.zeros_like(mixed_ref)
+
+        real = lax.broadcasted_iota(jnp.int32, (rows, rows), 1) < length
+        for item in range(group):
+            offset = (pl.program_id(1) * group + item) * HEAD
+            at_q, _ = head_window(offset, 0, rows)
+            at_v, in_v = head_window(offset, width, rows)
+            at_k, in_k = head_window(offset, 2 * width, rows)
+            at_o, in_o = head_window(offset, SHIFT, rows)
+            key_rows = jnp.where(in_k, qvk_ref[:, at_k], 0)
+            value_rows = jnp.where(in_v, qvk_ref[:, at_v], 0)
+            scores = jnp.where(real, matmul_nt(qvk_ref[:, at_q], key_rows), -1e30)
+            powers = jnp.exp(scores - jnp.max(scores, axis=1, keepdims=True))
+            total = jnp.sum(powers, axis=1, keepdims=True)
+            probs = (powers * (1.0 / total)).astype(jnp.bfloat16)
+            probs_ref[item] = probs
+            mixed = matmul(probs, value_rows).astype(jnp.bfloat16)
+            mixed_ref[:, at_o] = jnp.where(in_o, mixed, mixed_ref[:, at_o])
+
+    return call(
+        kernel,
+        "attention",
+        (count, steps),
+        jnp.zeros((1,), jnp.int32),
+        [(qvk, pl.BlockSpec((rows, qvk.shape[1]), lambda i, g, s: (i, 0)))],
+        [
+            ((count * rows, out_width), jnp.bfloat16, pl.BlockSpec((rows, out_width), lambda i, g, s: (i, 0))),
+            (
+                (count * heads, rows, rows),
+                jnp.bfloat16,
+                pl.BlockSpec((group, rows, rows), lambda i, g, s: (i * steps + g, 0, 0)),
+            ),
+        ],
+        flops=4 * count * heads * rows * rows * WINDOW,
+    )
+
+
+def attention_back(qvk, mixed, grad, probs, images, kept, rows, width, group):
+    heads = width // HEAD
+    steps = heads // group
+    at = images.start
+    count = len(images)
+
+    def kernel(none_ref, qvk_ref, mixed_ref, grad_ref, probs_ref, *refs):
+        out_ref, sums_ref = refs[-2:]
+
+        @pl.when(pl.program_id(1) == 0)
+        def _():
+            out_ref[...] = jnp.zeros_like(out_ref)
+
+        for item in range(group):
+            offset = (pl.program_id(1) * group + item) * HEAD
+            at_q, in_q = head_window(offset, 0, rows)
+            at_v, in_v = head_window(offset, width, rows)
+            at_k, in_k = head_window(offset, 2 * width, rows)
+            at_o, in_o = head_window(offset, SHIFT, rows)
+            grad = jnp.where(in_o, grad_ref[:, at_o], 0)
+            query_rows = jnp.where(in_q, qvk_ref[:, at_q], 0)
+            key_rows = jnp.where(in_k, qvk_ref[:, at_k], 0)
+            probs = probs_ref[item]
+            row_dot = jnp.sum(
+                grad.astype(jnp.float32) * mixed_ref[:, at_o].astype(jnp.float32), axis=1, keepdims=True
+            )
+            prob_grad = matmul_nt(grad, qvk_ref[:, at_v])
+            score_grad = (probs.astype(jnp.float32) * (prob_grad - row_dot)).astype(jnp.bfloat16)
+            value_grad = matmul_tn(probs, grad).astype(jnp.bfloat16)
+            query_grad = (matmul(score_grad, key_rows) * HEAD ** (-0.5)).astype(jnp.bfloat16)
+            key_grad = matmul_tn(score_grad, query_rows).astype(jnp.bfloat16)
+            out_ref[:, at_q] = jnp.where(in_q, query_grad, out_ref[:, at_q])
+            out_ref[:, at_v] = jnp.where(in_v, value_grad, out_ref[:, at_v])
+            out_ref[:, at_k] = jnp.where(in_k, key_grad, out_ref[:, at_k])
+
+        @pl.when(pl.program_id(1) == steps - 1)
+        def _():
+            total = jnp.sum(out_ref[...].astype(jnp.float32), axis=0, keepdims=True)
+            sums_ref[0] = jnp.broadcast_to(total, sums_ref.shape[1:])
+
+    ins = [
+        (qvk, pl.BlockSpec((rows, qvk.shape[1]), lambda i, g, s: (at + i, 0))),
+        (mixed, pl.BlockSpec((rows, mixed.shape[1]), lambda i, g, s: (at + i, 0))),
+        (grad, pl.BlockSpec((rows, mixed.shape[1]), lambda i, g, s: (at + i, 0))),
+        (probs, pl.BlockSpec((group, rows, rows), lambda i, g, s: ((at + i) * steps + g, 0, 0))),
+    ]
+    if kept is not None:
+        ins.append((kept, pl.BlockSpec(memory_space=pl.ANY)))
+    grads, sums = call(
+        kernel,
+        "attention_back",
+        (count, steps),
+        jnp.zeros((1,), jnp.int32),
+        ins,
+        [
+            (qvk.shape, jnp.bfloat16, pl.BlockSpec((rows, qvk.shape[1]), lambda i, g, s: (at + i, 0))),
+            ((count, 8, qvk.shape[1]), jnp.float32, pl.BlockSpec((1, 8, qvk.shape[1]), lambda i, g, s: (i, 0, 0))),
+        ],
+        flops=8 * count * heads * rows * rows * WINDOW,
+        aliases=None if kept is None else {5: 0},
+    )
+    return grads, jnp.sum(sums[:, 0], axis=0)
+
+
+def place(pieces, slots, total):
+    def kernel(slots_ref, *refs):
+        for at, ref in enumerate(refs[:-1]):
+            refs[-1][pl.ds(slots_ref[at], ref.shape[0])] = ref[...]
+
+    def whole(shape):
+        return fixed(shape, lambda i, s: (0, 0, 0))
+
+    shape = (total, *pieces[0].shape[1:])
+    return call(
+        kernel,
+        "place",
+        (1,),
+        jnp.stack(slots).astype(jnp.int32),
+        [(piece, whole(piece.shape)) for piece in pieces],
+        [(shape, pieces[0].dtype, whole(shape))],
+    )[0]
+
+
+def outer_sum(left, right, ranks, step):
+    rows, lines = left.shape
+    columns = right.shape[1] // ranks
+    steps = columns // step
+
+    def kernel(none_ref, left_ref, right_ref, out_ref):
+        out_ref[...] = matmul_tn(left_ref[...], right_ref[...]).astype(out_ref.dtype)
+
+    return call(
+        kernel,
+        "outer_sum",
+        (ranks, steps),
+        jnp.zeros((1,), jnp.int32),
+        [
+            (left, fixed((rows, lines), lambda t, j, s: (0, 0))),
+            (right, pl.BlockSpec((rows, step), lambda t, j, s: (0, t * steps + j))),
+        ],
+        [((ranks * lines, columns), jnp.bfloat16, pl.BlockSpec((lines, step), lambda t, j, s: (t, j)))],
+        flops=2 * rows * lines * columns * ranks,
+    )[0]
+
+
+def tie(*values):
+    return lax.optimization_barrier(values)
+
+
+def swap(array, axis, bits):
+    size = lax.axis_size(axis)
+    return lax.ppermute(array, axis, [(rank, rank ^ bits) for rank in range(size)])
+
+
+def turn(array, axis, steps):
+    size = lax.axis_size(axis)
+    return lax.ppermute(array, axis, [(rank, (rank + steps) % size) for rank in range(size)])
+
+
+def replica_bits():
+    bit = lax.axis_size("replica") // 2
+    bits = []
+    while bit:
+        bits.append(bit)
+        bit //= 2
+    return bits
+
+
+def among_replicas(piece):
+    found = {0: piece}
+    for bit in replica_bits():
+        found.update({bits ^ bit: swap(held, "replica", bit) for bits, held in list(found.items())})
+    return found
+
+
+def from_lines(shard):
+    copies = lax.axis_size("replica")
+    blocks = shard.reshape(copies, -1, shard.shape[1])
+    mine = lax.dynamic_slice_in_dim(blocks, lax.axis_index("replica"), 1, 0)
+    return [mine] + [turn(mine, "fsdp", step) for step in range(1, lax.axis_size("fsdp"))]
+
+
+def gather_parts(shard, parts):
+    copies, lines, ranks = (lax.axis_size(axis) for axis in ("replica", "fsdp", "tensor"))
+    copy, line = lax.axis_index("replica"), lax.axis_index("fsdp")
+    blocks = shard.reshape(copies, -1, shard.shape[1])
+    wholes = []
+    for rank in range(ranks):
+        pieces, slots = [], []
+        for step in range(lines):
+            start = (line - step) % lines * copies
+            if rank == 0 and step == 0:
+                pieces.append(blocks)
+                slots.append(start)
+                continue
+            piece = parts[step] if rank == 0 else swap(parts[step], "tensor", rank)
+            for bits, held in among_replicas(piece).items():
+                pieces.append(held)
+                slots.append(start + (copy ^ bits))
+        wholes.append(place(pieces, slots, lines * copies).reshape(-1, shard.shape[1]))
+    return wholes
+
+
+def gather_whole(shard):
+    share = shard.shape[0] // lax.axis_size("replica")
+    part = lax.dynamic_slice_in_dim(shard, lax.axis_index("replica") * share, share, 0)
+    return lax.all_gather(part, EVERY, axis=0, tiled=True)
+
+
+def add_low(first_term, *terms):
+    total = first_term.astype(jnp.float32)
+    for term in terms:
+        total = total + term.astype(jnp.float32)
+    return total.astype(jnp.bfloat16)
+
+
+def by_lines(term):
+    bits = len(replica_bits())
+    return term.reshape(lax.axis_size("fsdp"), *(2 for _ in range(bits)), -1, term.shape[1])
+
+
+def halve(held, bit):
+    side = lax.axis_index("replica") // bit % 2
+    axis = held.ndim - 3
+    keep = lax.dynamic_index_in_dim(held, side, axis, keepdims=False)
+    send = lax.dynamic_index_in_dim(held, 1 - side, axis, keepdims=False)
+    return add_low(keep, swap(send, "replica", bit))
+
+
+def sum_lines(held):
+    lines, line = lax.axis_size("fsdp"), lax.axis_index("fsdp")
+    terms = [lax.dynamic_index_in_dim(held, line, 0, keepdims=True)]
+    for step in range(1, lines):
+        send = lax.dynamic_index_in_dim(held, (line + step) % lines, 0, keepdims=True)
+        terms.append(turn(send, "fsdp", step))
+    return add_low(*terms)
+
+
+def join_replicas(piece):
+    copy = lax.axis_index("replica")
+    found = among_replicas(piece)
+    whole = place(list(found.values()), [copy ^ bits for bits in found], len(found))
+    return whole.reshape(-1, piece.shape[2])
+
+
+def sum_over(vector, axis):
+    bit = 1
+    while bit < lax.axis_size(axis):
+        vector = vector + swap(vector, axis, bit)
+        bit *= 2
+    return vector
+
+
+def norm_parts(values):
+    center = jnp.mean(values, axis=1, keepdims=True)
+    spread = jnp.mean(values * values, axis=1, keepdims=True) - center * center
+    scale_inv = lax.rsqrt(spread + EPSILON)
+    return (values - center) * scale_inv, scale_inv
+
+
+def norm_backward(grad, normed, scale_inv, gain_vec):
+    scaled = grad * gain_vec
+    mean_one = jnp.mean(scaled, axis=1, keepdims=True)
+    mean_two = jnp.mean(scaled * normed, axis=1, keepdims=True)
+    return scale_inv * (scaled - mean_one - normed * mean_two)
+
+
+def image_body(
+    images,
+    live,
+    cotangent,
+    ln1_gain,
+    ln1_bias,
+    q_weight,
+    q_bias,
+    k_weight,
+    v_weight,
+    v_bias,
+    o_weight,
+    o_bias,
+    ln2_gain,
+    ln2_bias,
+    fc1_weight,
+    fc1_bias,
+    fc2_weight,
+    fc2_bias,
+):
+    low, full = jnp.bfloat16, jnp.float32
+    tensor_count = lax.axis_size("tensor")
+    tensor_rank = lax.axis_index("tensor")
+    slots, length, wide = images.shape
+    count = slots // tensor_count
+    rows = ceil_to(length, 32)
+    half = rows // 2
+    width = q_weight.shape[1]
+    units = fc1_weight.shape[1]
+    qvk_width = ceil_to(3 * width, WINDOW)
+    o_width = ceil_to(width + SHIFT, WINDOW)
+    unit_width = ceil_to(units, WINDOW)
+    if unit_width % o_width:
+        unit_width = ceil_to(unit_width, o_width)
+    ranks = range(tensor_count)
+    all_rows = count * rows
+    blocks = all_rows // half
+    scalars = jnp.concatenate(
+        [
+            jnp.stack([tensor_rank * count] + [tensor_rank ^ rank for rank in ranks]).astype(jnp.int32),
+            lax.dynamic_slice_in_dim(live, tensor_rank * count, count, 0),
+        ]
+    )
+    live_at = 1 + tensor_count
+
+    def columns(parts, ahead, total):
+        body_part = jnp.concatenate(parts, axis=1)
+        return jnp.pad(body_part, ((0, 0), (ahead, total - ahead - body_part.shape[1])))
+
+    def row(vector):
+        return vector.reshape(1, -1)
+
+    def slots_spec(first=0):
+        return pl.BlockSpec((1, half, wide), lambda i, s: (s[0] + first + i // 2, i % 2, 0))
+
+    def rows_spec(size, first=0):
+        return pl.BlockSpec((half, size), lambda i, s: (2 * first + i, 0))
+
+    def vector_spec():
+        return pl.BlockSpec((1, wide), lambda i, s: (0, 0))
+
+    def sums_spec():
+        return pl.BlockSpec((8, wide), lambda i, s: (0, 0))
+
+    def real_rows(values):
+        at = lax.broadcasted_iota(jnp.int32, (half, 1), 0) + pl.program_id(0) % 2 * half
+        return jnp.where(at < length, values.astype(full), 0.0)
+
+    def live_slot(scalars_ref, first=0):
+        return scalars_ref[live_at + first + pl.program_id(0) // 2].astype(full)
+
+    def add_sums(sums_ref, *terms):
+        @pl.when(pl.program_id(0) == 0)
+        def _():
+            sums_ref[...] = jnp.zeros_like(sums_ref)
+
+        for at, term in enumerate(terms):
+            sums_ref[at : at + 1] += jnp.sum(term, axis=0, keepdims=True)
+
+    def product(part_refs, weight_refs):
+        total = matmul_nt(part_refs[0][...], weight_refs[0][...])
+        for part_ref, weight_ref in zip(part_refs[1:], weight_refs[1:]):
+            total = total + matmul_nt(part_ref[...], weight_ref[...])
+        return total
+
+    qvk_shard = columns([w.astype(low) for w in (q_weight, v_weight, k_weight)], 0, qvk_width)
+    parts = from_lines(qvk_shard)
+
+    def first_kernel(scalars_ref, images_ref, cot_ref, gain_ref, shift_ref, first_ref, grad_ref, sums_ref):
+        normed, _ = norm_parts(real_rows(images_ref[0]))
+        first_ref[...] = (normed * gain_ref[...] + shift_ref[...]).astype(low)
+        grad = real_rows(cot_ref[0]) * live_slot(scalars_ref)
+        grad_ref[...] = grad.astype(low)
+        add_sums(sums_ref, grad)
+
+    first, out_grad, first_sums = call(
+        first_kernel,
+        "first_norm",
+        (blocks,),
+        scalars,
+        [(images, slots_spec()), (cotangent, slots_spec()), (row(ln1_gain), vector_spec()), (row(ln1_bias), vector_spec())],
+        [
+            ((all_rows, wide), low, rows_spec(wide)),
+            ((all_rows, wide), low, rows_spec(wide)),
+            ((8, wide), full, sums_spec()),
+        ],
+    )
+
+    parts, first, out_grad = tie(parts, first, out_grad)
+    up_o_shard = jnp.concatenate(
+        [
+            columns([fc1_weight.astype(low)], 0, unit_width),
+            columns([o_weight.astype(low).T], SHIFT, o_width),
+        ],
+        axis=1,
+    )
+    down_shard = columns([fc2_weight.astype(low).T], 0, unit_width)
+    up_o_shard, down_shard, parts = tie(up_o_shard, down_shard, parts)
+    up_o_whole = gather_whole(up_o_shard)
+    down_whole = gather_whole(down_shard)
+    qvk_weights = gather_parts(qvk_shard, parts)
+
+    def of_rank(vector, rank, size):
+        return lax.dynamic_slice_in_dim(vector, (tensor_rank ^ rank) * size, size, 0)
+
+    scale_row = jnp.where(jnp.arange(qvk_width) < width, HEAD ** (-0.5), 1.0)
+    qvk, mixed, probs = [], [], []
+    for rank in ranks:
+        shift_row = jnp.pad(
+            jnp.concatenate([of_rank(q_bias, rank, width), of_rank(v_bias, rank, width)]),
+            (0, qvk_width - 2 * width),
+        )
+        qvk.append(((matmul(first, qvk_weights[rank]) + shift_row) * scale_row).astype(low))
+        mixed_part, probs_part = attention(qvk[rank], length, rows, width, 4)
+        mixed.append(mixed_part)
+        probs.append(probs_part)
+
+    def o_spec(rank):
+        return fixed((wide, o_width), lambda i, s: (s[1 + rank], unit_width // o_width))
+
+    def middle_kernel(scalars_ref, *refs):
+        images_ref, bias_ref, gain_ref, shift_ref, middle_ref, second_ref = refs[2 * tensor_count :]
+        total = product(refs[:tensor_count], refs[tensor_count : 2 * tensor_count])
+        middle = real_rows(images_ref[0]) + (total + bias_ref[...])
+        middle_ref[...] = middle
+        normed, _ = norm_parts(middle)
+        second_ref[...] = (normed * gain_ref[...] + shift_ref[...]).astype(low)
+
+    middle, second = call(
+        middle_kernel,
+        "middle_norm",
+        (blocks,),
+        scalars,
+        [(part, rows_spec(o_width)) for part in mixed]
+        + [(up_o_whole, o_spec(rank)) for rank in ranks]
+        + [
+            (images, slots_spec()),
+            (row(o_bias), vector_spec()),
+            (row(ln2_gain), vector_spec()),
+            (row(ln2_bias), vector_spec()),
+        ],
+        [((all_rows, wide), full, rows_spec(wide)), ((all_rows, wide), low, rows_spec(wide))],
+        flops=2 * all_rows * wide * o_width * tensor_count,
+    )
+
+    chunk = o_width if unit_width % o_width == 0 else unit_width
+
+    def unit_rows():
+        return pl.BlockSpec((half, unit_width), lambda t, i, s: (i, t))
+
+    def unit_weights():
+        return pl.BlockSpec((wide, unit_width), lambda t, i, s: (t, 0))
+
+    def hidden_kernel(scalars_ref, second_ref, weight_ref, shift_ref, hidden_ref, slope_ref):
+        for start in range(0, unit_width, chunk):
+            at = slice(start, start + chunk)
+            upper = matmul(second_ref[...], weight_ref[:, at]) + shift_ref[:, at]
+            square = upper * upper
+            share = 0.5 + 0.5 * jnp.tanh(upper * (GELU + GELU * 0.044715 * square))
+            hidden = upper * share
+            slope = share + (hidden - hidden * share) * (2 * GELU + 6 * GELU * 0.044715 * square)
+            hidden_ref[:, at] = hidden.astype(low)
+            slope_ref[:, at] = slope.astype(low)
+
+    unit_shift = jnp.pad(
+        fc1_bias.reshape(tensor_count, units), ((0, 0), (0, unit_width - units))
+    ).reshape(1, -1)
+    hidden, slopes = call(
+        hidden_kernel,
+        "hidden",
+        (tensor_count, blocks),
+        scalars,
+        [
+            (second, pl.BlockSpec((half, wide), lambda t, i, s: (i, 0))),
+            (up_o_whole, unit_weights()),
+            (unit_shift, pl.BlockSpec((1, unit_width), lambda t, i, s: (0, t))),
+        ],
+        [((all_rows, tensor_count * unit_width), low, unit_rows())] * 2,
+        flops=2 * all_rows * wide * unit_width * tensor_count,
+    )
+    down_terms = outer_sum(out_grad, hidden, tensor_count, chunk)
+    down_terms, hidden = tie(down_terms, hidden)
+    down_share = lax.psum_scatter(down_terms, EVERY, scatter_dimension=0, tiled=True)
+
+    def weight_spec(rank):
+        return fixed((wide, unit_width), lambda i, s: (rank, 0))
+
+    def unit_spec(rank):
+        return pl.BlockSpec((half, unit_width), lambda i, s: (i, rank))
+
+    def output_kernel(scalars_ref, *refs):
+        middle_ref, bias_ref, output_ref, whole_ref = refs[2 * tensor_count :]
+        total = product(refs[:tensor_count], refs[tensor_count : 2 * tensor_count])
+        result = middle_ref[...] + (total + bias_ref[...])
+        output_ref[0] = (result * live_slot(scalars_ref)).astype(low)
+        whole_ref[0] = output_ref[0]
+
+    output, out_whole = call(
+        output_kernel,
+        "output",
+        (blocks,),
+        scalars,
+        [(hidden, unit_spec(rank)) for rank in ranks]
+        + [(down_whole, weight_spec(rank)) for rank in ranks]
+        + [(middle, rows_spec(wide)), (row(fc2_bias), vector_spec())],
+        [
+            ((count, length, wide), low, pl.BlockSpec((1, half, wide), lambda i, s: (i // 2, i % 2, 0))),
+            ((slots, length, wide), low, slots_spec()),
+        ],
+        flops=2 * all_rows * wide * unit_width * tensor_count,
+    )
+
+    def trade(part):
+        return [swap(part, "tensor", rank) for rank in ranks[1:]]
+
+    def lay(whole, parts, first):
+        for rank, part in zip(ranks[1:], parts):
+            whole = lax.dynamic_update_slice_in_dim(whole, part, (tensor_rank ^ rank) * count + first, 0)
+        return whole
+
+    output, out_grad = tie(output, out_grad)
+    out_parts = [trade(output[slot : slot + 1]) for slot in range(count)]
+
+    def hidden_back_kernel(scalars_ref, grad_ref, weight_ref, slope_ref, upper_ref, sums_ref):
+        @pl.when(pl.program_id(1) == 0)
+        def _():
+            sums_ref[...] = jnp.zeros_like(sums_ref)
+
+        for start in range(0, unit_width, chunk):
+            at = slice(start, start + chunk)
+            upper = matmul(grad_ref[...], weight_ref[:, at]) * slope_ref[:, at].astype(full)
+            rounded = upper.astype(low)
+            upper_ref[:, at] = rounded
+            sums_ref[0:1, at] += jnp.sum(rounded.astype(full), axis=0, keepdims=True)
+
+    upper_grads, upper_sums = call(
+        hidden_back_kernel,
+        "hidden_back",
+        (tensor_count, blocks),
+        scalars,
+        [
+            (out_grad, pl.BlockSpec((half, wide), lambda t, i, s: (i, 0))),
+            (down_whole, unit_weights()),
+            (slopes, unit_rows()),
+        ],
+        [
+            ((all_rows, tensor_count * unit_width), low, unit_rows()),
+            ((8, tensor_count * unit_width), full, pl.BlockSpec((8, unit_width), lambda t, i, s: (0, t))),
+        ],
+        flops=2 * all_rows * wide * unit_width * tensor_count,
+    )
+    up_terms = outer_sum(second, upper_grads, tensor_count, chunk)
+    up_terms, upper_grads = tie(up_terms, upper_grads)
+    up_share = lax.psum_scatter(up_terms, EVERY, scatter_dimension=0, tiled=True)
+
+    def middle_back_kernel(scalars_ref, *refs):
+        middle_ref, grad_ref, gain_ref, middle_grad_ref, low_ref, sums_ref = refs[2 * tensor_count :]
+        total = product(refs[:tensor_count], refs[tensor_count : 2 * tensor_count])
+        normed, scale_inv = norm_parts(middle_ref[...])
+        middle_grad = grad_ref[...].astype(full) + norm_backward(total, normed, scale_inv, gain_ref[...])
+        middle_grad_ref[...] = middle_grad
+        rounded = middle_grad.astype(low)
+        low_ref[...] = rounded
+        add_sums(sums_ref, total * normed, total, rounded.astype(full))
+
+    middle_grad, middle_low, second_sums = call(
+        middle_back_kernel,
+        "middle_back",
+        (blocks,),
+        scalars,
+        [(upper_grads, unit_spec(rank)) for rank in ranks]
+        + [(up_o_whole, weight_spec(rank)) for rank in ranks]
+        + [(middle, rows_spec(wide)), (out_grad, rows_spec(wide)), (row(ln2_gain), vector_spec())],
+        [
+            ((all_rows, wide), full, rows_spec(wide)),
+            ((all_rows, wide), low, rows_spec(wide)),
+            ((8, wide), full, sums_spec()),
+        ],
+        flops=2 * all_rows * wide * unit_width * tensor_count,
+    )
+
+    def o_block(rank):
+        block = lax.dynamic_slice_in_dim(up_o_whole, (tensor_rank ^ rank) * wide, wide, 0)
+        return block[:, unit_width:]
+
+    o_held = [by_lines(outer_sum(middle_low, mixed[rank], 1, o_width)) for rank in ranks]
+    o_held, middle_low = tie(o_held, middle_low)
+    mixed_grads = [matmul(middle_low, o_block(rank)).astype(low) for rank in ranks]
+    bits = replica_bits()[::-1]
+    halved = [halve(held, bits[0]) for held in o_held] if bits else o_held
+    halved, mixed_grads, out_parts = tie(halved, mixed_grads, out_parts)
+    for slot in range(count):
+        out_whole = lay(out_whole, out_parts[slot], slot)
+
+    def back(rank, which, kept):
+        return attention_back(
+            qvk[rank], mixed[rank], mixed_grads[rank], probs[rank], which, kept, rows, width, 2
+        )
+
+    def first_back_kernel(first_slot, scalars_ref, *refs):
+        images_ref, grad_ref, gain_ref = refs[2 * tensor_count : 2 * tensor_count + 3]
+        out_ref, whole_ref, sums_ref = refs[-3:]
+        total = product(refs[:tensor_count], refs[tensor_count : 2 * tensor_count])
+        normed, scale_inv = norm_parts(real_rows(images_ref[0]))
+        grad = grad_ref[...] + norm_backward(total, normed, scale_inv, gain_ref[...])
+        out_ref[0] = grad.astype(low)
+        whole_ref[0] = out_ref[0]
+        add_sums(sums_ref, total * normed, total)
+
+    qvk_grads, qvk_sums = [None] * tensor_count, [0.0] * tensor_count
+    for rank in ranks[1:]:
+        qvk_grads[rank], qvk_sums[rank] = back(rank, range(count), None)
+    for bit in bits[1:]:
+        halved = [halve(held, bit) for held in halved]
+    halved, qvk_grads[1:] = tie(halved, qvk_grads[1:])
+    far = [by_lines(outer_sum(first, grads, 1, qvk_width // 2)) for grads in qvk_grads[1:]]
+    o_held = halved[0]
+    for rank in ranks[1:]:
+        o_held = add_low(o_held, swap(halved[rank], "tensor", rank))
+    o_held, far, mixed_grads[0], out_whole = tie(o_held, far, mixed_grads[0], out_whole)
+    input_whole = None
+    third_sums = 0.0
+    in_parts = []
+    for slot in range(count):
+        qvk_grads[0], sums = back(0, range(slot, slot + 1), qvk_grads[0])
+        qvk_sums[0] = qvk_sums[0] + sums
+        if slot == 0:
+            far = [halve(held, bits[0]) for held in far] if bits else far
+            o_held = sum_lines(o_held)
+            far, o_held, qvk_grads[0], down_share = tie(far, o_held, qvk_grads[0], down_share)
+            down_grads = lax.all_gather(down_share, "replica", axis=0, tiled=True)
+        if slot == count - 1:
+            near = by_lines(outer_sum(first, qvk_grads[0], 1, qvk_width // 2))
+            near, in_parts, qvk_grads[0], far, o_grads, down_grads, up_grads = tie(
+                near, in_parts, qvk_grads[0], far, o_grads, down_grads, up_grads
+            )
+        ahead = [] if input_whole is None else [(input_whole, pl.BlockSpec(memory_space=pl.ANY))]
+        input_grad, input_whole, sums = call(
+            functools.partial(first_back_kernel, slot),
+            "first_back",
+            (2,),
+            scalars,
+            [(grads, rows_spec(qvk_width, slot)) for grads in qvk_grads]
+            + [(weight, fixed((wide, qvk_width), lambda i, s: (0, 0))) for weight in qvk_weights]
+            + [(images, slots_spec(slot)), (middle_grad, rows_spec(wide, slot)), (row(ln1_gain), vector_spec())]
+            + ahead,
+            [
+                ((1, length, wide), low, pl.BlockSpec((1, half, wide), lambda i, s: (0, i, 0))),
+                ((slots, length, wide), low, slots_spec(slot)),
+                ((8, wide), full, sums_spec()),
+            ],
+            flops=2 * rows * wide * qvk_width * tensor_count,
+            aliases={2 * tensor_count + 4: 1} if ahead else None,
+        )
+        third_sums = third_sums + sums
+        input_grad, mixed_grads[0] = tie(input_grad, mixed_grads[0])
+        in_parts.append(trade(input_grad))
+        if slot == 0:
+            for bit in bits[1:]:
+                far = [halve(held, bit) for held in far]
+            far, mixed_grads[0], up_share = tie(far, mixed_grads[0], up_share)
+            up_grads = lax.all_gather(up_share, "replica", axis=0, tiled=True)
+            o_grads = join_replicas(o_held)
+            far = [swap(held, "tensor", rank) for rank, held in zip(ranks[1:], far)]
+    for bit in bits:
+        near = halve(near, bit)
+    in_grads = join_replicas(sum_lines(add_low(near, *far)))
+
+    def all_ranks(parts, size):
+        whole = jnp.zeros((tensor_count * size,), full)
+        for rank in ranks:
+            whole = lax.dynamic_update_slice_in_dim(whole, parts[rank], (tensor_rank ^ rank) * size, 0)
+        return whole
+
+    vectors = [
+        third_sums[0],
+        third_sums[1],
+        all_ranks([sums[:width] for sums in qvk_sums], width),
+        all_ranks([sums[width : 2 * width] for sums in qvk_sums], width),
+        second_sums[2],
+        second_sums[0],
+        second_sums[1],
+        upper_sums[0].reshape(tensor_count, unit_width)[:, :units].reshape(-1),
+        first_sums[0],
+    ]
+    sizes = [vector.shape[0] for vector in vectors]
+    joined = jnp.concatenate(vectors)
+    padded = ceil_to(joined.shape[0], 8 * LANES)
+    summed = jnp.pad(joined, (0, padded - joined.shape[0])).reshape(-1, LANES)
+    summed = sum_over(sum_over(summed, "replica"), "fsdp")
+    summed, in_parts = tie(summed, in_parts)
+    summed = sum_over(summed, "tensor").reshape(-1)
+    for slot in range(count):
+        input_whole = lay(input_whole, in_parts[slot], slot)
+    ends, start = [], 0
+    for size in sizes:
+        share = size // tensor_count
+        ends.append(lax.dynamic_slice_in_dim(summed, start + tensor_rank * share, share, 0))
+        start += size
+    gain_one, shift_one, q_sum, v_sum, o_sum, gain_two, shift_two, up_sum, down_sum = ends
+    return (
+        out_whole,
+        input_whole,
+        gain_one,
+        shift_one,
+        in_grads[:, :width].astype(full),
+        q_sum,
+        in_grads[:, 2 * width : 3 * width].astype(full),
+        in_grads[:, width : 2 * width].astype(full),
+        v_sum,
+        o_grads[:, SHIFT : SHIFT + width].astype(full).T,
+        o_sum,
+        gain_two,
+        shift_two,
+        up_grads[:, :units].astype(full),
+        up_sum,
+        down_grads[:, :units].astype(full).T,
+        down_sum,
+    )
+
+
+def halves(size):
+    return size & (size - 1) == 0
+
+
+def by_images(mesh):
+    return SLOTS * MB % mesh.shape["tensor"] == 0 and all(halves(size) for size in mesh.shape.values())
+
+
 def solution(mesh):
     in_specs = (
         P(("replica", "fsdp"), None, None),
@@ -435,4 +1203,5 @@
         P("tensor", "fsdp"),
         P("tensor"),
     )
+    body = image_body if by_images(mesh) else split_heads_body
     return jax.shard_map(body, mesh=mesh, in_specs=in_specs, out_specs=out_specs, check_vma=False)

time: 2780 us -> 851 us (0.31)
  waiting for transfers between devices: 1390 us -> 129 us
  matrix products: 735 us -> 49.1 us
  Pallas kernels: 0 us -> 530 us
  other arithmetic: 261 us -> 26.1 us
  local copies, waits for them, and re-layouts: 263 us -> 49.1 us
  blocking collectives: 94.2 us -> 0 us
  starting transfers between devices: 13.5 us -> 47.7 us
    reduce_scatter x14 -> x2, waiting for transfers between devices: 704 us -> 0.04 us  [the longest x1 0.02 us: image_body(): lax.psum_scatter(up_terms, EVERY, scatter_dimension=0, tiled=True)]
    all_gather x18 -> x4, waiting for transfers between devices: 612 us -> 0.01 us  [the longest x2 0.01 us: gather_whole(): return lax.all_gather(part, EVERY, axis=0, tiled=True)]
    dot_general x36 -> x0, matrix products: 558 us -> none  [the longest x12 147 us: matmul_tn(): lax.dot_general(first_op, second_op, (((0,), (0,)), ((), ())), preferred_...]
    pallas_call x0 -> x25, Pallas kernels: none -> 530 us  [call(): pl.pallas_call(kernel, grid_spec=pltpu.PrefetchScalarGridSpec(num_scalar_...]
    convert_element_type x21 -> x17, other arithmetic: 157 us -> 17.2 us  [the longest x11 7.5 us: add_low(): return total.astype(jnp.bfloat16)]
    ppermute x0 -> x61, waiting for transfers between devices: none -> 129 us  [the longest x52 107 us: swap(): lax.ppermute(array, axis, [(rank, rank ^ bits) for rank in range(size)])]
    dot_general x12 -> x4, matrix products: 177 us -> 49.1 us  [matmul(): return jnp.dot(first_op, second_op, preferred_element_type=jnp.float32)]
    reshape x16 -> x9, local copies, waits for them, and re-layouts: 100 us -> 4.37 us  [the longest x6 3.58 us: row(): return vector.reshape(1, -1)]
  transfers between devices with their start and end apart: 33 -> 67, of which waited for: 21 -> 20; matrix products, arithmetic and copies ran while one was open for 43% -> 12% of each run, Pallas kernels for 0% -> 62%
where the time goes in v1:
time: 851 us; the launch traced here: 847 us
  Pallas kernels  530 us (62%)
  waiting for transfers between devices  129 us (15%)
  local copies, waits for them, and re-layouts  49.1 us (6%)
  matrix products  49.1 us (6%)
  starting transfers between devices  47.7 us (6%)
  other arithmetic  26.1 us (3%)
  between operations  15.4 us (2%)
    pallas_call x25, Pallas kernels, call(): pl.pallas_call(kernel, grid_spec=pltpu.PrefetchScalarGridSpec(num_scalar_...  530 us
    ppermute x52, waiting for transfers between devices, swap(): lax.ppermute(array, axis, [(rank, rank ^ bits) for rank in range(size)])  107 us
    dot_general x4, matrix products, matmul(): return jnp.dot(first_op, second_op, preferred_element_type=jnp.float32)  49.1 us
    ppermute x52, starting transfers between devices, swap(): lax.ppermute(array, axis, [(rank, rank ^ bits) for rank in range(size)])  31.9 us
    ppermute x9, waiting for transfers between devices, turn(): lax.ppermute(array, axis, [(rank, (rank + steps) % size) for rank in rang...  22.5 us
  transfers between devices with their start and end apart: 67, of which 20 were waited for; matrix products, arithmetic and copies ran while one was open for 12% of the time, Pallas kernels for 62%

profile of v1, /device:TPU:0, one launch (start us, length us, event | category | flops | bytes accessed | tf_op | source)
XLA Modules:
  0.0 847.1 jit_solution(12280904916224271020)
XLA Ops:
  25.2 11.4 %first_norm.1 = (bf16[2208,1152]{1,0:T(8,128)(2,1)}, bf16[2208,1152]{1,0:T(8,128)(2,1)}, f32[8,1152]{1,0:T(8,128)}) custom-call(s32[6]{0:T(128)} %pad_add_fusion.scalars_ref, bf16[6,729,1152]{2,1,0:T(8,128)(2,1)} %refs_4_.7, bf16[6,729,1152]{2,1,0:T(8,128)(2,1)} %cot_ref.1, f32[1,1152]{1,0:T(1,128)} %reshape.133.gain_ref.refs_6_, f32[1,1152]{1,0:T(1,128)} %reshape.134.shift_ref), custom_call_target="tpu_custom_call" | custom-call | bytes 20164608 | tf_op jit(solution)/shard_map/first_norm/pallas_call | solution.py:416
  51.9 6.6 collective-permute-done.16.refs_4_
  82.4 15.6 %multiply_convert_fusion.1.qvk_ref = bf16[2208,1792]{1,0:T(8,128)(2,1)} fusion(bf16[2208,1152]{1,0:T(8,128)(2,1)} %get-tuple-element.113.left_ref, bf16[1152,1792]{1,0:T(8,128)(2,1)} %bitcast.99, f32[1792]{0:T(1024)S(1)} %fusion.13, f32[1792]{0:T(1024)S(1)} %select_maximum_fusion.1), kind=kOutput, calls=%fused_computation.1 | convolution fusion | flops 9128189952 | bytes 17143808 | tf_op jit(solution)/shard_map/dot_general | solution.py:19
  105.5 30.9 %attention.2 = (bf16[2208,768]{1,0:T(8,128)(2,1)}, bf16[24,736,736]{2,1,0:T(8,128)(2,1)}) custom-call(s32[1]{0:T(128)} %constant.211.clone.1.none_ref, bf16[2208,1792]{1,0:T(8,128)(2,1)} %multiply_convert_fusion.1.qvk_ref), custom_call_target="tpu_custom_call" | custom-call | flops 13312720896 | bytes 7913472 | tf_op jit(solution)/shard_map/attention/pallas_call | solution.py:416
  138.1 5.6 place.5
  143.7 15.8 %multiply_convert_fusion.qvk_ref = bf16[2208,1792]{1,0:T(8,128)(2,1)} fusion(bf16[2208,1152]{1,0:T(8,128)(2,1)} %get-tuple-element.113.left_ref, bf16[1152,1792]{1,0:T(8,128)(2,1)} %bitcast.103, f32[1792]{0:T(1024)S(1)} %select_maximum_fusion, f32[1792]{0:T(1024)S(1)} %fusion.13), kind=kOutput, calls=%fused_computation | convolution fusion | flops 9128189952 | bytes 17143808 | tf_op jit(solution)/shard_map/dot_general | solution.py:19
  159.6 30.7 %attention.3 = (bf16[2208,768]{1,0:T(8,128)(2,1)}, bf16[24,736,736]{2,1,0:T(8,128)(2,1)}) custom-call(s32[1]{0:T(128)} %constant.211.clone.1.none_ref, bf16[2208,1792]{1,0:T(8,128)(2,1)} %multiply_convert_fusion.qvk_ref), custom_call_target="tpu_custom_call" | custom-call | flops 13312720896 | bytes 7913472 | tf_op jit(solution)/shard_map/attention/pallas_call | solution.py:416
  190.3 17.3 %middle_norm.1 = (f32[2208,1152]{1,0:T(8,128)}, bf16[2208,1152]{1,0:T(8,128)(2,1)}) custom-call(s32[6]{0:T(128)} %pad_add_fusion.scalars_ref, bf16[2208,768]{1,0:T(8,128)(2,1)} %get-tuple-element.121.refs_0_.right_ref.mixed_ref, bf16[2208,768]{1,0:T(8,128)(2,1)} %get-tuple-element.123.refs_1_.right_ref.mixed_ref, ...), custom_call_target="tpu_custom_call" | custom-call | flops 7813988352 | bytes 45186048 | tf_op jit(solution)/shard_map/middle_norm/pallas_call | solution.py:416
  207.6 48.5 %hidden.1 = (bf16[2208,4608]{1,0:T(8,128)(2,1)}, bf16[2208,4608]{1,0:T(8,128)(2,1)}) custom-call(s32[6]{0:T(128)} %pad_add_fusion.scalars_ref, bf16[2208,1152]{1,0:T(8,128)(2,1)} %get-tuple-element.125.second_ref.left_ref, bf16[2304,3072]{1,0:T(8,128)(2,1)} %all-gather.5.cloned.1.call-done.refs_2_.refs_3_.weight_ref, f32[1,4608]{1,0:T(1,128)} %bitcast.119), custom_call_target="tpu_custom_call" | custom-call | flops 23441965056 | bytes 19261440 | tf_op jit(solution)/shard_map/hidden/pallas_call | solution.py:416
  256.2 31.1 %outer_sum.6 = bf16[2304,2304]{1,0:T(8,128)(2,1)} custom-call(s32[1]{0:T(128)} %constant.211.clone.1.none_ref, bf16[2208,1152]{1,0:T(8,128)(2,1)} %get-tuple-element.132.left_ref.grad_ref.refs_5_, bf16[2208,4608]{1,0:T(8,128)(2,1)} %get-tuple-element.128.right_ref.refs_0_.refs_1_), custom_call_target="tpu_custom_call" | custom-call | flops 23441965056 | bytes 25436160 | tf_op jit(solution)/shard_map/outer_sum/pallas_call | solution.py:416
  288.6 36.2 %output.1 = (bf16[3,729,1152]{2,1,0:T(8,128)(2,1)}, bf16[6,729,1152]{2,1,0:T(8,128)(2,1)}) custom-call(s32[6]{0:T(128)} %pad_add_fusion.scalars_ref, bf16[2208,4608]{1,0:T(8,128)(2,1)} %get-tuple-element.128.right_ref.refs_0_.refs_1_, bf16[2208,4608]{1,0:T(8,128)(2,1)} %get-tuple-element.128.right_ref.refs_0_.refs_1_, ...), custom_call_target="tpu_custom_call" | custom-call | flops 23441965056 | bytes 72110592 | tf_op jit(solution)/shard_map/output/pallas_call | solution.py:416
  333.1 37.4 %hidden_back.1 = (bf16[2208,4608]{1,0:T(8,128)(2,1)}, f32[8,4608]{1,0:T(8,128)}) custom-call(s32[6]{0:T(128)} %pad_add_fusion.scalars_ref, bf16[2208,1152]{1,0:T(8,128)(2,1)} %get-tuple-element.132.left_ref.grad_ref.refs_5_, bf16[2304,2304]{1,0:T(8,128)(2,1)} %all-gather.7.cloned.1.call-done.refs_2_.refs_3_.weight_ref, ...), custom_call_target="tpu_custom_call" | custom-call | flops 23441965056 | bytes 36052992 | tf_op jit(solution)/shard_map/hidden_back/pallas_call | solution.py:416
  370.5 31.3 %outer_sum.7 = bf16[2304,2304]{1,0:T(8,128)(2,1)} custom-call(s32[1]{0:T(128)} %constant.211.clone.1.none_ref, bf16[2208,1152]{1,0:T(8,128)(2,1)} %get-tuple-element.125.second_ref.left_ref, bf16[2208,4608]{1,0:T(8,128)(2,1)} %get-tuple-element.135.right_ref.refs_0_.refs_1_), custom_call_target="tpu_custom_call" | custom-call | flops 23441965056 | bytes 25436160 | tf_op jit(solution)/shard_map/outer_sum/pallas_call | solution.py:416
  401.9 42.0 %middle_back.1 = (f32[2208,1152]{1,0:T(8,128)}, bf16[2208,1152]{1,0:T(8,128)(2,1)}, f32[8,1152]{1,0:T(8,128)}) custom-call(s32[6]{0:T(128)} %pad_add_fusion.scalars_ref, bf16[2208,4608]{1,0:T(8,128)(2,1)} %get-tuple-element.135.right_ref.refs_0_.refs_1_, bf16[2208,4608]{1,0:T(8,128)(2,1)} %get-tuple-element.135.right_ref.refs_0_.refs_1_, ...), custom_call_target="tpu_custom_call" | custom-call | flops 23441965056 | bytes 84275712 | tf_op jit(solution)/shard_map/middle_back/pallas_call | solution.py:416
  443.9 9.1 %outer_sum.9 = bf16[1152,768]{1,0:T(8,128)(2,1)} custom-call(s32[1]{0:T(128)} %constant.211.clone.1.none_ref, bf16[2208,1152]{1,0:T(8,128)(2,1)} %get-tuple-element.139.left_ref, bf16[2208,768]{1,0:T(8,128)(2,1)} %get-tuple-element.123.refs_1_.right_ref.mixed_ref), custom_call_target="tpu_custom_call" | custom-call | flops 3906994176 | bytes 8478720 | tf_op jit(solution)/shard_map/outer_sum/pallas_call | solution.py:416
  453.0 9.2 %outer_sum.8 = bf16[1152,768]{1,0:T(8,128)(2,1)} custom-call(s32[1]{0:T(128)} %constant.211.clone.1.none_ref, bf16[2208,1152]{1,0:T(8,128)(2,1)} %get-tuple-element.139.left_ref, bf16[2208,768]{1,0:T(8,128)(2,1)} %get-tuple-element.121.refs_0_.right_ref.mixed_ref), custom_call_target="tpu_custom_call" | custom-call | flops 3906994176 | bytes 8478720 | tf_op jit(solution)/shard_map/outer_sum/pallas_call | solution.py:416
  464.3 9.5 %convolution_convert_fusion.grad_ref = bf16[2208,768]{1,0:T(8,128)(2,1)} fusion(bf16[2208,1152]{1,0:T(8,128)(2,1)} %get-tuple-element.139.left_ref, bf16[2304,3072]{1,0:T(8,128)(2,1)} %all-gather.5.cloned.1.call-done.refs_2_.refs_3_.weight_ref, s32[]{:T(128)S(6)} %select_n.213, s32[]{:T(128)S(6)} %add.480), kind=kOutput, calls=%fused_computation.2 | convolution fusion | flops 3908689920 | bytes 10248200 | tf_op jit(solution)/shard_map/dot_general | solution.py:19
  473.9 8.2 convolution_convert_fusion.1.grad_ref
  487.6 44.4 %attention_back.4 = (bf16[2208,1792]{1,0:T(8,128)(2,1)}, f32[3,8,1792]{2,1,0:T(8,128)}) custom-call(s32[1]{0:T(128)} %constant.211.clone.1.none_ref, bf16[2208,1792]{1,0:T(8,128)(2,1)} %multiply_convert_fusion.qvk_ref, bf16[2208,768]{1,0:T(8,128)(2,1)} %get-tuple-element.123.refs_1_.right_ref.mixed_ref, bf16[2208,768]{1,0:T(8,128)(2,1)} %convolution_convert_fusion.grad_ref, ...), custom_call_target="tpu_custom_call" | custom-call | flops 26625441792 | bytes 40697856 | tf_op jit(solution)/shard_map/attention_back/pallas_call | solution.py:416
  539.4 16.7 %outer_sum.10 = bf16[1152,1792]{1,0:T(8,128)(2,1)} custom-call(s32[1]{0:T(128)} %constant.211.clone.1.none_ref, bf16[2208,1152]{1,0:T(8,128)(2,1)} %get-tuple-element.113.left_ref, bf16[2208,1792]{1,0:T(8,128)(2,1)} %get-tuple-element.148.right_ref.refs_1_), custom_call_target="tpu_custom_call" | custom-call | flops 9116319744 | bytes 13000704 | tf_op jit(solution)/shard_map/outer_sum/pallas_call | solution.py:416
  566.9 17.7 %attention_back.5 = (bf16[2208,1792]{1,0:T(8,128)(2,1)}, f32[1,8,1792]{2,1,0:T(8,128)}) custom-call(s32[1]{0:T(128)} %constant.211.clone.1.none_ref, bf16[2208,1792]{1,0:T(8,128)(2,1)} %multiply_convert_fusion.1.qvk_ref, bf16[2208,768]{1,0:T(8,128)(2,1)} %get-tuple-element.121.refs_0_.right_ref.mixed_ref, ...), custom_call_target="tpu_custom_call" | custom-call | flops 8875147264 | bytes 40697856 | tf_op jit(solution)/shard_map/attention_back/pallas_call | solution.py:416
  593.6 23.3 %collective-permute-done.44.refs_1_ = bf16[1,72,768]{2,1,0:T(8,128)(2,1)S(1)} collective-permute-done((bf16[1,72,768]{2,1,0:T(8,128)(2,1)S(1)}, bf16[1,72,768]{2,1,0:T(8,128)(2,1)S(1)}, u32[]{:S(2)}, u32[]{:S(2)}) %collective-permute-start.44) | collective-permute-done | bytes 110624 | tf_op jit(solution)/shard_map/ppermute | solution.py:601
  616.9 16.2 %first_back.3 = (bf16[1,729,1152]{2,1,0:T(8,128)(2,1)}, bf16[6,729,1152]{2,1,0:T(8,128)(2,1)}, f32[8,1152]{1,0:T(8,128)}) custom-call(s32[6]{0:T(128)} %pad_add_fusion.scalars_ref, bf16[2208,1792]{1,0:T(8,128)(2,1)} %get-tuple-element.162.refs_0_, bf16[2208,1792]{1,0:T(8,128)(2,1)} %get-tuple-element.148.right_ref.refs_1_, bf16[1152,1792]{1,0:T(8,128)(2,1)} %bitcast.100, ...), custom_call_target="tpu_custom_call" | custom-call | flops 6077546496 | bytes 44341248 | tf_op jit(solution)/shard_map/first_back/pallas_call | solution.py:416
  640.6 17.5 %attention_back.6 = (bf16[2208,1792]{1,0:T(8,128)(2,1)}, f32[1,8,1792]{2,1,0:T(8,128)}) custom-call(s32[1]{0:T(128)} %constant.211.clone.1.none_ref, bf16[2208,1792]{1,0:T(8,128)(2,1)} %multiply_convert_fusion.1.qvk_ref, bf16[2208,768]{1,0:T(8,128)(2,1)} %get-tuple-element.121.refs_0_.right_ref.mixed_ref, ...), custom_call_target="tpu_custom_call", output_to_operand_aliasing={{0}: (5, {})} | custom-call | flops 8875147264 | bytes 48611328 | tf_op jit(solution)/shard_map/attention_back/pallas_call | solution.py:416
  658.1 15.8 %first_back.4 = (bf16[1,729,1152]{2,1,0:T(8,128)(2,1)}, bf16[6,729,1152]{2,1,0:T(8,128)(2,1)}, f32[8,1152]{1,0:T(8,128)}) custom-call(s32[6]{0:T(128)} %pad_add_fusion.scalars_ref, bf16[2208,1792]{1,0:T(8,128)(2,1)} %get-tuple-element.168.refs_0_, bf16[2208,1792]{1,0:T(8,128)(2,1)} %get-tuple-element.148.right_ref.refs_1_, ...), custom_call_target="tpu_custom_call", output_to_operand_aliasing={{1}: (8, {})} | custom-call | flops 6077546496 | bytes 54418944 | tf_op jit(solution)/shard_map/first_back/pallas_call | solution.py:416
  674.3 18.0 %attention_back.7 = (bf16[2208,1792]{1,0:T(8,128)(2,1)}, f32[1,8,1792]{2,1,0:T(8,128)}) custom-call(s32[1]{0:T(128)} %constant.211.clone.1.none_ref, bf16[2208,1792]{1,0:T(8,128)(2,1)} %multiply_convert_fusion.1.qvk_ref, bf16[2208,768]{1,0:T(8,128)(2,1)} %get-tuple-element.121.refs_0_.right_ref.mixed_ref, ...), custom_call_target="tpu_custom_call", output_to_operand_aliasing={{0}: (5, {})} | custom-call | flops 8875147264 | bytes 48611328 | tf_op jit(solution)/shard_map/attention_back/pallas_call | solution.py:416
  694.0 16.4 %outer_sum.11 = bf16[1152,1792]{1,0:T(8,128)(2,1)} custom-call(s32[1]{0:T(128)} %constant.211.clone.1.none_ref, bf16[2208,1152]{1,0:T(8,128)(2,1)} %get-tuple-element.113.left_ref, bf16[2208,1792]{1,0:T(8,128)(2,1)} %get-tuple-element.179.right_ref.refs_0_), custom_call_target="tpu_custom_call" | custom-call | flops 9116319744 | bytes 13000704 | tf_op jit(solution)/shard_map/outer_sum/pallas_call | solution.py:416
  710.5 20.8 %collective-permute-done.42 = bf16[1,729,1152]{2,1,0:T(8,128)(2,1)S(1)} collective-permute-done((bf16[1,729,1152]{2,1,0:T(8,128)(2,1)}, bf16[1,729,1152]{2,1,0:T(8,128)(2,1)S(1)}, u32[]{:S(2)}, u32[]{:S(2)}) %collective-permute-start.42) | collective-permute-done | bytes 1679648 | tf_op jit(solution)/shard_map/ppermute | solution.py:601
  735.5 15.9 %first_back.5 = (bf16[1,729,1152]{2,1,0:T(8,128)(2,1)}, bf16[6,729,1152]{2,1,0:T(8,128)(2,1)}, f32[8,1152]{1,0:T(8,128)}) custom-call(s32[6]{0:T(128)} %pad_add_fusion.scalars_ref, bf16[2208,1792]{1,0:T(8,128)(2,1)} %get-tuple-element.179.right_ref.refs_0_, bf16[2208,1792]{1,0:T(8,128)(2,1)} %get-tuple-element.148.right_ref.refs_1_, ...), custom_call_target="tpu_custom_call", output_to_operand_aliasing={{1}: (8, {})} | custom-call | flops 6077546496 | bytes 54418944 | tf_op jit(solution)/shard_map/first_back/pallas_call | solution.py:416
  768.3 24.4 %collective-permute-done.51 = bf16[1,729,1152]{2,1,0:T(8,128)(2,1)S(1)} collective-permute-done((bf16[1,729,1152]{2,1,0:T(8,128)(2,1)}, bf16[1,729,1152]{2,1,0:T(8,128)(2,1)S(1)}, u32[]{:S(2)}, u32[]{:S(2)}) %collective-permute-start.51) | collective-permute-done | bytes 1679648 | tf_op jit(solution)/shard_map/ppermute | solution.py:601
  810.9 12.1 %collective-permute-done.56 = bf16[1,72,1792]{2,1,0:T(8,128)(2,1)S(1)} collective-permute-done((bf16[1,72,1792]{2,1,0:T(8,128)(2,1)S(1)}, bf16[1,72,1792]{2,1,0:T(8,128)(2,1)S(1)}, u32[]{:S(2)}, u32[]{:S(2)}) %collective-permute-start.56) | collective-permute-done | bytes 258080 | tf_op jit(solution)/shard_map/ppermute | solution.py:606
  825.0 6.4 collective-permute-done.58.refs_1_
  (338 shorter events, 169.3 us)
Async XLA Ops:
  7.2 183.1 %all-gather.5.cloned.1.call-start = ((), (), s32[]{:S(2)}) async-start(), calls=%async_computation.2 | async-start | bytes 14598144 | tf_op jit(solution)/shard_map/all_gather | solution.py:656
  12.3 24.7 %collective-permute-start.2 = (bf16[1,72,1792]{2,1,0:T(8,128)(2,1)}, bf16[1,72,1792]{2,1,0:T(8,128)(2,1)}, u32[]{:S(2)}, u32[]{:S(2)}) collective-permute-start(bf16[1,72,1792]{2,1,0:T(8,128)(2,1)} %constant_dynamic-slice_fusion.12), channel_id=1, source_target_pairs={{0,6},{2,0},{4,2},{6,4},{1,7},{3,1},{5,3},{7,5},{8,14},{10,8},{12,... | collective-permute-start | bytes 774152 | tf_op jit(solution)/shard_map/ppermute | solution.py:606
  40.5 248.1 %all-gather.7.cloned.1.call-start = ((), (), s32[]{:S(2)}) async-start(), calls=%async_computation.3 | async-start | bytes 10948608 | tf_op jit(solution)/shard_map/all_gather | solution.py:656
  42.3 545.3 %reduce-scatter.3.cloned.1.call-start = ((), (), s32[]{:S(2)}) async-start(), calls=%async_computation.4 | async-start | bytes 10948608 | tf_op jit(solution)/shard_map/reduce_scatter | solution.py:919
  73.9 24.0 %collective-permute-start.18 = (bf16[1,72,1792]{2,1,0:T(8,128)(2,1)S(1)}, bf16[1,72,1792]{2,1,0:T(8,128)(2,1)S(1)}, u32[]{:S(2)}, u32[]{:S(2)}) collective-permute-start(bf16[1,72,1792]{2,1,0:T(8,128)(2,1)S(1)} %collective-permute-done.16.refs_4_), channel_id=1, source_target_pairs={{0,8},{8,0},{16,24},{24,16},{1,9},{9,1},{17,25},{25,17},{2,10},{10... | collective-permute-start | bytes 774152 | tf_op jit(solution)/shard_map/ppermute | solution.py:601
  81.8 23.7 %collective-permute-start.25 = (bf16[1,72,1792]{2,1,0:T(8,128)(2,1)S(1)}, bf16[1,72,1792]{2,1,0:T(8,128)(2,1)S(1)}, u32[]{:S(2)}, u32[]{:S(2)}) collective-permute-start(bf16[1,72,1792]{2,1,0:T(8,128)(2,1)S(1)} %collective-permute-done.24.refs_12_), channel_id=1, source_target_pairs={{0,16},{8,24},{16,0},{24,8},{1,17},{9,25},{17,1},{25,9},{2,18},{10... | collective-permute-start | bytes 774152 | tf_op jit(solution)/shard_map/ppermute | solution.py:601
  98.0 38.5 %collective-permute-start.26 = (bf16[1,72,1792]{2,1,0:T(8,128)(2,1)S(1)}, bf16[1,72,1792]{2,1,0:T(8,128)(2,1)S(1)}, u32[]{:S(2)}, u32[]{:S(2)}) collective-permute-start(bf16[1,72,1792]{2,1,0:T(8,128)(2,1)S(1)} %collective-permute-done.24.refs_12_), channel_id=1, source_target_pairs={{0,8},{8,0},{16,24},{24,16},{1,9},{9,1},{17,25},{25,17},{2,10},{10... | collective-permute-start | bytes 774152 | tf_op jit(solution)/shard_map/ppermute | solution.py:601
  98.1 38.4 %collective-permute-start.15 = (bf16[1,72,1792]{2,1,0:T(8,128)(2,1)S(1)}, bf16[1,72,1792]{2,1,0:T(8,128)(2,1)S(1)}, u32[]{:S(2)}, u32[]{:S(2)}) collective-permute-start(bf16[1,72,1792]{2,1,0:T(8,128)(2,1)S(1)} %collective-permute-done.13.refs_1_), channel_id=1, source_target_pairs={{0,8},{8,0},{16,24},{24,16},{1,9},{9,1},{17,25},{25,17},{2,10},{10... | collective-permute-start | bytes 774152 | tf_op jit(solution)/shard_map/ppermute | solution.py:601
  98.6 37.9 %collective-permute-start.19 = (bf16[1,72,1792]{2,1,0:T(8,128)(2,1)S(1)}, bf16[1,72,1792]{2,1,0:T(8,128)(2,1)S(1)}, u32[]{:S(2)}, u32[]{:S(2)}) collective-permute-start(bf16[1,72,1792]{2,1,0:T(8,128)(2,1)S(1)} %collective-permute-done.17.refs_5_), channel_id=1, source_target_pairs={{0,8},{8,0},{16,24},{24,16},{1,9},{9,1},{17,25},{25,17},{2,10},{10... | collective-permute-start | bytes 774152 | tf_op jit(solution)/shard_map/ppermute | solution.py:601
  100.3 36.2 %collective-permute-start.23 = (bf16[1,72,1792]{2,1,0:T(8,128)(2,1)S(1)}, bf16[1,72,1792]{2,1,0:T(8,128)(2,1)S(1)}, u32[]{:S(2)}, u32[]{:S(2)}) collective-permute-start(bf16[1,72,1792]{2,1,0:T(8,128)(2,1)S(1)} %collective-permute-done.21.refs_9_), channel_id=1, source_target_pairs={{0,8},{8,0},{16,24},{24,16},{1,9},{9,1},{17,25},{25,17},{2,10},{10... | collective-permute-start | bytes 774152 | tf_op jit(solution)/shard_map/ppermute | solution.py:601
  105.5 31.0 %collective-permute-start.27 = (bf16[1,72,1792]{2,1,0:T(8,128)(2,1)S(1)}, bf16[1,72,1792]{2,1,0:T(8,128)(2,1)S(1)}, u32[]{:S(2)}, u32[]{:S(2)}) collective-permute-start(bf16[1,72,1792]{2,1,0:T(8,128)(2,1)S(1)} %collective-permute-done.25.refs_13_), channel_id=1, source_target_pairs={{0,8},{8,0},{16,24},{24,16},{1,9},{9,1},{17,25},{25,17},{2,10},{10... | collective-permute-start | bytes 774152 | tf_op jit(solution)/shard_map/ppermute | solution.py:601
  287.3 351.4 %reduce-scatter.5.cloned.1.call-start = ((), (), s32[]{:S(2)}) async-start(), calls=%async_computation.5 | async-start | bytes 10948608 | tf_op jit(solution)/shard_map/reduce_scatter | solution.py:990
  330.0 152.5 %collective-permute-start.32 = (bf16[1,729,1152]{2,1,0:T(8,128)(2,1)}, bf16[1,729,1152]{2,1,0:T(8,128)(2,1)}, u32[]{:S(2)}, u32[]{:S(2)}) collective-permute-start(bf16[1,729,1152]{2,1,0:T(8,128)(2,1)} %get-tuple-element.212), channel_id=1, source_target_pairs={{0,1},{1,0},{2,3},{3,2},{4,5},{5,4},{6,7},{7,6},{8,9},{9,8},{10,11... | collective-permute-start | bytes 5038856 | tf_op jit(solution)/shard_map/ppermute | solution.py:601
  331.1 151.4 %collective-permute-start.31 = (bf16[1,729,1152]{2,1,0:T(8,128)(2,1)}, bf16[1,729,1152]{2,1,0:T(8,128)(2,1)}, u32[]{:S(2)}, u32[]{:S(2)}) collective-permute-start(bf16[1,729,1152]{2,1,0:T(8,128)(2,1)} %get-tuple-element.213), channel_id=1, source_target_pairs={{0,1},{1,0},{2,3},{3,2},{4,5},{5,4},{6,7},{7,6},{8,9},{9,8},{10,11... | collective-permute-start | bytes 5038856 | tf_op jit(solution)/shard_map/ppermute | solution.py:601
  332.1 150.5 %collective-permute-start.30 = (bf16[1,729,1152]{2,1,0:T(8,128)(2,1)}, bf16[1,729,1152]{2,1,0:T(8,128)(2,1)}, u32[]{:S(2)}, u32[]{:S(2)}) collective-permute-start(bf16[1,729,1152]{2,1,0:T(8,128)(2,1)} %get-tuple-element.214), channel_id=1, source_target_pairs={{0,1},{1,0},{2,3},{3,2},{4,5},{5,4},{6,7},{7,6},{8,9},{9,8},{10,11... | collective-permute-start | bytes 5038856 | tf_op jit(solution)/shard_map/ppermute | solution.py:601
  401.9 308.6 %all-gather.9.cloned.1.call-start = ((), (), s32[]{:S(2)}) async-start(), calls=%async_computation.6 | async-start | bytes 1658880 | tf_op jit(solution)/shard_map/all_gather | solution.py:1067
  482.6 55.1 %collective-permute-start.34 = (bf16[4,72,768]{2,1,0:T(8,128)(2,1)S(1)}, bf16[4,72,768]{2,1,0:T(8,128)(2,1)S(1)}, u32[]{:S(2)}, u32[]{:S(2)}) collective-permute-start(bf16[4,72,768]{2,1,0:T(8,128)(2,1)S(1)} %dynamic-slice_bitcast_fusion.2), channel_id=1, source_target_pairs={{0,16},{8,24},{16,0},{24,8},{1,17},{9,25},{17,1},{25,9},{2,18},{10... | collective-permute-start | bytes 1327112 | tf_op jit(solution)/shard_map/ppermute | solution.py:601
  483.4 54.4 %collective-permute-start.33 = (bf16[4,72,768]{2,1,0:T(8,128)(2,1)S(1)}, bf16[4,72,768]{2,1,0:T(8,128)(2,1)S(1)}, u32[]{:S(2)}, u32[]{:S(2)}) collective-permute-start(bf16[4,72,768]{2,1,0:T(8,128)(2,1)S(1)} %dynamic-slice_bitcast_fusion.3), channel_id=1, source_target_pairs={{0,16},{8,24},{16,0},{24,8},{1,17},{9,25},{17,1},{25,9},{2,18},{10... | collective-permute-start | bytes 1327112 | tf_op jit(solution)/shard_map/ppermute | solution.py:601
  560.9 23.8 %collective-permute-start.36 = (bf16[4,2,72,1792]{3,2,0,1:T(8,128)(2,1)S(1)}, bf16[4,2,72,1792]{3,2,0,1:T(8,128)(2,1)}, u32[]{:S(2)}, u32[]{:S(2)}) collective-permute-start(bf16[4,2,72,1792]{3,2,0,1:T(8,128)(2,1)S(1)} %copy_bitcast_fusion.1), channel_id=1, source_target_pairs={{0,8},{8,0},{16,24},{24,16},{1,9},{9,1},{17,25},{25,17},{2,10},{10... | collective-permute-start | bytes 6193160 | tf_op jit(solution)/shard_map/ppermute | solution.py:601
  561.9 22.7 %collective-permute-start.37 = (bf16[1,72,768]{2,1,0:T(8,128)(2,1)S(1)}, bf16[1,72,768]{2,1,0:T(8,128)(2,1)S(1)}, u32[]{:S(2)}, u32[]{:S(2)}) collective-permute-start(bf16[1,72,768]{2,1,0:T(8,128)(2,1)S(1)} %get-tuple-element.221), channel_id=1, source_target_pairs={{0,2},{2,4},{4,6},{6,0},{1,3},{3,5},{5,7},{7,1},{8,10},{10,12},{12... | collective-permute-start | bytes 331784 | tf_op jit(solution)/shard_map/ppermute | solution.py:606
  561.9 22.7 %collective-permute-start.39 = (bf16[1,72,768]{2,1,0:T(8,128)(2,1)S(1)}, bf16[1,72,768]{2,1,0:T(8,128)(2,1)S(1)}, u32[]{:S(2)}, u32[]{:S(2)}) collective-permute-start(bf16[1,72,768]{2,1,0:T(8,128)(2,1)S(1)} %get-tuple-element.222), channel_id=1, source_target_pairs={{0,6},{2,0},{4,2},{6,4},{1,7},{3,1},{5,3},{7,5},{8,14},{10,8},{12,... | collective-permute-start | bytes 331784 | tf_op jit(solution)/shard_map/ppermute | solution.py:606
  587.7 49.6 %collective-permute-start.40 = (bf16[4,72,1792]{2,1,0:T(8,128)(2,1)S(1)}, bf16[4,72,1792]{2,1,0:T(8,128)(2,1)}, u32[]{:S(2)}, u32[]{:S(2)}) collective-permute-start(bf16[4,72,1792]{2,1,0:T(8,128)(2,1)S(1)} %dynamic-slice_bitcast_fusion.1), channel_id=1, source_target_pairs={{0,16},{8,24},{16,0},{24,8},{1,17},{9,25},{17,1},{25,9},{2,18},{10... | collective-permute-start | bytes 3096584 | tf_op jit(solution)/shard_map/ppermute | solution.py:601
  591.8 25.0 %collective-permute-start.44 = (bf16[1,72,768]{2,1,0:T(8,128)(2,1)S(1)}, bf16[1,72,768]{2,1,0:T(8,128)(2,1)S(1)}, u32[]{:S(2)}, u32[]{:S(2)}) collective-permute-start(bf16[1,72,768]{2,1,0:T(8,128)(2,1)S(1)} %add_convert_fusion.3.refs_0_), channel_id=1, source_target_pairs={{0,16},{8,24},{16,0},{24,8},{1,17},{9,25},{17,1},{25,9},{2,18},{10... | collective-permute-start | bytes 331784 | tf_op jit(solution)/shard_map/ppermute | solution.py:601
  593.4 40.1 %collective-permute-start.45 = (bf16[1,72,768]{2,1,0:T(8,128)(2,1)S(1)}, bf16[1,72,768]{2,1,0:T(8,128)(2,1)S(1)}, u32[]{:S(2)}, u32[]{:S(2)}) collective-permute-start(bf16[1,72,768]{2,1,0:T(8,128)(2,1)S(1)} %add_convert_fusion.3.refs_0_), channel_id=1, source_target_pairs={{0,8},{8,0},{16,24},{24,16},{1,9},{9,1},{17,25},{25,17},{2,10},{10... | collective-permute-start | bytes 331784 | tf_op jit(solution)/shard_map/ppermute | solution.py:601
  593.5 137.8 %all-gather.11.cloned.1.call-start = ((), (), s32[]{:S(2)}) async-start(), calls=%async_computation.7 | async-start | bytes 1658880 | tf_op jit(solution)/shard_map/all_gather | solution.py:1098
  633.1 77.3 %collective-permute-start.41 = (bf16[1,729,1152]{2,1,0:T(8,128)(2,1)}, bf16[1,729,1152]{2,1,0:T(8,128)(2,1)}, u32[]{:S(2)}, u32[]{:S(2)}) collective-permute-start(bf16[1,729,1152]{2,1,0:T(8,128)(2,1)} %get-tuple-element.173), channel_id=1, source_target_pairs={{0,1},{1,0},{2,3},{3,2},{4,5},{5,4},{6,7},{7,6},{8,9},{9,8},{10,11... | collective-permute-start | bytes 5038856 | tf_op jit(solution)/shard_map/ppermute | solution.py:601
  638.8 71.7 %collective-permute-start.43 = (bf16[4,72,1792]{2,1,0:T(8,128)(2,1)S(1)}, bf16[4,72,1792]{2,1,0:T(8,128)(2,1)}, u32[]{:S(2)}, u32[]{:S(2)}) collective-permute-start(bf16[4,72,1792]{2,1,0:T(8,128)(2,1)S(1)} %fusion.5), channel_id=1, source_target_pairs={{0,1},{1,0},{2,3},{3,2},{4,5},{5,4},{6,7},{7,6},{8,9},{9,8},{10,11... | collective-permute-start | bytes 3096584 | tf_op jit(solution)/shard_map/ppermute | solution.py:601
  673.9 57.4 %collective-permute-start.42 = (bf16[1,729,1152]{2,1,0:T(8,128)(2,1)}, bf16[1,729,1152]{2,1,0:T(8,128)(2,1)S(1)}, u32[]{:S(2)}, u32[]{:S(2)}) collective-permute-start(bf16[1,729,1152]{2,1,0:T(8,128)(2,1)} %get-tuple-element.174), channel_id=1, source_target_pairs={{0,1},{1,0},{2,3},{3,2},{4,5},{5,4},{6,7},{7,6},{8,9},{9,8},{10,11... | collective-permute-start | bytes 5038856 | tf_op jit(solution)/shard_map/ppermute | solution.py:601
  735.5 23.5 %collective-permute-start.53 = (bf16[4,2,72,1792]{3,2,0,1:T(8,128)(2,1)}, bf16[4,2,72,1792]{3,2,0,1:T(8,128)(2,1)S(1)}, u32[]{:S(2)}, u32[]{:S(2)}) collective-permute-start(bf16[4,2,72,1792]{3,2,0,1:T(8,128)(2,1)} %copy_bitcast_fusion), channel_id=1, source_target_pairs={{0,8},{8,0},{16,24},{24,16},{1,9},{9,1},{17,25},{25,17},{2,10},{10... | collective-permute-start | bytes 6193160 | tf_op jit(solution)/shard_map/ppermute | solution.py:601
  753.5 39.2 %collective-permute-start.51 = (bf16[1,729,1152]{2,1,0:T(8,128)(2,1)}, bf16[1,729,1152]{2,1,0:T(8,128)(2,1)S(1)}, u32[]{:S(2)}, u32[]{:S(2)}) collective-permute-start(bf16[1,729,1152]{2,1,0:T(8,128)(2,1)} %get-tuple-element.195), channel_id=1, source_target_pairs={{0,1},{1,0},{2,3},{3,2},{4,5},{5,4},{6,7},{7,6},{8,9},{9,8},{10,11... | collective-permute-start | bytes 5038856 | tf_op jit(solution)/shard_map/ppermute | solution.py:601
  759.6 36.2 %collective-permute-start.54 = (bf16[4,72,1792]{2,1,0:T(8,128)(2,1)S(1)}, bf16[4,72,1792]{2,1,0:T(8,128)(2,1)S(1)}, u32[]{:S(2)}, u32[]{:S(2)}) collective-permute-start(bf16[4,72,1792]{2,1,0:T(8,128)(2,1)S(1)} %dynamic-slice_bitcast_fusion), channel_id=1, source_target_pairs={{0,16},{8,24},{16,0},{24,8},{1,17},{9,25},{17,1},{25,9},{2,18},{10... | collective-permute-start | bytes 3096584 | tf_op jit(solution)/shard_map/ppermute | solution.py:601
  792.7 38.7 %collective-permute-start.52 = (f32[112,128]{1,0:T(8,128)S(1)}, f32[112,128]{1,0:T(8,128)S(1)}, u32[]{:S(2)}, u32[]{:S(2)}) collective-permute-start(f32[112,128]{1,0:T(8,128)S(1)} %add.447), channel_id=1, source_target_pairs={{0,1},{1,0},{2,3},{3,2},{4,5},{5,4},{6,7},{7,6},{8,9},{9,8},{10,11... | collective-permute-start | bytes 172040 | tf_op jit(solution)/shard_map/ppermute | solution.py:601
  (91 other events, 1161.2 us)
Sparse Core Ops, SparseCore 0:
  40.6 116.6 all-gather.4
  160.7 85.2 all-gather.6
  287.5 169.1 reduce-scatter.2
  462.6 151.5 reduce-scatter.4
  615.6 17.0 all-gather.8
  674.4 16.7 all-gather.10

commit v2 on v1

--- a/solution.py
+++ b/solution.py
@@ -453,15 +453,24 @@
             mixed_ref[...] = jnp.zeros_like(mixed_ref)
 
         real = lax.broadcasted_iota(jnp.int32, (rows, rows), 1) < length
+
+        def head(item):
+            return (pl.program_id(1) * group + item) * HEAD
+
+        def scores_of(item):
+            at_q, _ = head_window(head(item), 0, rows)
+            at_k, in_k = head_window(head(item), 2 * width, rows)
+            key_rows = jnp.where(in_k, qvk_ref[:, at_k], 0)
+            return jnp.where(real, matmul_nt(qvk_ref[:, at_q], key_rows), -1e30)
+
+        following = scores_of(0)
         for item in range(group):
-            offset = (pl.program_id(1) * group + item) * HEAD
-            at_q, _ = head_window(offset, 0, rows)
-            at_v, in_v = head_window(offset, width, rows)
-            at_k, in_k = head_window(offset, 2 * width, rows)
-            at_o, in_o = head_window(offset, SHIFT, rows)
-            key_rows = jnp.where(in_k, qvk_ref[:, at_k], 0)
+            scores = following
+            if item + 1 < group:
+                following = scores_of(item + 1)
+            at_v, in_v = head_window(head(item), width, rows)
+            at_o, in_o = head_window(head(item), SHIFT, rows)
             value_rows = jnp.where(in_v, qvk_ref[:, at_v], 0)
-            scores = jnp.where(real, matmul_nt(qvk_ref[:, at_q], key_rows), -1e30)
             powers = jnp.exp(scores - jnp.max(scores, axis=1, keepdims=True))
             total = jnp.sum(powers, axis=1, keepdims=True)
             probs = (powers * (1.0 / total)).astype(jnp.bfloat16)
@@ -545,16 +554,19 @@
             (qvk.shape, jnp.bfloat16, pl.BlockSpec((rows, qvk.shape[1]), lambda i, g, s: (at + i, 0))),
             ((count, 8, qvk.shape[1]), jnp.float32, pl.BlockSpec((1, 8, qvk.shape[1]), lambda i, g, s: (i, 0, 0))),
         ],
+        aliases=None if kept is None else {5: 0},
         flops=8 * count * heads * rows * rows * WINDOW,
-        aliases=None if kept is None else {5: 0},
     )
     return grads, jnp.sum(sums[:, 0], axis=0)
 
 
 def place(pieces, slots, total):
     def kernel(slots_ref, *refs):
-        for at, ref in enumerate(refs[:-1]):
-            refs[-1][pl.ds(slots_ref[at], ref.shape[0])] = ref[...]
+        at = 0
+        for ref in refs[:-1]:
+            for block in range(ref.shape[0]):
+                refs[-1][pl.ds(slots_ref[at], 1)] = ref[block : block + 1]
+                at += 1
 
     def whole(shape):
         return fixed(shape, lambda i, s: (0, 0, 0))
@@ -564,31 +576,37 @@
         kernel,
         "place",
         (1,),
-        jnp.stack(slots).astype(jnp.int32),
+        jnp.stack([slot for group in slots for slot in group]).astype(jnp.int32),
         [(piece, whole(piece.shape)) for piece in pieces],
         [(shape, pieces[0].dtype, whole(shape))],
     )[0]
 
 
-def outer_sum(left, right, ranks, step):
+def outer_sum(left, right, ranks, step, total=None, kept=None, at=None, scalars=None):
     rows, lines = left.shape
     columns = right.shape[1] // ranks
     steps = columns // step
-
-    def kernel(none_ref, left_ref, right_ref, out_ref):
-        out_ref[...] = matmul_tn(left_ref[...], right_ref[...]).astype(out_ref.dtype)
+    held = ranks * lines if kept is None else kept.shape[0]
+
+    def kernel(scalars_ref, left_ref, right_ref, *refs):
+        refs[-1][...] = matmul_tn(left_ref[...], right_ref[...]).astype(refs[-1].dtype)
+
+    def place_of(t, j, s):
+        return (t, j) if kept is None else (s[at[0]], at[1])
 
     return call(
         kernel,
         "outer_sum",
         (ranks, steps),
-        jnp.zeros((1,), jnp.int32),
+        jnp.zeros((1,), jnp.int32) if scalars is None else scalars,
         [
             (left, fixed((rows, lines), lambda t, j, s: (0, 0))),
             (right, pl.BlockSpec((rows, step), lambda t, j, s: (0, t * steps + j))),
-        ],
-        [((ranks * lines, columns), jnp.bfloat16, pl.BlockSpec((lines, step), lambda t, j, s: (t, j)))],
+        ]
+        + ([] if kept is None else [(kept, pl.BlockSpec(memory_space=pl.ANY))]),
+        [((held, total or columns), jnp.bfloat16, pl.BlockSpec((lines, step), place_of))],
         flops=2 * rows * lines * columns * ranks,
+        aliases=None if kept is None else {3: 0},
     )[0]
 
 
@@ -615,10 +633,14 @@
     return bits
 
 
+def swap_found(found, bit):
+    return {**found, **{bits ^ bit: swap(held, "replica", bit) for bits, held in found.items()}}
+
+
 def among_replicas(piece):
     found = {0: piece}
     for bit in replica_bits():
-        found.update({bits ^ bit: swap(held, "replica", bit) for bits, held in list(found.items())})
+        found = swap_found(found, bit)
     return found
 
 
@@ -629,25 +651,37 @@
     return [mine] + [turn(mine, "fsdp", step) for step in range(1, lax.axis_size("fsdp"))]
 
 
-def gather_parts(shard, parts):
-    copies, lines, ranks = (lax.axis_size(axis) for axis in ("replica", "fsdp", "tensor"))
+def slots_of(found, skip):
+    copies, lines = lax.axis_size("replica"), lax.axis_size("fsdp")
     copy, line = lax.axis_index("replica"), lax.axis_index("fsdp")
+    starts = [(line - step) % lines * copies for step in range(skip, lines)]
+    return [[start + (copy ^ bits) for start in starts] for bits in found]
+
+
+def gather_own(shard, parts):
+    copies, lines, line = lax.axis_size("replica"), lax.axis_size("fsdp"), lax.axis_index("fsdp")
     blocks = shard.reshape(copies, -1, shard.shape[1])
-    wholes = []
-    for rank in range(ranks):
-        pieces, slots = [], []
-        for step in range(lines):
-            start = (line - step) % lines * copies
-            if rank == 0 and step == 0:
-                pieces.append(blocks)
-                slots.append(start)
-                continue
-            piece = parts[step] if rank == 0 else swap(parts[step], "tensor", rank)
-            for bits, held in among_replicas(piece).items():
-                pieces.append(held)
-                slots.append(start + (copy ^ bits))
-        wholes.append(place(pieces, slots, lines * copies).reshape(-1, shard.shape[1]))
-    return wholes
+    pieces, slots = [blocks], [[line * copies + at for at in range(copies)]]
+    if lines > 1:
+        found = among_replicas(jnp.concatenate(parts[1:], axis=0))
+        pieces += list(found.values())
+        slots += slots_of(found, 1)
+    return place(pieces, slots, lines * copies).reshape(-1, shard.shape[1])
+
+
+def gather_far(parts, rank):
+    found = {0: swap(jnp.concatenate(parts, axis=0), "tensor", rank)}
+    for bit in replica_bits()[:-1]:
+        found = swap_found(found, bit)
+    return found
+
+
+def finish_far(found):
+    for bit in replica_bits()[-1:]:
+        found = swap_found(found, bit)
+    total = lax.axis_size("replica") * lax.axis_size("fsdp")
+    whole = place(list(found.values()), slots_of(found, 0), total)
+    return whole.reshape(-1, whole.shape[2])
 
 
 def gather_whole(shard):
@@ -685,19 +719,20 @@
     return add_low(*terms)
 
 
-def join_replicas(piece):
+def place_found(found):
     copy = lax.axis_index("replica")
-    found = among_replicas(piece)
-    whole = place(list(found.values()), [copy ^ bits for bits in found], len(found))
-    return whole.reshape(-1, piece.shape[2])
-
-
-def sum_over(vector, axis):
-    bit = 1
-    while bit < lax.axis_size(axis):
-        vector = vector + swap(vector, axis, bit)
-        bit *= 2
-    return vector
+    whole = place(list(found.values()), [[copy ^ bits] for bits in found], len(found))
+    return whole.reshape(-1, whole.shape[2])
+
+
+def sum_over(vector, axes):
+    size = lax.axis_size(axes)
+    terms = [vector] + [
+        lax.ppermute(vector, axes, [(rank, rank ^ bits) for rank in range(size)]) for bits in range(1, size)
+    ]
+    while len(terms) > 1:
+        terms = [left + right for left, right in zip(terms[::2], terms[1::2])]
+    return terms[0]
 
 
 def norm_parts(values):
@@ -746,10 +781,11 @@
     qvk_width = ceil_to(3 * width, WINDOW)
     o_width = ceil_to(width + SHIFT, WINDOW)
     unit_width = ceil_to(units, WINDOW)
-    if unit_width % o_width:
-        unit_width = ceil_to(unit_width, o_width)
+    unit_width = ceil_to(unit_width, o_width)
     ranks = range(tensor_count)
     all_rows = count * rows
+    heads = width // HEAD
+    group = next(size for size in (8, 4, 2, 1) if heads % size == 0)
     blocks = all_rows // half
     scalars = jnp.concatenate(
         [
@@ -834,7 +870,8 @@
     up_o_shard, down_shard, parts = tie(up_o_shard, down_shard, parts)
     up_o_whole = gather_whole(up_o_shard)
     down_whole = gather_whole(down_shard)
-    qvk_weights = gather_parts(qvk_shard, parts)
+    qvk_weights = [gather_own(qvk_shard, parts)]
+    far_parts = [gather_far(parts, rank) for rank in ranks[1:]]
 
     def of_rank(vector, rank, size):
         return lax.dynamic_slice_in_dim(vector, (tensor_rank ^ rank) * size, size, 0)
@@ -847,7 +884,10 @@
             (0, qvk_width - 2 * width),
         )
         qvk.append(((matmul(first, qvk_weights[rank]) + shift_row) * scale_row).astype(low))
-        mixed_part, probs_part = attention(qvk[rank], length, rows, width, 4)
+        mixed_part, probs_part = attention(qvk[rank], length, rows, width, group)
+        if rank == 0:
+            mixed_part, first, far_parts = tie(mixed_part, first, far_parts)
+            qvk_weights += [finish_far(found) for found in far_parts]
         mixed.append(mixed_part)
         probs.append(probs_part)
 
@@ -879,7 +919,7 @@
         flops=2 * all_rows * wide * o_width * tensor_count,
     )
 
-    chunk = o_width if unit_width % o_width == 0 else unit_width
+    chunk = o_width
 
     def unit_rows():
         return pl.BlockSpec((half, unit_width), lambda t, i, s: (i, t))
@@ -955,7 +995,7 @@
         return whole
 
     output, out_grad = tie(output, out_grad)
-    out_parts = [trade(output[slot : slot + 1]) for slot in range(count)]
+    out_parts = trade(output)
 
     def hidden_back_kernel(scalars_ref, grad_ref, weight_ref, slope_ref, upper_ref, sums_ref):
         @pl.when(pl.program_id(1) == 0)
@@ -985,55 +1025,61 @@
         ],
         flops=2 * all_rows * wide * unit_width * tensor_count,
     )
-    up_terms = outer_sum(second, upper_grads, tensor_count, chunk)
+    up_terms = outer_sum(second, upper_grads, tensor_count, o_width, unit_width + o_width)
     up_terms, upper_grads = tie(up_terms, upper_grads)
-    up_share = lax.psum_scatter(up_terms, EVERY, scatter_dimension=0, tiled=True)
 
     def middle_back_kernel(scalars_ref, *refs):
-        middle_ref, grad_ref, gain_ref, middle_grad_ref, low_ref, sums_ref = refs[2 * tensor_count :]
+        middle_ref, grad_ref, gain_ref, *o_refs = refs[2 * tensor_count : 3 * tensor_count + 3]
+        middle_grad_ref, low_ref, sums_ref, *mixed_grad_refs = refs[3 * tensor_count + 3 :]
         total = product(refs[:tensor_count], refs[tensor_count : 2 * tensor_count])
         normed, scale_inv = norm_parts(middle_ref[...])
         middle_grad = grad_ref[...].astype(full) + norm_backward(total, normed, scale_inv, gain_ref[...])
         middle_grad_ref[...] = middle_grad
         rounded = middle_grad.astype(low)
         low_ref[...] = rounded
+        for o_ref, mixed_grad_ref in zip(o_refs, mixed_grad_refs):
+            mixed_grad_ref[...] = matmul(rounded, o_ref[...]).astype(low)
         add_sums(sums_ref, total * normed, total, rounded.astype(full))
 
-    middle_grad, middle_low, second_sums = call(
+    middle_grad, middle_low, second_sums, *mixed_grads = call(
         middle_back_kernel,
         "middle_back",
         (blocks,),
         scalars,
         [(upper_grads, unit_spec(rank)) for rank in ranks]
         + [(up_o_whole, weight_spec(rank)) for rank in ranks]
-        + [(middle, rows_spec(wide)), (out_grad, rows_spec(wide)), (row(ln2_gain), vector_spec())],
+        + [(middle, rows_spec(wide)), (out_grad, rows_spec(wide)), (row(ln2_gain), vector_spec())]
+        + [(up_o_whole, o_spec(rank)) for rank in ranks],
         [
             ((all_rows, wide), full, rows_spec(wide)),
             ((all_rows, wide), low, rows_spec(wide)),
             ((8, wide), full, sums_spec()),
-        ],
-        flops=2 * all_rows * wide * unit_width * tensor_count,
-    )
-
-    def o_block(rank):
-        block = lax.dynamic_slice_in_dim(up_o_whole, (tensor_rank ^ rank) * wide, wide, 0)
-        return block[:, unit_width:]
-
-    o_held = [by_lines(outer_sum(middle_low, mixed[rank], 1, o_width)) for rank in ranks]
-    o_held, middle_low = tie(o_held, middle_low)
-    mixed_grads = [matmul(middle_low, o_block(rank)).astype(low) for rank in ranks]
+        ]
+        + [((all_rows, o_width), low, rows_spec(o_width)) for rank in ranks],
+        flops=2 * all_rows * wide * (unit_width + o_width) * tensor_count,
+    )
+
+    for rank in ranks:
+        up_terms = outer_sum(
+            middle_low,
+            mixed[rank],
+            1,
+            o_width,
+            unit_width + o_width,
+            up_terms,
+            (1 + rank, unit_width // o_width),
+            scalars,
+        )
+    up_terms, mixed_grads[-1], out_parts = tie(up_terms, mixed_grads[-1], out_parts)
+    up_share = lax.psum_scatter(up_terms, EVERY, scatter_dimension=0, tiled=True)
     bits = replica_bits()[::-1]
-    halved = [halve(held, bits[0]) for held in o_held] if bits else o_held
-    halved, mixed_grads, out_parts = tie(halved, mixed_grads, out_parts)
-    for slot in range(count):
-        out_whole = lay(out_whole, out_parts[slot], slot)
 
     def back(rank, which, kept):
         return attention_back(
-            qvk[rank], mixed[rank], mixed_grads[rank], probs[rank], which, kept, rows, width, 2
+            qvk[rank], mixed[rank], mixed_grads[rank], probs[rank], which, kept, rows, width, group
         )
 
-    def first_back_kernel(first_slot, scalars_ref, *refs):
+    def first_back_kernel(scalars_ref, *refs):
         images_ref, grad_ref, gain_ref = refs[2 * tensor_count : 2 * tensor_count + 3]
         out_ref, whole_ref, sums_ref = refs[-3:]
         total = product(refs[:tensor_count], refs[tensor_count : 2 * tensor_count])
@@ -1044,35 +1090,18 @@
         add_sums(sums_ref, total * normed, total)
 
     qvk_grads, qvk_sums = [None] * tensor_count, [0.0] * tensor_count
-    for rank in ranks[1:]:
-        qvk_grads[rank], qvk_sums[rank] = back(rank, range(count), None)
-    for bit in bits[1:]:
-        halved = [halve(held, bit) for held in halved]
-    halved, qvk_grads[1:] = tie(halved, qvk_grads[1:])
-    far = [by_lines(outer_sum(first, grads, 1, qvk_width // 2)) for grads in qvk_grads[1:]]
-    o_held = halved[0]
-    for rank in ranks[1:]:
-        o_held = add_low(o_held, swap(halved[rank], "tensor", rank))
-    o_held, far, mixed_grads[0], out_whole = tie(o_held, far, mixed_grads[0], out_whole)
     input_whole = None
     third_sums = 0.0
     in_parts = []
-    for slot in range(count):
-        qvk_grads[0], sums = back(0, range(slot, slot + 1), qvk_grads[0])
-        qvk_sums[0] = qvk_sums[0] + sums
-        if slot == 0:
-            far = [halve(held, bits[0]) for held in far] if bits else far
-            o_held = sum_lines(o_held)
-            far, o_held, qvk_grads[0], down_share = tie(far, o_held, qvk_grads[0], down_share)
-            down_grads = lax.all_gather(down_share, "replica", axis=0, tiled=True)
-        if slot == count - 1:
-            near = by_lines(outer_sum(first, qvk_grads[0], 1, qvk_width // 2))
-            near, in_parts, qvk_grads[0], far, o_grads, down_grads, up_grads = tie(
-                near, in_parts, qvk_grads[0], far, o_grads, down_grads, up_grads
-            )
-        ahead = [] if input_whole is None else [(input_whole, pl.BlockSpec(memory_space=pl.ANY))]
-        input_grad, input_whole, sums = call(
-            functools.partial(first_back_kernel, slot),
+
+    def attend(rank, which):
+        qvk_grads[rank], sums = back(rank, which, qvk_grads[rank])
+        qvk_sums[rank] = qvk_sums[rank] + sums
+
+    def first_back(slot, whole):
+        ahead = [] if whole is None else [(whole, pl.BlockSpec(memory_space=pl.ANY))]
+        return call(
+            first_back_kernel,
             "first_back",
             (2,),
             scalars,
@@ -1085,22 +1114,98 @@
                 ((slots, length, wide), low, slots_spec(slot)),
                 ((8, wide), full, sums_spec()),
             ],
+            aliases={2 * tensor_count + 4: 1} if ahead else None,
             flops=2 * rows * wide * qvk_width * tensor_count,
-            aliases={2 * tensor_count + 4: 1} if ahead else None,
         )
+
+    last = count - 1
+
+    def halve_all(terms, which):
+        for bit in which:
+            terms = [halve(term, bit) for term in terms]
+        return terms
+
+    def join_on(found, which):
+        for bit in which:
+            found = swap_found(found, bit)
+        return found
+
+    far_bits, far_bit = replica_bits()[:-1], replica_bits()[-1:]
+
+    down_found = join_on({0: down_share[None]}, far_bits)
+    for rank in ranks[1:]:
+        attend(rank, range(count))
+    qvk_grads[1:], mixed_grads[0], down_found, first = tie(qvk_grads[1:], mixed_grads[0], down_found, first)
+    far = [by_lines(outer_sum(first, grads, 1, qvk_width // 2)) for grads in qvk_grads[1:]]
+    down_grads = place_found(join_on(down_found, far_bit))
+    far, mixed_grads[0], down_grads = tie(far, mixed_grads[0], down_grads)
+    far_done = 0
+    for slot in range(last):
+        if slot > 0:
+            in_parts.append(trade(input_grad))
+        attend(0, range(slot, slot + 1))
+        if slot == 0:
+            far = halve_all(far, bits[:1])
+            far, qvk_grads[0] = tie(far, qvk_grads[0])
+        elif far_done == 1:
+            far = halve_all(far, bits[1:])
+        far_done += 1
+        input_grad, input_whole, sums = first_back(slot, input_whole)
         third_sums = third_sums + sums
-        input_grad, mixed_grads[0] = tie(input_grad, mixed_grads[0])
+        far, in_parts, input_grad, mixed_grads[0] = tie(far, in_parts, input_grad, mixed_grads[0])
+    if last > 0:
         in_parts.append(trade(input_grad))
-        if slot == 0:
-            for bit in bits[1:]:
-                far = [halve(held, bit) for held in far]
-            far, mixed_grads[0], up_share = tie(far, mixed_grads[0], up_share)
-            up_grads = lax.all_gather(up_share, "replica", axis=0, tiled=True)
-            o_grads = join_replicas(o_held)
-            far = [swap(held, "tensor", rank) for rank, held in zip(ranks[1:], far)]
-    for bit in bits:
-        near = halve(near, bit)
-    in_grads = join_replicas(sum_lines(add_low(near, *far)))
+    attend(0, range(last, count))
+    near = by_lines(outer_sum(first, qvk_grads[0], 1, qvk_width // 2))
+    if far_done < 2:
+        far = halve_all(far, bits[far_done:])
+    near, far, in_parts, qvk_grads[0] = tie(near, far, in_parts, qvk_grads[0])
+    near = halve_all([near], bits[:1])
+    near, qvk_grads[0], far = tie(near, qvk_grads[0], far)
+    input_grad, input_whole, sums = first_back(last, input_whole)
+    near = halve_all(near, bits[1:])
+    far = [sum_lines(held) for held in far]
+    (
+        near,
+        far,
+        input_grad,
+        input_whole,
+        sums,
+        third_sums,
+        qvk_sums,
+        first_sums,
+        second_sums,
+        upper_sums,
+        out_whole,
+        out_parts,
+        down_grads,
+        up_share,
+    ) = tie(
+        near,
+        far,
+        input_grad,
+        input_whole,
+        sums,
+        third_sums,
+        qvk_sums,
+        first_sums,
+        second_sums,
+        upper_sums,
+        out_whole,
+        out_parts,
+        down_grads,
+        up_share,
+    )
+    third_sums = third_sums + sums
+    in_parts.append(trade(input_grad))
+    out_whole = lay(out_whole, out_parts, 0)
+    for slot in range(last):
+        input_whole = lay(input_whole, in_parts[slot], slot)
+    near_total = add_low(
+        sum_lines(near[0]), *(swap(term, "tensor", rank) for rank, term in zip(ranks[1:], far))
+    )
+    near_found = among_replicas(near_total)
+    up_found = among_replicas(up_share[None])
 
     def all_ranks(parts, size):
         whole = jnp.zeros((tensor_count * size,), full)
@@ -1124,10 +1229,11 @@
     padded = ceil_to(joined.shape[0], 8 * LANES)
     summed = jnp.pad(joined, (0, padded - joined.shape[0])).reshape(-1, LANES)
     summed = sum_over(sum_over(summed, "replica"), "fsdp")
-    summed, in_parts = tie(summed, in_parts)
+    near_found, up_found, summed, in_parts[-1] = tie(near_found, up_found, summed, in_parts[-1])
     summed = sum_over(summed, "tensor").reshape(-1)
-    for slot in range(count):
-        input_whole = lay(input_whole, in_parts[slot], slot)
+    in_grads = place_found(near_found)
+    up_o_grads = place_found(up_found)
+    input_whole = lay(input_whole, in_parts[-1], last)
     ends, start = [], 0
     for size in sizes:
         share = size // tensor_count
@@ -1144,11 +1250,11 @@
         in_grads[:, 2 * width : 3 * width].astype(full),
         in_grads[:, width : 2 * width].astype(full),
         v_sum,
-        o_grads[:, SHIFT : SHIFT + width].astype(full).T,
+        up_o_grads[:, unit_width + SHIFT : unit_width + SHIFT + width].astype(full).T,
         o_sum,
         gain_two,
         shift_two,
-        up_grads[:, :units].astype(full),
+        up_o_grads[:, :units].astype(full),
         up_sum,
         down_grads[:, :units].astype(full).T,
         down_sum,

time: 851 us -> 782 us (0.919)
  waiting for transfers between devices: 129 us -> 71.6 us
  matrix products: 49.1 us -> 31.4 us
  local copies, waits for them, and re-layouts: 49.1 us -> 37.1 us
  Pallas kernels: 530 us -> 541 us
  other arithmetic: 26.1 us -> 35.9 us
    ppermute x52 -> x25, waiting for transfers between devices: 107 us -> 61.4 us  [swap(): lax.ppermute(array, axis, [(rank, rank ^ bits) for rank in range(size)])]
    dot_general x4 -> x2, matrix products: 49.1 us -> 31.4 us  [matmul(): return jnp.dot(first_op, second_op, preferred_element_type=jnp.float32)]
    ppermute x52 -> x25, starting transfers between devices: 31.9 us -> 16.5 us  [swap(): lax.ppermute(array, axis, [(rank, rank ^ bits) for rank in range(size)])]
    ppermute x0 -> x7, starting transfers between devices: none -> 12.4 us  [sum_over(): lax.ppermute(vector, axes, [(rank, rank ^ bits) for rank in range(size)])]
    ppermute x9, waiting for transfers between devices: 22.5 us -> 10.2 us  [turn(): lax.ppermute(array, axis, [(rank, (rank + steps) % size) for rank in rang...]
    pallas_call x25 -> x26, Pallas kernels: 530 us -> 541 us  [call(): pl.pallas_call(kernel, grid_spec=pltpu.PrefetchScalarGridSpec(num_scalar_...]
  transfers between devices with their start and end apart: 67 -> 45, of which waited for: 20 -> 14; matrix products, arithmetic and copies ran while one was open for 12% -> 12% of each run, Pallas kernels for 62% -> 70%
where the time goes in v2:
time: 782 us; the launch traced here: 777 us
  Pallas kernels  541 us (69%)
  waiting for transfers between devices  71.6 us (9%)
  starting transfers between devices  44.9 us (6%)
  local copies, waits for them, and re-layouts  37.1 us (5%)
  other arithmetic  35.9 us (5%)
  matrix products  31.4 us (4%)
  between operations  14.7 us (2%)
    pallas_call x26, Pallas kernels, call(): pl.pallas_call(kernel, grid_spec=pltpu.PrefetchScalarGridSpec(num_scalar_...  541 us
    ppermute x25, waiting for transfers between devices, swap(): lax.ppermute(array, axis, [(rank, rank ^ bits) for rank in range(size)])  61.4 us
    dot_general x2, matrix products, matmul(): return jnp.dot(first_op, second_op, preferred_element_type=jnp.float32)  31.4 us
    ppermute x25, starting transfers between devices, swap(): lax.ppermute(array, axis, [(rank, rank ^ bits) for rank in range(size)])  16.5 us
    ppermute x9, starting transfers between devices, turn(): lax.ppermute(array, axis, [(rank, (rank + steps) % size) for rank in rang...  15.8 us
  transfers between devices with their start and end apart: 45, of which 14 were waited for; matrix products, arithmetic and copies ran while one was open for 12% of the time, Pallas kernels for 70%

profile of v2, /device:TPU:0, one launch (start us, length us, event | category | flops | bytes accessed | tf_op | source)
XLA Modules:
  0.0 777.0 jit_solution(10474240875411805852)
XLA Ops:
  11.5 5.1 collective-permute-start.2
  25.5 11.4 %first_norm.1 = (bf16[2208,1152]{1,0:T(8,128)(2,1)}, bf16[2208,1152]{1,0:T(8,128)(2,1)}, f32[8,1152]{1,0:T(8,128)}) custom-call(s32[6]{0:T(128)} %pad_add_fusion.scalars_ref, bf16[6,729,1152]{2,1,0:T(8,128)(2,1)} %refs_4_.7, bf16[6,729,1152]{2,1,0:T(8,128)(2,1)} %cot_ref.1, f32[1,1152]{1,0:T(1,128)} %reshape.120.gain_ref.refs_6_, f32[1,1152]{1,0:T(1,128)} %reshape.121.shift_ref), custom_call_target="tpu_custom_call" | custom-call | bytes 20164608 | tf_op jit(solution)/shard_map/first_norm/pallas_call | solution.py:416
  46.5 17.3 %collective-permute-done.3.refs_2_ = bf16[3,72,1792]{2,1,0:T(8,128)(2,1)} collective-permute-done((bf16[3,72,1792]{2,1,0:T(8,128)(2,1)S(1)}, bf16[3,72,1792]{2,1,0:T(8,128)(2,1)}, u32[]{:S(2)}, u32[]{:S(2)}) %collective-permute-start.3) | collective-permute-done | bytes 774176 | tf_op jit(solution)/shard_map/ppermute | solution.py:619
  64.5 7.0 collective-permute-done.6.refs_0_
  72.0 5.1 place.5
  77.1 15.6 %multiply_convert_fusion.1.qvk_ref = bf16[2208,1792]{1,0:T(8,128)(2,1)} fusion(bf16[2208,1152]{1,0:T(8,128)(2,1)} %get-tuple-element.167.left_ref, bf16[1152,1792]{1,0:T(8,128)(2,1)} %bitcast.79, f32[1792]{0:T(1024)S(1)} %fusion.7, f32[1792]{0:T(1024)S(1)} %select_maximum_fusion.1), kind=kOutput, calls=%fused_computation.1 | convolution fusion | flops 9128189952 | bytes 17143808 | tf_op jit(solution)/shard_map/dot_general | solution.py:19
  92.8 26.7 %attention.2 = (bf16[2208,768]{1,0:T(8,128)(2,1)}, bf16[24,736,736]{2,1,0:T(8,128)(2,1)}) custom-call(s32[1]{0:T(128)} %constant.171.clone.1.none_ref.scalars_ref, bf16[2208,1792]{1,0:T(8,128)(2,1)} %multiply_convert_fusion.1.qvk_ref), custom_call_target="tpu_custom_call" | custom-call | flops 13312720896 | bytes 7913472 | tf_op jit(solution)/shard_map/attention/pallas_call | solution.py:416
  128.9 15.7 %multiply_convert_fusion.qvk_ref = bf16[2208,1792]{1,0:T(8,128)(2,1)} fusion(bf16[2208,1152]{1,0:T(8,128)(2,1)} %get-tuple-element.167.left_ref, bf16[1152,1792]{1,0:T(8,128)(2,1)} %bitcast.83, f32[1792]{0:T(1024)S(1)} %select_maximum_fusion, f32[1792]{0:T(1024)S(1)} %fusion.7), kind=kOutput, calls=%fused_computation | convolution fusion | flops 9128189952 | bytes 17143808 | tf_op jit(solution)/shard_map/dot_general | solution.py:19
  144.7 26.7 %attention.3 = (bf16[2208,768]{1,0:T(8,128)(2,1)}, bf16[24,736,736]{2,1,0:T(8,128)(2,1)}) custom-call(s32[1]{0:T(128)} %constant.171.clone.1.none_ref.scalars_ref, bf16[2208,1792]{1,0:T(8,128)(2,1)} %multiply_convert_fusion.qvk_ref), custom_call_target="tpu_custom_call" | custom-call | flops 13312720896 | bytes 7913472 | tf_op jit(solution)/shard_map/attention/pallas_call | solution.py:416
  171.4 17.7 %middle_norm.1 = (f32[2208,1152]{1,0:T(8,128)}, bf16[2208,1152]{1,0:T(8,128)(2,1)}) custom-call(s32[6]{0:T(128)} %pad_add_fusion.scalars_ref, bf16[2208,768]{1,0:T(8,128)(2,1)} %get-tuple-element.145.refs_0_.right_ref.mixed_ref, bf16[2208,768]{1,0:T(8,128)(2,1)} %get-tuple-element.144.refs_1_.right_ref.mixed_ref, ...), custom_call_target="tpu_custom_call" | custom-call | flops 7813988352 | bytes 45186048 | tf_op jit(solution)/shard_map/middle_norm/pallas_call | solution.py:416
  189.1 48.5 %hidden.1 = (bf16[2208,4608]{1,0:T(8,128)(2,1)}, bf16[2208,4608]{1,0:T(8,128)(2,1)}) custom-call(s32[6]{0:T(128)} %pad_add_fusion.scalars_ref, bf16[2208,1152]{1,0:T(8,128)(2,1)} %get-tuple-element.147.second_ref.left_ref, bf16[2304,3072]{1,0:T(8,128)(2,1)} %all-gather.3.cloned.1.call-done.refs_2_.refs_3_.weight_ref.refs_7_.refs_8_, f32[1,4608]{1,0:T(1,128)} %bitcast.103), custom_call_target="tpu_custom_call" | custom-call | flops 23441965056 | bytes 19261440 | tf_op jit(solution)/shard_map/hidden/pallas_call | solution.py:416
  237.6 31.3 %outer_sum.6 = bf16[2304,2304]{1,0:T(8,128)(2,1)} custom-call(s32[1]{0:T(128)} %constant.171.clone.1.none_ref.scalars_ref, bf16[2208,1152]{1,0:T(8,128)(2,1)} %get-tuple-element.154.left_ref.grad_ref.refs_5_, bf16[2208,4608]{1,0:T(8,128)(2,1)} %get-tuple-element.150.right_ref.refs_0_.refs_1_), custom_call_target="tpu_custom_call" | custom-call | flops 23441965056 | bytes 25436160 | tf_op jit(solution)/shard_map/outer_sum/pallas_call | solution.py:416
  270.3 36.0 %output.1 = (bf16[3,729,1152]{2,1,0:T(8,128)(2,1)}, bf16[6,729,1152]{2,1,0:T(8,128)(2,1)}) custom-call(s32[6]{0:T(128)} %pad_add_fusion.scalars_ref, bf16[2208,4608]{1,0:T(8,128)(2,1)} %get-tuple-element.150.right_ref.refs_0_.refs_1_, bf16[2208,4608]{1,0:T(8,128)(2,1)} %get-tuple-element.150.right_ref.refs_0_.refs_1_, ...), custom_call_target="tpu_custom_call" | custom-call | flops 23441965056 | bytes 72110592 | tf_op jit(solution)/shard_map/output/pallas_call | solution.py:416
  307.8 37.6 %hidden_back.1 = (bf16[2208,4608]{1,0:T(8,128)(2,1)}, f32[8,4608]{1,0:T(8,128)}) custom-call(s32[6]{0:T(128)} %pad_add_fusion.scalars_ref, bf16[2208,1152]{1,0:T(8,128)(2,1)} %get-tuple-element.154.left_ref.grad_ref.refs_5_, bf16[2304,2304]{1,0:T(8,128)(2,1)} %all-gather.5.cloned.1.call-done.refs_2_.refs_3_.weight_ref, ...), custom_call_target="tpu_custom_call" | custom-call | flops 23441965056 | bytes 36052992 | tf_op jit(solution)/shard_map/hidden_back/pallas_call | solution.py:416
  345.4 31.5 %outer_sum.7.refs_0_ = bf16[2304,3072]{1,0:T(8,128)(2,1)} custom-call(s32[1]{0:T(128)} %constant.171.clone.1.none_ref.scalars_ref, bf16[2208,1152]{1,0:T(8,128)(2,1)} %get-tuple-element.147.second_ref.left_ref, bf16[2208,4608]{1,0:T(8,128)(2,1)} %get-tuple-element.157.right_ref.refs_0_.refs_1_), custom_call_target="tpu_custom_call" | custom-call | flops 23441965056 | bytes 25436160 | tf_op jit(solution)/shard_map/outer_sum/pallas_call | solution.py:416
  376.9 62.6 %middle_back.1 = (f32[2208,1152]{1,0:T(8,128)}, bf16[2208,1152]{1,0:T(8,128)(2,1)}, f32[8,1152]{1,0:T(8,128)}, bf16[2208,768]{1,0:T(8,128)(2,1)}, bf16[2208,768]{1,0:T(8,128)(2,1)}) custom-call(s32[6]{0:T(128)} %pad_add_fusion.scalars_ref, bf16[2208,4608]{1,0:T(8,128)(2,1)} %get-tuple-element.157.right_ref.refs_0_.refs_1_, ...), custom_call_target="tpu_custom_call" | custom-call | flops 31255953408 | bytes 112587264 | tf_op jit(solution)/shard_map/middle_back/pallas_call | solution.py:416
  439.5 9.8 %outer_sum.8.refs_0_ = bf16[2304,3072]{1,0:T(8,128)(2,1)} custom-call(s32[6]{0:T(128)} %pad_add_fusion.scalars_ref, bf16[2208,1152]{1,0:T(8,128)(2,1)} %get-tuple-element.158.left_ref, bf16[2208,768]{1,0:T(8,128)(2,1)} %get-tuple-element.145.refs_0_.right_ref.mixed_ref, bf16[2304,3072]{1,0:T(8,128)(2,1)} %outer_sum.7.refs_0_), custom_call_target="tpu_custom_call", output_to_operand_aliasing={{}: (3, {})} | custom-call | flops 3906994176 | bytes 22634496 | tf_op jit(solution)/shard_map/outer_sum/pallas_call | solution.py:416
  449.4 9.9 %outer_sum.9 = bf16[2304,3072]{1,0:T(8,128)(2,1)} custom-call(s32[6]{0:T(128)} %pad_add_fusion.scalars_ref, bf16[2208,1152]{1,0:T(8,128)(2,1)} %get-tuple-element.158.left_ref, bf16[2208,768]{1,0:T(8,128)(2,1)} %get-tuple-element.144.refs_1_.right_ref.mixed_ref, bf16[2304,3072]{1,0:T(8,128)(2,1)} %outer_sum.8.refs_0_), custom_call_target="tpu_custom_call", output_to_operand_aliasing={{}: (3, {})} | custom-call | flops 3906994176 | bytes 22634496 | tf_op jit(solution)/shard_map/outer_sum/pallas_call | solution.py:416
  461.1 38.3 %attention_back.4 = (bf16[2208,1792]{1,0:T(8,128)(2,1)}, f32[3,8,1792]{2,1,0:T(8,128)}) custom-call(s32[1]{0:T(128)} %constant.171.clone.1.none_ref.scalars_ref, bf16[2208,1792]{1,0:T(8,128)(2,1)} %multiply_convert_fusion.qvk_ref, bf16[2208,768]{1,0:T(8,128)(2,1)} %get-tuple-element.144.refs_1_.right_ref.mixed_ref, ...), custom_call_target="tpu_custom_call" | custom-call | flops 26625441792 | bytes 40697856 | tf_op jit(solution)/shard_map/attention_back/pallas_call | solution.py:416
  500.0 17.1 %outer_sum.10 = bf16[1152,1792]{1,0:T(8,128)(2,1)} custom-call(s32[1]{0:T(128)} %constant.171.clone.1.none_ref.scalars_ref, bf16[2208,1152]{1,0:T(8,128)(2,1)} %get-tuple-element.167.left_ref, bf16[2208,1792]{1,0:T(8,128)(2,1)} %get-tuple-element.168.right_ref.refs_1_), custom_call_target="tpu_custom_call" | custom-call | flops 9116319744 | bytes 13000704 | tf_op jit(solution)/shard_map/outer_sum/pallas_call | solution.py:416
  524.8 16.9 %attention_back.5 = (bf16[2208,1792]{1,0:T(8,128)(2,1)}, f32[1,8,1792]{2,1,0:T(8,128)}) custom-call(s32[1]{0:T(128)} %constant.171.clone.1.none_ref.scalars_ref, bf16[2208,1792]{1,0:T(8,128)(2,1)} %multiply_convert_fusion.1.qvk_ref, bf16[2208,768]{1,0:T(8,128)(2,1)} %get-tuple-element.145.refs_0_.right_ref.mixed_ref, ...), custom_call_target="tpu_custom_call" | custom-call | flops 8875147264 | bytes 40697856 | tf_op jit(solution)/shard_map/attention_back/pallas_call | solution.py:416
  543.9 16.5 %first_back.3 = (bf16[1,729,1152]{2,1,0:T(8,128)(2,1)}, bf16[6,729,1152]{2,1,0:T(8,128)(2,1)}, f32[8,1152]{1,0:T(8,128)}) custom-call(s32[6]{0:T(128)} %pad_add_fusion.scalars_ref, bf16[2208,1792]{1,0:T(8,128)(2,1)} %get-tuple-element.177.refs_0_, bf16[2208,1792]{1,0:T(8,128)(2,1)} %get-tuple-element.168.right_ref.refs_1_, bf16[1152,1792]{1,0:T(8,128)(2,1)} %bitcast.80, ...), custom_call_target="tpu_custom_call" | custom-call | flops 6077546496 | bytes 44341248 | tf_op jit(solution)/shard_map/first_back/pallas_call | solution.py:416
  562.2 17.1 %attention_back.6 = (bf16[2208,1792]{1,0:T(8,128)(2,1)}, f32[1,8,1792]{2,1,0:T(8,128)}) custom-call(s32[1]{0:T(128)} %constant.171.clone.1.none_ref.scalars_ref, bf16[2208,1792]{1,0:T(8,128)(2,1)} %multiply_convert_fusion.1.qvk_ref, bf16[2208,768]{1,0:T(8,128)(2,1)} %get-tuple-element.145.refs_0_.right_ref.mixed_ref, ...), custom_call_target="tpu_custom_call", output_to_operand_aliasing={{0}: (5, {})} | custom-call | flops 8875147264 | bytes 48611328 | tf_op jit(solution)/shard_map/attention_back/pallas_call | solution.py:416
  579.3 16.0 %first_back.4 = (bf16[1,729,1152]{2,1,0:T(8,128)(2,1)}, bf16[6,729,1152]{2,1,0:T(8,128)(2,1)}, f32[8,1152]{1,0:T(8,128)}) custom-call(s32[6]{0:T(128)} %pad_add_fusion.scalars_ref, bf16[2208,1792]{1,0:T(8,128)(2,1)} %get-tuple-element.183.refs_0_, bf16[2208,1792]{1,0:T(8,128)(2,1)} %get-tuple-element.168.right_ref.refs_1_, ...), custom_call_target="tpu_custom_call", output_to_operand_aliasing={{1}: (8, {})} | custom-call | flops 6077546496 | bytes 54418944 | tf_op jit(solution)/shard_map/first_back/pallas_call | solution.py:416
  597.8 16.4 %collective-permute-done.16 = bf16[1,729,1152]{2,1,0:T(8,128)(2,1)S(1)} collective-permute-done((bf16[1,729,1152]{2,1,0:T(8,128)(2,1)}, bf16[1,729,1152]{2,1,0:T(8,128)(2,1)S(1)}, u32[]{:S(2)}, u32[]{:S(2)}) %collective-permute-start.16) | collective-permute-done | bytes 1679648 | tf_op jit(solution)/shard_map/ppermute | solution.py:619
  614.4 17.4 %attention_back.7 = (bf16[2208,1792]{1,0:T(8,128)(2,1)}, f32[1,8,1792]{2,1,0:T(8,128)}) custom-call(s32[1]{0:T(128)} %constant.171.clone.1.none_ref.scalars_ref, bf16[2208,1792]{1,0:T(8,128)(2,1)} %multiply_convert_fusion.1.qvk_ref, bf16[2208,768]{1,0:T(8,128)(2,1)} %get-tuple-element.145.refs_0_.right_ref.mixed_ref, ...), custom_call_target="tpu_custom_call", output_to_operand_aliasing={{0}: (5, {})} | custom-call | flops 8875147264 | bytes 48611328 | tf_op jit(solution)/shard_map/attention_back/pallas_call | solution.py:416
  631.8 16.9 %outer_sum.11 = bf16[1152,1792]{1,0:T(8,128)(2,1)} custom-call(s32[1]{0:T(128)} %constant.171.clone.1.none_ref.scalars_ref, bf16[2208,1152]{1,0:T(8,128)(2,1)} %get-tuple-element.167.left_ref, bf16[2208,1792]{1,0:T(8,128)(2,1)} %get-tuple-element.196.right_ref.refs_0_), custom_call_target="tpu_custom_call" | custom-call | flops 9116319744 | bytes 13000704 | tf_op jit(solution)/shard_map/outer_sum/pallas_call | solution.py:416
  648.7 7.5 collective-permute-done.17
  675.1 15.8 %first_back.5 = (bf16[1,729,1152]{2,1,0:T(8,128)(2,1)}, bf16[6,729,1152]{2,1,0:T(8,128)(2,1)}, f32[8,1152]{1,0:T(8,128)}) custom-call(s32[6]{0:T(128)} %pad_add_fusion.scalars_ref, bf16[2208,1792]{1,0:T(8,128)(2,1)} %get-tuple-element.196.right_ref.refs_0_, bf16[2208,1792]{1,0:T(8,128)(2,1)} %get-tuple-element.168.right_ref.refs_1_, ...), custom_call_target="tpu_custom_call", output_to_operand_aliasing={{1}: (8, {})} | custom-call | flops 6077546496 | bytes 54418944 | tf_op jit(solution)/shard_map/first_back/pallas_call | solution.py:416
  715.0 5.1 constant_dynamic-update-slice_fusion.6
  722.8 7.8 %collective-permute-start.37 = (f32[112,128]{1,0:T(8,128)S(1)}, f32[112,128]{1,0:T(8,128)S(1)}, u32[]{:S(2)}, u32[]{:S(2)}) collective-permute-start(f32[112,128]{1,0:T(8,128)S(1)} %add_add_fusion.1), channel_id=1, source_target_pairs={{0,4},{2,6},{4,0},{6,2},{1,5},{3,7},{5,1},{7,3},{8,12},{10,14},{12... | collective-permute-start | bytes 172040 | tf_op jit(solution)/shard_map/ppermute | solution.py:731
  730.6 5.8 collective-permute-done.24
  (239 shorter events, 132.2 us)
Async XLA Ops:
  7.2 164.2 %all-gather.3.cloned.1.call-start = ((), (), s32[]{:S(2)}) async-start(), calls=%async_computation.2 | async-start | bytes 14598144 | tf_op jit(solution)/shard_map/all_gather | solution.py:690
  11.5 25.7 %collective-permute-start.2 = (bf16[1,72,1792]{2,1,0:T(8,128)(2,1)S(1)}, bf16[1,72,1792]{2,1,0:T(8,128)(2,1)S(1)}, u32[]{:S(2)}, u32[]{:S(2)}) collective-permute-start(bf16[1,72,1792]{2,1,0:T(8,128)(2,1)S(1)} %constant_dynamic-slice_fusion.10), channel_id=1, source_target_pairs={{0,6},{2,0},{4,2},{6,4},{1,7},{3,1},{5,3},{7,5},{8,14},{10,8},{12,... | collective-permute-start | bytes 774152 | tf_op jit(solution)/shard_map/ppermute | solution.py:624
  16.6 22.0 %collective-permute-start.1 = (bf16[1,72,1792]{2,1,0:T(8,128)(2,1)S(1)}, bf16[1,72,1792]{2,1,0:T(8,128)(2,1)S(1)}, u32[]{:S(2)}, u32[]{:S(2)}) collective-permute-start(bf16[1,72,1792]{2,1,0:T(8,128)(2,1)S(1)} %constant_dynamic-slice_fusion.10), channel_id=1, source_target_pairs={{0,4},{2,6},{4,0},{6,2},{1,5},{3,7},{5,1},{7,3},{8,12},{10,14},{12... | collective-permute-start | bytes 774152 | tf_op jit(solution)/shard_map/ppermute | solution.py:624
  16.6 22.0 %collective-permute-start = (bf16[1,72,1792]{2,1,0:T(8,128)(2,1)S(1)}, bf16[1,72,1792]{2,1,0:T(8,128)(2,1)}, u32[]{:S(2)}, u32[]{:S(2)}) collective-permute-start(bf16[1,72,1792]{2,1,0:T(8,128)(2,1)S(1)} %constant_dynamic-slice_fusion.10), channel_id=1, source_target_pairs={{0,2},{2,4},{4,6},{6,0},{1,3},{3,5},{5,7},{7,1},{8,10},{10,12},{12... | collective-permute-start | bytes 774152 | tf_op jit(solution)/shard_map/ppermute | solution.py:624
  39.3 230.9 %all-gather.5.cloned.1.call-start = ((), (), s32[]{:S(2)}) async-start(), calls=%async_computation.3 | async-start | bytes 10948608 | tf_op jit(solution)/shard_map/all_gather | solution.py:690
  41.1 418.7 %reduce-scatter.3.cloned.1.call-start = ((), (), s32[]{:S(2)}) async-start(), calls=%async_computation.4 | async-start | bytes 10948608 | tf_op jit(solution)/shard_map/reduce_scatter | solution.py:959
  42.2 21.5 %collective-permute-start.3 = (bf16[3,72,1792]{2,1,0:T(8,128)(2,1)S(1)}, bf16[3,72,1792]{2,1,0:T(8,128)(2,1)}, u32[]{:S(2)}, u32[]{:S(2)}) collective-permute-start(bf16[3,72,1792]{2,1,0:T(8,128)(2,1)S(1)} %constant_dynamic-update-slice_fusion.refs_1_), channel_id=1, source_target_pairs={{0,16},{8,24},{16,0},{24,8},{1,17},{9,25},{17,1},{25,9},{2,18},{10... | collective-permute-start | bytes 2322440 | tf_op jit(solution)/shard_map/ppermute | solution.py:619
  44.9 26.6 %collective-permute-start.6 = (bf16[4,72,1792]{2,1,0:T(8,128)(2,1)S(1)}, bf16[4,72,1792]{2,1,0:T(8,128)(2,1)S(1)}, u32[]{:S(2)}, u32[]{:S(2)}) collective-permute-start(bf16[4,72,1792]{2,1,0:T(8,128)(2,1)S(1)} %pad_maximum_fusion), channel_id=1, source_target_pairs={{0,1},{1,0},{2,3},{3,2},{4,5},{5,4},{6,7},{7,6},{8,9},{9,8},{10,11... | collective-permute-start | bytes 3096584 | tf_op jit(solution)/shard_map/ppermute | solution.py:619
  46.5 25.6 %collective-permute-start.4 = (bf16[3,72,1792]{2,1,0:T(8,128)(2,1)S(1)}, bf16[3,72,1792]{2,1,0:T(8,128)(2,1)}, u32[]{:S(2)}, u32[]{:S(2)}) collective-permute-start(bf16[3,72,1792]{2,1,0:T(8,128)(2,1)S(1)} %constant_dynamic-update-slice_fusion.refs_1_), channel_id=1, source_target_pairs={{0,8},{8,0},{16,24},{24,16},{1,9},{9,1},{17,25},{25,17},{2,10},{10... | collective-permute-start | bytes 2322440 | tf_op jit(solution)/shard_map/ppermute | solution.py:619
  71.5 48.0 %collective-permute-start.7 = (bf16[4,72,1792]{2,1,0:T(8,128)(2,1)S(1)}, bf16[4,72,1792]{2,1,0:T(8,128)(2,1)S(1)}, u32[]{:S(2)}, u32[]{:S(2)}) collective-permute-start(bf16[4,72,1792]{2,1,0:T(8,128)(2,1)S(1)} %collective-permute-done.6.refs_0_), channel_id=1, source_target_pairs={{0,16},{8,24},{16,0},{24,8},{1,17},{9,25},{17,1},{25,9},{2,18},{10... | collective-permute-start | bytes 3096584 | tf_op jit(solution)/shard_map/ppermute | solution.py:619
  269.0 431.3 %reduce-scatter.5.cloned.1.call-start = ((), (), s32[]{:S(2)}) async-start(), calls=%async_computation.5 | async-start | bytes 14598144 | tf_op jit(solution)/shard_map/reduce_scatter | solution.py:1074
  306.3 152.9 %collective-permute-start.10 = (bf16[3,729,1152]{2,1,0:T(8,128)(2,1)}, bf16[3,729,1152]{2,1,0:T(8,128)(2,1)}, u32[]{:S(2)}, u32[]{:S(2)}) collective-permute-start(bf16[3,729,1152]{2,1,0:T(8,128)(2,1)} %get-tuple-element.161), channel_id=1, source_target_pairs={{0,1},{1,0},{2,3},{3,2},{4,5},{5,4},{6,7},{7,6},{8,9},{9,8},{10,11... | collective-permute-start | bytes 15116552 | tf_op jit(solution)/shard_map/ppermute | solution.py:619
  459.9 39.5 %collective-permute-start.11 = (bf16[1,72,2304]{2,1,0:T(8,128)(2,1)}, bf16[1,72,2304]{2,1,0:T(8,128)(2,1)S(1)}, u32[]{:S(2)}, u32[]{:S(2)}) collective-permute-start(bf16[1,72,2304]{2,1,0:T(8,128)(2,1)} %bitcast.100), channel_id=1, source_target_pairs={{0,16},{8,24},{16,0},{24,8},{1,17},{9,25},{17,1},{25,9},{2,18},{10... | collective-permute-start | bytes 995336 | tf_op jit(solution)/shard_map/ppermute | solution.py:619
  499.4 17.7 %collective-permute-start.12 = (bf16[1,72,2304]{2,1,0:T(8,128)(2,1)S(1)}, bf16[1,72,2304]{2,1,0:T(8,128)(2,1)S(1)}, u32[]{:S(2)}, u32[]{:S(2)}) collective-permute-start(bf16[1,72,2304]{2,1,0:T(8,128)(2,1)S(1)} %bitcast.102), channel_id=1, source_target_pairs={{0,8},{8,0},{16,24},{24,16},{1,9},{9,1},{17,25},{25,17},{2,10},{10... | collective-permute-start | bytes 995336 | tf_op jit(solution)/shard_map/ppermute | solution.py:619
  499.5 17.7 %collective-permute-start.13 = (bf16[1,72,2304]{2,1,0:T(8,128)(2,1)S(1)}, bf16[1,72,2304]{2,1,0:T(8,128)(2,1)S(1)}, u32[]{:S(2)}, u32[]{:S(2)}) collective-permute-start(bf16[1,72,2304]{2,1,0:T(8,128)(2,1)S(1)} %collective-permute-done.11.refs_1_), channel_id=1, source_target_pairs={{0,8},{8,0},{16,24},{24,16},{1,9},{9,1},{17,25},{25,17},{2,10},{10... | collective-permute-start | bytes 995336 | tf_op jit(solution)/shard_map/ppermute | solution.py:619
  524.7 17.0 %collective-permute-start.14 = (bf16[4,2,72,1792]{3,2,0,1:T(8,128)(2,1)}, bf16[4,2,72,1792]{3,2,0,1:T(8,128)(2,1)S(1)}, u32[]{:S(2)}, u32[]{:S(2)}) collective-permute-start(bf16[4,2,72,1792]{3,2,0,1:T(8,128)(2,1)} %copy_bitcast_fusion.1), channel_id=1, source_target_pairs={{0,8},{8,0},{16,24},{24,16},{1,9},{9,1},{17,25},{25,17},{2,10},{10... | collective-permute-start | bytes 6193160 | tf_op jit(solution)/shard_map/ppermute | solution.py:619
  561.4 33.9 %collective-permute-start.15 = (bf16[4,72,1792]{2,1,0:T(8,128)(2,1)}, bf16[4,72,1792]{2,1,0:T(8,128)(2,1)}, u32[]{:S(2)}, u32[]{:S(2)}) collective-permute-start(bf16[4,72,1792]{2,1,0:T(8,128)(2,1)} %dynamic-slice_bitcast_fusion.1), channel_id=1, source_target_pairs={{0,16},{8,24},{16,0},{24,8},{1,17},{9,25},{17,1},{25,9},{2,18},{10... | collective-permute-start | bytes 3096584 | tf_op jit(solution)/shard_map/ppermute | solution.py:619
  561.9 52.2 %collective-permute-start.16 = (bf16[1,729,1152]{2,1,0:T(8,128)(2,1)}, bf16[1,729,1152]{2,1,0:T(8,128)(2,1)S(1)}, u32[]{:S(2)}, u32[]{:S(2)}) collective-permute-start(bf16[1,729,1152]{2,1,0:T(8,128)(2,1)} %get-tuple-element.181), channel_id=1, source_target_pairs={{0,1},{1,0},{2,3},{3,2},{4,5},{5,4},{6,7},{7,6},{8,9},{9,8},{10,11... | collective-permute-start | bytes 5038856 | tf_op jit(solution)/shard_map/ppermute | solution.py:619
  614.1 42.1 %collective-permute-start.17 = (bf16[1,729,1152]{2,1,0:T(8,128)(2,1)}, bf16[1,729,1152]{2,1,0:T(8,128)(2,1)S(1)}, u32[]{:S(2)}, u32[]{:S(2)}) collective-permute-start(bf16[1,729,1152]{2,1,0:T(8,128)(2,1)} %get-tuple-element.190), channel_id=1, source_target_pairs={{0,1},{1,0},{2,3},{3,2},{4,5},{5,4},{6,7},{7,6},{8,9},{9,8},{10,11... | collective-permute-start | bytes 5038856 | tf_op jit(solution)/shard_map/ppermute | solution.py:619
  666.9 24.1 %collective-permute-start.20 = (bf16[1,72,1792]{2,1,0:T(8,128)(2,1)}, bf16[1,72,1792]{2,1,0:T(8,128)(2,1)}, u32[]{:S(2)}, u32[]{:S(2)}) collective-permute-start(bf16[1,72,1792]{2,1,0:T(8,128)(2,1)} %get-tuple-element.252), channel_id=1, source_target_pairs={{0,2},{2,4},{4,6},{6,0},{1,3},{3,5},{5,7},{7,1},{8,10},{10,12},{12... | collective-permute-start | bytes 774152 | tf_op jit(solution)/shard_map/ppermute | solution.py:624
  668.1 22.8 %collective-permute-start.22 = (bf16[1,72,1792]{2,1,0:T(8,128)(2,1)S(1)}, bf16[1,72,1792]{2,1,0:T(8,128)(2,1)}, u32[]{:S(2)}, u32[]{:S(2)}) collective-permute-start(bf16[1,72,1792]{2,1,0:T(8,128)(2,1)S(1)} %get-tuple-element.253), channel_id=1, source_target_pairs={{0,6},{2,0},{4,2},{6,4},{1,7},{3,1},{5,3},{7,5},{8,14},{10,8},{12,... | collective-permute-start | bytes 774152 | tf_op jit(solution)/shard_map/ppermute | solution.py:624
  670.7 23.1 %collective-permute-start.21 = (bf16[1,72,1792]{2,1,0:T(8,128)(2,1)S(1)}, bf16[1,72,1792]{2,1,0:T(8,128)(2,1)}, u32[]{:S(2)}, u32[]{:S(2)}) collective-permute-start(bf16[1,72,1792]{2,1,0:T(8,128)(2,1)S(1)} %get-tuple-element.254), channel_id=1, source_target_pairs={{0,4},{2,6},{4,0},{6,2},{1,5},{3,7},{5,1},{7,3},{8,12},{10,14},{12... | collective-permute-start | bytes 774152 | tf_op jit(solution)/shard_map/ppermute | solution.py:624
  673.5 24.3 %collective-permute-start.19 = (bf16[4,72,1792]{2,1,0:T(8,128)(2,1)}, bf16[4,72,1792]{2,1,0:T(8,128)(2,1)}, u32[]{:S(2)}, u32[]{:S(2)}) collective-permute-start(bf16[4,72,1792]{2,1,0:T(8,128)(2,1)} %dynamic-slice_bitcast_fusion), channel_id=1, source_target_pairs={{0,16},{8,24},{16,0},{24,8},{1,17},{9,25},{17,1},{25,9},{2,18},{10... | collective-permute-start | bytes 3096584 | tf_op jit(solution)/shard_map/ppermute | solution.py:619
  705.9 14.3 %collective-permute-start.26 = (bf16[1,72,1792]{2,1,0:T(8,128)(2,1)}, bf16[1,72,1792]{2,1,0:T(8,128)(2,1)S(1)}, u32[]{:S(2)}, u32[]{:S(2)}) collective-permute-start(bf16[1,72,1792]{2,1,0:T(8,128)(2,1)} %add_convert_fusion.2), channel_id=1, source_target_pairs={{0,1},{1,0},{2,3},{3,2},{4,5},{5,4},{6,7},{7,6},{8,9},{9,8},{10,11... | collective-permute-start | bytes 774152 | tf_op jit(solution)/shard_map/ppermute | solution.py:619
  707.6 14.3 %collective-permute-start.23 = (bf16[1,72,1792]{2,1,0:T(8,128)(2,1)S(1)}, bf16[1,72,1792]{2,1,0:T(8,128)(2,1)S(1)}, u32[]{:S(2)}, u32[]{:S(2)}) collective-permute-start(bf16[1,72,1792]{2,1,0:T(8,128)(2,1)S(1)} %get-tuple-element.249), channel_id=1, source_target_pairs={{0,2},{2,4},{4,6},{6,0},{1,3},{3,5},{5,7},{7,1},{8,10},{10,12},{12... | collective-permute-start | bytes 774152 | tf_op jit(solution)/shard_map/ppermute | solution.py:624
  709.5 13.3 %collective-permute-start.25 = (bf16[1,72,1792]{2,1,0:T(8,128)(2,1)S(1)}, bf16[1,72,1792]{2,1,0:T(8,128)(2,1)S(1)}, u32[]{:S(2)}, u32[]{:S(2)}) collective-permute-start(bf16[1,72,1792]{2,1,0:T(8,128)(2,1)S(1)} %get-tuple-element.250), channel_id=1, source_target_pairs={{0,6},{2,0},{4,2},{6,4},{1,7},{3,1},{5,3},{7,5},{8,14},{10,8},{12,... | collective-permute-start | bytes 774152 | tf_op jit(solution)/shard_map/ppermute | solution.py:624
  713.3 23.1 %collective-permute-start.24 = (bf16[1,72,1792]{2,1,0:T(8,128)(2,1)S(1)}, bf16[1,72,1792]{2,1,0:T(8,128)(2,1)S(1)}, u32[]{:S(2)}, u32[]{:S(2)}) collective-permute-start(bf16[1,72,1792]{2,1,0:T(8,128)(2,1)S(1)} %get-tuple-element.251), channel_id=1, source_target_pairs={{0,4},{2,6},{4,0},{6,2},{1,5},{3,7},{5,1},{7,3},{8,12},{10,14},{12... | collective-permute-start | bytes 774152 | tf_op jit(solution)/shard_map/ppermute | solution.py:624
  713.3 38.4 %collective-permute-start.39 = (bf16[1,729,1152]{2,1,0:T(8,128)(2,1)}, bf16[1,729,1152]{2,1,0:T(8,128)(2,1)S(1)}, u32[]{:S(2)}, u32[]{:S(2)}) collective-permute-start(bf16[1,729,1152]{2,1,0:T(8,128)(2,1)} %get-tuple-element.229), channel_id=1, source_target_pairs={{0,1},{1,0},{2,3},{3,2},{4,5},{5,4},{6,7},{7,6},{8,9},{9,8},{10,11... | collective-permute-start | bytes 5038856 | tf_op jit(solution)/shard_map/ppermute | solution.py:619
  720.2 20.9 %collective-permute-start.31 = (bf16[1,72,3072]{2,1,0:T(8,128)(2,1)S(1)}, bf16[1,72,3072]{2,1,0:T(8,128)(2,1)S(1)}, u32[]{:S(2)}, u32[]{:S(2)}) collective-permute-start(bf16[1,72,3072]{2,1,0:T(8,128)(2,1)S(1)} %bitcast.98), channel_id=1, source_target_pairs={{0,16},{8,24},{16,0},{24,8},{1,17},{9,25},{17,1},{25,9},{2,18},{10... | collective-permute-start | bytes 1327112 | tf_op jit(solution)/shard_map/ppermute | solution.py:619
  721.9 15.7 %collective-permute-start.38 = (f32[112,128]{1,0:T(8,128)S(1)}, f32[112,128]{1,0:T(8,128)S(1)}, u32[]{:S(2)}, u32[]{:S(2)}) collective-permute-start(f32[112,128]{1,0:T(8,128)S(1)} %add_add_fusion.1), channel_id=1, source_target_pairs={{0,6},{2,4},{4,2},{6,0},{1,7},{3,5},{5,3},{7,1},{8,14},{10,12},{12... | collective-permute-start | bytes 172040 | tf_op jit(solution)/shard_map/ppermute | solution.py:731
  722.8 17.8 %collective-permute-start.37 = (f32[112,128]{1,0:T(8,128)S(1)}, f32[112,128]{1,0:T(8,128)S(1)}, u32[]{:S(2)}, u32[]{:S(2)}) collective-permute-start(f32[112,128]{1,0:T(8,128)S(1)} %add_add_fusion.1), channel_id=1, source_target_pairs={{0,4},{2,6},{4,0},{6,2},{1,5},{3,7},{5,1},{7,3},{8,12},{10,14},{12... | collective-permute-start | bytes 172040 | tf_op jit(solution)/shard_map/ppermute | solution.py:731
  751.7 17.1 %collective-permute-start.40 = (f32[112,128]{1,0:T(8,128)S(1)}, f32[112,128]{1,0:T(8,128)S(1)}, u32[]{:S(2)}, u32[]{:S(2)}) collective-permute-start(f32[112,128]{1,0:T(8,128)S(1)} %add_add_fusion), channel_id=1, source_target_pairs={{0,1},{1,0},{2,3},{3,2},{4,5},{5,4},{6,7},{7,6},{8,9},{9,8},{10,11... | collective-permute-start | bytes 172040 | tf_op jit(solution)/shard_map/ppermute | solution.py:731
  (48 other events, 626.6 us)
Sparse Core Ops, SparseCore 0:
  39.5 119.2 all-gather.2
  162.2 84.9 all-gather.4
  269.1 169.9 reduce-scatter.2
  459.4 180.6 reduce-scatter.4

commit v3 on v2

--- a/solution.py
+++ b/solution.py
@@ -989,6 +989,16 @@
     def trade(part):
         return [swap(part, "tensor", rank) for rank in ranks[1:]]
 
+    def trade_halves(part):
+        return [trade(piece) for piece in part]
+
+    def lay_halves(whole, parts, first):
+        for rank, *pieces in zip(ranks[1:], *parts):
+            for at, piece in enumerate(pieces):
+                start = ((tensor_rank ^ rank) * count + first, at * half, 0)
+                whole = lax.dynamic_update_slice(whole, piece, start)
+        return whole
+
     def lay(whole, parts, first):
         for rank, part in zip(ranks[1:], parts):
             whole = lax.dynamic_update_slice_in_dim(whole, part, (tensor_rank ^ rank) * count + first, 0)
@@ -1081,12 +1091,20 @@
 
     def first_back_kernel(scalars_ref, *refs):
         images_ref, grad_ref, gain_ref = refs[2 * tensor_count : 2 * tensor_count + 3]
-        out_ref, whole_ref, sums_ref = refs[-3:]
+        upper_ref, lower_ref, whole_ref, sums_ref = refs[-4:]
         total = product(refs[:tensor_count], refs[tensor_count : 2 * tensor_count])
         normed, scale_inv = norm_parts(real_rows(images_ref[0]))
         grad = grad_ref[...] + norm_backward(total, normed, scale_inv, gain_ref[...])
-        out_ref[0] = grad.astype(low)
-        whole_ref[0] = out_ref[0]
+        whole_ref[0] = grad.astype(low)
+
+        @pl.when(pl.program_id(0) == 0)
+        def _():
+            upper_ref[...] = whole_ref[...]
+
+        @pl.when(pl.program_id(0) == 1)
+        def _():
+            lower_ref[...] = whole_ref[:, : length - half]
+
         add_sums(sums_ref, total * normed, total)
 
     qvk_grads, qvk_sums = [None] * tensor_count, [0.0] * tensor_count
@@ -1100,7 +1118,7 @@
 
     def first_back(slot, whole):
         ahead = [] if whole is None else [(whole, pl.BlockSpec(memory_space=pl.ANY))]
-        return call(
+        upper, lower, whole, sums = call(
             first_back_kernel,
             "first_back",
             (2,),
@@ -1110,13 +1128,15 @@
             + [(images, slots_spec(slot)), (middle_grad, rows_spec(wide, slot)), (row(ln1_gain), vector_spec())]
             + ahead,
             [
-                ((1, length, wide), low, pl.BlockSpec((1, half, wide), lambda i, s: (0, i, 0))),
+                ((1, half, wide), low, pl.BlockSpec((1, half, wide), lambda i, s: (0, 0, 0))),
+                ((1, length - half, wide), low, pl.BlockSpec((1, length - half, wide), lambda i, s: (0, 0, 0))),
                 ((slots, length, wide), low, slots_spec(slot)),
                 ((8, wide), full, sums_spec()),
             ],
-            aliases={2 * tensor_count + 4: 1} if ahead else None,
+            aliases={2 * tensor_count + 4: 2} if ahead else None,
             flops=2 * rows * wide * qvk_width * tensor_count,
         )
+        return (upper, lower), whole, sums
 
     last = count - 1
 
@@ -1142,7 +1162,7 @@
     far_done = 0
     for slot in range(last):
         if slot > 0:
-            in_parts.append(trade(input_grad))
+            in_parts.append(trade_halves(input_grad))
         attend(0, range(slot, slot + 1))
         if slot == 0:
             far = halve_all(far, bits[:1])
@@ -1152,16 +1172,20 @@
         far_done += 1
         input_grad, input_whole, sums = first_back(slot, input_whole)
         third_sums = third_sums + sums
-        far, in_parts, input_grad, mixed_grads[0] = tie(far, in_parts, input_grad, mixed_grads[0])
+        far, input_grad, mixed_grads[0] = tie(far, input_grad, mixed_grads[0])
+        if slot > 0:
+            in_parts[-1][0], input_grad, mixed_grads[0] = tie(in_parts[-1][0], input_grad, mixed_grads[0])
     if last > 0:
-        in_parts.append(trade(input_grad))
+        in_parts.append(trade_halves(input_grad))
     attend(0, range(last, count))
     near = by_lines(outer_sum(first, qvk_grads[0], 1, qvk_width // 2))
     if far_done < 2:
         far = halve_all(far, bits[far_done:])
-    near, far, in_parts, qvk_grads[0] = tie(near, far, in_parts, qvk_grads[0])
+    near, far, in_parts[:-1], qvk_grads[0] = tie(near, far, in_parts[:-1], qvk_grads[0])
+    if last > 0:
+        in_parts[-1][0], near, qvk_grads[0] = tie(in_parts[-1][0], near, qvk_grads[0])
     near = halve_all([near], bits[:1])
-    near, qvk_grads[0], far = tie(near, qvk_grads[0], far)
+    near, qvk_grads[0], far, up_share = tie(near, qvk_grads[0], far, up_share)
     input_grad, input_whole, sums = first_back(last, input_whole)
     near = halve_all(near, bits[1:])
     far = [sum_lines(held) for held in far]
@@ -1180,6 +1204,7 @@
         out_parts,
         down_grads,
         up_share,
+        in_parts,
     ) = tie(
         near,
         far,
@@ -1195,17 +1220,48 @@
         out_parts,
         down_grads,
         up_share,
+        in_parts,
     )
     third_sums = third_sums + sums
-    in_parts.append(trade(input_grad))
+    in_parts.append(trade_halves(input_grad))
+    lower = in_parts[-1][1]
+    up_found = join_on({0: up_share[None]}, far_bits)
+    near_total = add_low(
+        sum_lines(near[0]), *(swap(term, "tensor", rank) for rank, term in zip(ranks[1:], far))
+    )
+    (
+        near_total,
+        in_parts,
+        up_found,
+        out_parts,
+        out_whole,
+        input_whole,
+        third_sums,
+        qvk_sums,
+        first_sums,
+        second_sums,
+        upper_sums,
+        down_grads,
+    ) = tie(
+        near_total,
+        [*in_parts[:-1], in_parts[-1][:1]],
+        up_found,
+        out_parts,
+        out_whole,
+        input_whole,
+        third_sums,
+        qvk_sums,
+        first_sums,
+        second_sums,
+        upper_sums,
+        down_grads,
+    )
+    in_parts[-1].append(lower)
     out_whole = lay(out_whole, out_parts, 0)
     for slot in range(last):
-        input_whole = lay(input_whole, in_parts[slot], slot)
-    near_total = add_low(
-        sum_lines(near[0]), *(swap(term, "tensor", rank) for rank, term in zip(ranks[1:], far))
-    )
+        input_whole = lay_halves(input_whole, in_parts[slot], slot)
     near_found = among_replicas(near_total)
-    up_found = among_replicas(up_share[None])
+    up_o_grads = place_found(join_on(up_found, far_bit))
 
     def all_ranks(parts, size):
         whole = jnp.zeros((tensor_count * size,), full)
@@ -1228,12 +1284,13 @@
     joined = jnp.concatenate(vectors)
     padded = ceil_to(joined.shape[0], 8 * LANES)
     summed = jnp.pad(joined, (0, padded - joined.shape[0])).reshape(-1, LANES)
-    summed = sum_over(sum_over(summed, "replica"), "fsdp")
-    near_found, up_found, summed, in_parts[-1] = tie(near_found, up_found, summed, in_parts[-1])
+    summed = sum_over(summed, "replica")
+    near_found, summed = tie(near_found, summed)
+    summed = sum_over(summed, "fsdp")
+    summed, in_parts[-1][1] = tie(summed, in_parts[-1][1])
     summed = sum_over(summed, "tensor").reshape(-1)
     in_grads = place_found(near_found)
-    up_o_grads = place_found(up_found)
-    input_whole = lay(input_whole, in_parts[-1], last)
+    input_whole = lay_halves(input_whole, in_parts[-1], last)
     ends, start = [], 0
     for size in sizes:
         share = size // tensor_count

time: 782 us -> 766 us (0.980)
  waiting for transfers between devices: 71.6 us -> 54.4 us
    ppermute x25 -> x28, waiting for transfers between devices: 61.4 us -> 33.2 us  [swap(): lax.ppermute(array, axis, [(rank, rank ^ bits) for rank in range(size)])]
    dynamic_update_slice x0 -> x6, local copies, waits for them, and re-layouts: none -> 9.25 us  [lay_halves(): whole = lax.dynamic_update_slice(whole, piece, start)]
    ppermute x9, waiting for transfers between devices: 10.2 us -> 19.3 us  [turn(): lax.ppermute(array, axis, [(rank, (rank + steps) % size) for rank in rang...]
    ppermute x25 -> x28, starting transfers between devices: 16.5 us -> 16.6 us  [swap(): lax.ppermute(array, axis, [(rank, rank ^ bits) for rank in range(size)])]
  transfers between devices with their start and end apart: 45 -> 48, of which waited for: 14 -> 13; matrix products, arithmetic and copies ran while one was open for 12% -> 12% of each run, Pallas kernels for 70% -> 71%
where the time goes in v3:
time: 766 us; the launch traced here: 761 us
  Pallas kernels  543 us (71%)
  waiting for transfers between devices  54.4 us (7%)
  local copies, waits for them, and re-layouts  42.5 us (6%)
  starting transfers between devices  41.3 us (5%)
  other arithmetic  34.2 us (4%)
  matrix products  31.4 us (4%)
  between operations  14.7 us (2%)
    pallas_call x26, Pallas kernels, call(): pl.pallas_call(kernel, grid_spec=pltpu.PrefetchScalarGridSpec(num_scalar_...  543 us
    ppermute x28, waiting for transfers between devices, swap(): lax.ppermute(array, axis, [(rank, rank ^ bits) for rank in range(size)])  33.2 us
    dot_general x2, matrix products, matmul(): return jnp.dot(first_op, second_op, preferred_element_type=jnp.float32)  31.4 us
    ppermute x9, waiting for transfers between devices, turn(): lax.ppermute(array, axis, [(rank, (rank + steps) % size) for rank in rang...  19.3 us
    ppermute x28, starting transfers between devices, swap(): lax.ppermute(array, axis, [(rank, rank ^ bits) for rank in range(size)])  16.6 us
    ppermute x9, starting transfers between devices, turn(): lax.ppermute(array, axis, [(rank, (rank + steps) % size) for rank in rang...  16.3 us
  transfers between devices with their start and end apart: 48, of which 13 were waited for; matrix products, arithmetic and copies ran while one was open for 12% of the time, Pallas kernels for 71%

profile of v3, /device:TPU:0, one launch (start us, length us, event | category | flops | bytes accessed | tf_op | source)
XLA Modules:
  0.0 761.0 jit_solution(7790020975292178165)
XLA Ops:
  11.5 5.1 collective-permute-start.2
  25.5 11.4 %first_norm.1 = (bf16[2208,1152]{1,0:T(8,128)(2,1)}, bf16[2208,1152]{1,0:T(8,128)(2,1)}, f32[8,1152]{1,0:T(8,128)}) custom-call(s32[6]{0:T(128)} %pad_add_fusion.scalars_ref, bf16[6,729,1152]{2,1,0:T(8,128)(2,1)} %refs_4_.7, bf16[6,729,1152]{2,1,0:T(8,128)(2,1)} %cot_ref.1, f32[1,1152]{1,0:T(1,128)} %reshape.120.gain_ref.refs_6_, f32[1,1152]{1,0:T(1,128)} %reshape.121.shift_ref), custom_call_target="tpu_custom_call" | custom-call | bytes 20164608 | tf_op jit(solution)/shard_map/first_norm/pallas_call | solution.py:416
  46.5 17.3 %collective-permute-done.3.refs_2_ = bf16[3,72,1792]{2,1,0:T(8,128)(2,1)} collective-permute-done((bf16[3,72,1792]{2,1,0:T(8,128)(2,1)S(1)}, bf16[3,72,1792]{2,1,0:T(8,128)(2,1)}, u32[]{:S(2)}, u32[]{:S(2)}) %collective-permute-start.3) | collective-permute-done | bytes 774176 | tf_op jit(solution)/shard_map/ppermute | solution.py:619
  64.5 7.0 collective-permute-done.6.refs_0_
  72.0 5.1 place.5
  77.1 15.7 %multiply_convert_fusion.1.qvk_ref = bf16[2208,1792]{1,0:T(8,128)(2,1)} fusion(bf16[2208,1152]{1,0:T(8,128)(2,1)} %get-tuple-element.199.left_ref, bf16[1152,1792]{1,0:T(8,128)(2,1)} %bitcast.79, f32[1792]{0:T(1024)S(1)} %fusion.7, f32[1792]{0:T(1024)S(1)} %select_maximum_fusion.1), kind=kOutput, calls=%fused_computation.1 | convolution fusion | flops 9128189952 | bytes 17143808 | tf_op jit(solution)/shard_map/dot_general | solution.py:19
  92.8 26.7 %attention.2 = (bf16[2208,768]{1,0:T(8,128)(2,1)}, bf16[24,736,736]{2,1,0:T(8,128)(2,1)}) custom-call(s32[1]{0:T(128)} %constant.172.clone.1.none_ref.scalars_ref, bf16[2208,1792]{1,0:T(8,128)(2,1)} %multiply_convert_fusion.1.qvk_ref), custom_call_target="tpu_custom_call" | custom-call | flops 13312720896 | bytes 7913472 | tf_op jit(solution)/shard_map/attention/pallas_call | solution.py:416
  123.9 5.1 place.6
  129.0 15.7 %multiply_convert_fusion.qvk_ref = bf16[2208,1792]{1,0:T(8,128)(2,1)} fusion(bf16[2208,1152]{1,0:T(8,128)(2,1)} %get-tuple-element.199.left_ref, bf16[1152,1792]{1,0:T(8,128)(2,1)} %bitcast.83, f32[1792]{0:T(1024)S(1)} %select_maximum_fusion, f32[1792]{0:T(1024)S(1)} %fusion.7), kind=kOutput, calls=%fused_computation | convolution fusion | flops 9128189952 | bytes 17143808 | tf_op jit(solution)/shard_map/dot_general | solution.py:19
  144.7 26.7 %attention.3 = (bf16[2208,768]{1,0:T(8,128)(2,1)}, bf16[24,736,736]{2,1,0:T(8,128)(2,1)}) custom-call(s32[1]{0:T(128)} %constant.172.clone.1.none_ref.scalars_ref, bf16[2208,1792]{1,0:T(8,128)(2,1)} %multiply_convert_fusion.qvk_ref), custom_call_target="tpu_custom_call" | custom-call | flops 13312720896 | bytes 7913472 | tf_op jit(solution)/shard_map/attention/pallas_call | solution.py:416
  171.4 17.7 %middle_norm.1 = (f32[2208,1152]{1,0:T(8,128)}, bf16[2208,1152]{1,0:T(8,128)(2,1)}) custom-call(s32[6]{0:T(128)} %pad_add_fusion.scalars_ref, bf16[2208,768]{1,0:T(8,128)(2,1)} %get-tuple-element.177.refs_0_.right_ref.mixed_ref, bf16[2208,768]{1,0:T(8,128)(2,1)} %get-tuple-element.176.refs_1_.right_ref.mixed_ref, ...), custom_call_target="tpu_custom_call" | custom-call | flops 7813988352 | bytes 45186048 | tf_op jit(solution)/shard_map/middle_norm/pallas_call | solution.py:416
  189.1 48.6 %hidden.1 = (bf16[2208,4608]{1,0:T(8,128)(2,1)}, bf16[2208,4608]{1,0:T(8,128)(2,1)}) custom-call(s32[6]{0:T(128)} %pad_add_fusion.scalars_ref, bf16[2208,1152]{1,0:T(8,128)(2,1)} %get-tuple-element.179.second_ref.left_ref, bf16[2304,3072]{1,0:T(8,128)(2,1)} %all-gather.3.cloned.1.call-done.refs_2_.refs_3_.weight_ref.refs_7_.refs_8_, f32[1,4608]{1,0:T(1,128)} %bitcast.103), custom_call_target="tpu_custom_call" | custom-call | flops 23441965056 | bytes 19261440 | tf_op jit(solution)/shard_map/hidden/pallas_call | solution.py:416
  237.8 31.3 %outer_sum.6 = bf16[2304,2304]{1,0:T(8,128)(2,1)} custom-call(s32[1]{0:T(128)} %constant.172.clone.1.none_ref.scalars_ref, bf16[2208,1152]{1,0:T(8,128)(2,1)} %get-tuple-element.186.left_ref.grad_ref.refs_5_, bf16[2208,4608]{1,0:T(8,128)(2,1)} %get-tuple-element.182.right_ref.refs_0_.refs_1_), custom_call_target="tpu_custom_call" | custom-call | flops 23441965056 | bytes 25436160 | tf_op jit(solution)/shard_map/outer_sum/pallas_call | solution.py:416
  270.4 36.0 %output.1 = (bf16[3,729,1152]{2,1,0:T(8,128)(2,1)}, bf16[6,729,1152]{2,1,0:T(8,128)(2,1)}) custom-call(s32[6]{0:T(128)} %pad_add_fusion.scalars_ref, bf16[2208,4608]{1,0:T(8,128)(2,1)} %get-tuple-element.182.right_ref.refs_0_.refs_1_, bf16[2208,4608]{1,0:T(8,128)(2,1)} %get-tuple-element.182.right_ref.refs_0_.refs_1_, ...), custom_call_target="tpu_custom_call" | custom-call | flops 23441965056 | bytes 72110592 | tf_op jit(solution)/shard_map/output/pallas_call | solution.py:416
  307.9 37.6 %hidden_back.1 = (bf16[2208,4608]{1,0:T(8,128)(2,1)}, f32[8,4608]{1,0:T(8,128)}) custom-call(s32[6]{0:T(128)} %pad_add_fusion.scalars_ref, bf16[2208,1152]{1,0:T(8,128)(2,1)} %get-tuple-element.186.left_ref.grad_ref.refs_5_, bf16[2304,2304]{1,0:T(8,128)(2,1)} %all-gather.5.cloned.1.call-done.refs_2_.refs_3_.weight_ref, ...), custom_call_target="tpu_custom_call" | custom-call | flops 23441965056 | bytes 36052992 | tf_op jit(solution)/shard_map/hidden_back/pallas_call | solution.py:416
  345.5 31.6 %outer_sum.7.refs_0_ = bf16[2304,3072]{1,0:T(8,128)(2,1)} custom-call(s32[1]{0:T(128)} %constant.172.clone.1.none_ref.scalars_ref, bf16[2208,1152]{1,0:T(8,128)(2,1)} %get-tuple-element.179.second_ref.left_ref, bf16[2208,4608]{1,0:T(8,128)(2,1)} %get-tuple-element.189.right_ref.refs_0_.refs_1_), custom_call_target="tpu_custom_call" | custom-call | flops 23441965056 | bytes 25436160 | tf_op jit(solution)/shard_map/outer_sum/pallas_call | solution.py:416
  377.1 62.6 %middle_back.1 = (f32[2208,1152]{1,0:T(8,128)}, bf16[2208,1152]{1,0:T(8,128)(2,1)}, f32[8,1152]{1,0:T(8,128)}, bf16[2208,768]{1,0:T(8,128)(2,1)}, bf16[2208,768]{1,0:T(8,128)(2,1)}) custom-call(s32[6]{0:T(128)} %pad_add_fusion.scalars_ref, bf16[2208,4608]{1,0:T(8,128)(2,1)} %get-tuple-element.189.right_ref.refs_0_.refs_1_, ...), custom_call_target="tpu_custom_call" | custom-call | flops 31255953408 | bytes 112587264 | tf_op jit(solution)/shard_map/middle_back/pallas_call | solution.py:416
  439.8 9.8 %outer_sum.8.refs_0_ = bf16[2304,3072]{1,0:T(8,128)(2,1)} custom-call(s32[6]{0:T(128)} %pad_add_fusion.scalars_ref, bf16[2208,1152]{1,0:T(8,128)(2,1)} %get-tuple-element.190.left_ref, bf16[2208,768]{1,0:T(8,128)(2,1)} %get-tuple-element.177.refs_0_.right_ref.mixed_ref, bf16[2304,3072]{1,0:T(8,128)(2,1)} %outer_sum.7.refs_0_), custom_call_target="tpu_custom_call", output_to_operand_aliasing={{}: (3, {})} | custom-call | flops 3906994176 | bytes 22634496 | tf_op jit(solution)/shard_map/outer_sum/pallas_call | solution.py:416
  449.6 9.8 %outer_sum.9 = bf16[2304,3072]{1,0:T(8,128)(2,1)} custom-call(s32[6]{0:T(128)} %pad_add_fusion.scalars_ref, bf16[2208,1152]{1,0:T(8,128)(2,1)} %get-tuple-element.190.left_ref, bf16[2208,768]{1,0:T(8,128)(2,1)} %get-tuple-element.176.refs_1_.right_ref.mixed_ref, bf16[2304,3072]{1,0:T(8,128)(2,1)} %outer_sum.8.refs_0_), custom_call_target="tpu_custom_call", output_to_operand_aliasing={{}: (3, {})} | custom-call | flops 3906994176 | bytes 22634496 | tf_op jit(solution)/shard_map/outer_sum/pallas_call | solution.py:416
  461.1 38.3 %attention_back.4 = (bf16[2208,1792]{1,0:T(8,128)(2,1)}, f32[3,8,1792]{2,1,0:T(8,128)}) custom-call(s32[1]{0:T(128)} %constant.172.clone.1.none_ref.scalars_ref, bf16[2208,1792]{1,0:T(8,128)(2,1)} %multiply_convert_fusion.qvk_ref, bf16[2208,768]{1,0:T(8,128)(2,1)} %get-tuple-element.176.refs_1_.right_ref.mixed_ref, ...), custom_call_target="tpu_custom_call" | custom-call | flops 26625441792 | bytes 40697856 | tf_op jit(solution)/shard_map/attention_back/pallas_call | solution.py:416
  500.0 17.1 %outer_sum.10 = bf16[1152,1792]{1,0:T(8,128)(2,1)} custom-call(s32[1]{0:T(128)} %constant.172.clone.1.none_ref.scalars_ref, bf16[2208,1152]{1,0:T(8,128)(2,1)} %get-tuple-element.199.left_ref, bf16[2208,1792]{1,0:T(8,128)(2,1)} %get-tuple-element.200.right_ref.refs_1_), custom_call_target="tpu_custom_call" | custom-call | flops 9116319744 | bytes 13000704 | tf_op jit(solution)/shard_map/outer_sum/pallas_call | solution.py:416
  524.8 16.9 %attention_back.5 = (bf16[2208,1792]{1,0:T(8,128)(2,1)}, f32[1,8,1792]{2,1,0:T(8,128)}) custom-call(s32[1]{0:T(128)} %constant.172.clone.1.none_ref.scalars_ref, bf16[2208,1792]{1,0:T(8,128)(2,1)} %multiply_convert_fusion.1.qvk_ref, bf16[2208,768]{1,0:T(8,128)(2,1)} %get-tuple-element.177.refs_0_.right_ref.mixed_ref, ...), custom_call_target="tpu_custom_call" | custom-call | flops 8875147264 | bytes 40697856 | tf_op jit(solution)/shard_map/attention_back/pallas_call | solution.py:416
  543.9 17.0 %first_back.3 = (bf16[1,368,1152]{2,1,0:T(8,128)(2,1)}, bf16[1,361,1152]{2,1,0:T(8,128)(2,1)}, bf16[6,729,1152]{2,1,0:T(8,128)(2,1)}, f32[8,1152]{1,0:T(8,128)}) custom-call(s32[6]{0:T(128)} %pad_add_fusion.scalars_ref, bf16[2208,1792]{1,0:T(8,128)(2,1)} %get-tuple-element.209.refs_0_, bf16[2208,1792]{1,0:T(8,128)(2,1)} %get-tuple-element.200.right_ref.refs_1_, ...), custom_call_target="tpu_custom_call" | custom-call | flops 6077546496 | bytes 44341248 | tf_op jit(solution)/shard_map/first_back/pallas_call | solution.py:416
  563.6 17.2 %attention_back.6 = (bf16[2208,1792]{1,0:T(8,128)(2,1)}, f32[1,8,1792]{2,1,0:T(8,128)}) custom-call(s32[1]{0:T(128)} %constant.172.clone.1.none_ref.scalars_ref, bf16[2208,1792]{1,0:T(8,128)(2,1)} %multiply_convert_fusion.1.qvk_ref, bf16[2208,768]{1,0:T(8,128)(2,1)} %get-tuple-element.177.refs_0_.right_ref.mixed_ref, ...), custom_call_target="tpu_custom_call", output_to_operand_aliasing={{0}: (5, {})} | custom-call | flops 8875147264 | bytes 48611328 | tf_op jit(solution)/shard_map/attention_back/pallas_call | solution.py:416
  580.8 16.4 %first_back.4 = (bf16[1,368,1152]{2,1,0:T(8,128)(2,1)}, bf16[1,361,1152]{2,1,0:T(8,128)(2,1)}, bf16[6,729,1152]{2,1,0:T(8,128)(2,1)}, f32[8,1152]{1,0:T(8,128)}) custom-call(s32[6]{0:T(128)} %pad_add_fusion.scalars_ref, bf16[2208,1792]{1,0:T(8,128)(2,1)} %get-tuple-element.216.refs_0_, ...), custom_call_target="tpu_custom_call", output_to_operand_aliasing={{2}: (8, {})} | custom-call | flops 6077546496 | bytes 54418944 | tf_op jit(solution)/shard_map/first_back/pallas_call | solution.py:416
  598.7 17.0 %attention_back.7 = (bf16[2208,1792]{1,0:T(8,128)(2,1)}, f32[1,8,1792]{2,1,0:T(8,128)}) custom-call(s32[1]{0:T(128)} %constant.172.clone.1.none_ref.scalars_ref, bf16[2208,1792]{1,0:T(8,128)(2,1)} %multiply_convert_fusion.1.qvk_ref, bf16[2208,768]{1,0:T(8,128)(2,1)} %get-tuple-element.177.refs_0_.right_ref.mixed_ref, ...), custom_call_target="tpu_custom_call", output_to_operand_aliasing={{0}: (5, {})} | custom-call | flops 8875147264 | bytes 48611328 | tf_op jit(solution)/shard_map/attention_back/pallas_call | solution.py:416
  615.8 16.7 %outer_sum.11 = bf16[1152,1792]{1,0:T(8,128)(2,1)} custom-call(s32[1]{0:T(128)} %constant.172.clone.1.none_ref.scalars_ref, bf16[2208,1152]{1,0:T(8,128)(2,1)} %get-tuple-element.199.left_ref, bf16[2208,1792]{1,0:T(8,128)(2,1)} %get-tuple-element.237.right_ref.refs_0_), custom_call_target="tpu_custom_call" | custom-call | flops 9116319744 | bytes 13000704 | tf_op jit(solution)/shard_map/outer_sum/pallas_call | solution.py:416
  652.2 16.3 %first_back.5 = (bf16[1,368,1152]{2,1,0:T(8,128)(2,1)}, bf16[1,361,1152]{2,1,0:T(8,128)(2,1)}, bf16[6,729,1152]{2,1,0:T(8,128)(2,1)}, f32[8,1152]{1,0:T(8,128)}) custom-call(s32[6]{0:T(128)} %pad_add_fusion.scalars_ref, bf16[2208,1792]{1,0:T(8,128)(2,1)} %get-tuple-element.237.right_ref.refs_0_, ...), custom_call_target="tpu_custom_call", output_to_operand_aliasing={{2}: (8, {})} | custom-call | flops 6077546496 | bytes 54418944 | tf_op jit(solution)/shard_map/first_back/pallas_call | solution.py:416
  680.5 3.5 collective-permute-start.27
  692.6 10.6 %collective-permute-done.26 = bf16[1,72,1792]{2,1,0:T(8,128)(2,1)} collective-permute-done((bf16[1,72,1792]{2,1,0:T(8,128)(2,1)S(1)}, bf16[1,72,1792]{2,1,0:T(8,128)(2,1)}, u32[]{:S(2)}, u32[]{:S(2)}) %collective-permute-start.26) | collective-permute-done | bytes 258080 | tf_op jit(solution)/shard_map/ppermute | solution.py:624
  713.1 5.2 constant_dynamic-update-slice_fusion.9
  729.8 3.4 place.9
  (244 shorter events, 129.8 us)
Async XLA Ops:
  7.2 164.2 %all-gather.3.cloned.1.call-start = ((), (), s32[]{:S(2)}) async-start(), calls=%async_computation.2 | async-start | bytes 14598144 | tf_op jit(solution)/shard_map/all_gather | solution.py:690
  11.5 25.8 %collective-permute-start.2 = (bf16[1,72,1792]{2,1,0:T(8,128)(2,1)S(1)}, bf16[1,72,1792]{2,1,0:T(8,128)(2,1)S(1)}, u32[]{:S(2)}, u32[]{:S(2)}) collective-permute-start(bf16[1,72,1792]{2,1,0:T(8,128)(2,1)S(1)} %constant_dynamic-slice_fusion.10), channel_id=1, source_target_pairs={{0,6},{2,0},{4,2},{6,4},{1,7},{3,1},{5,3},{7,5},{8,14},{10,8},{12,... | collective-permute-start | bytes 774152 | tf_op jit(solution)/shard_map/ppermute | solution.py:624
  16.6 22.0 %collective-permute-start.1 = (bf16[1,72,1792]{2,1,0:T(8,128)(2,1)S(1)}, bf16[1,72,1792]{2,1,0:T(8,128)(2,1)S(1)}, u32[]{:S(2)}, u32[]{:S(2)}) collective-permute-start(bf16[1,72,1792]{2,1,0:T(8,128)(2,1)S(1)} %constant_dynamic-slice_fusion.10), channel_id=1, source_target_pairs={{0,4},{2,6},{4,0},{6,2},{1,5},{3,7},{5,1},{7,3},{8,12},{10,14},{12... | collective-permute-start | bytes 774152 | tf_op jit(solution)/shard_map/ppermute | solution.py:624
  16.6 22.0 %collective-permute-start = (bf16[1,72,1792]{2,1,0:T(8,128)(2,1)S(1)}, bf16[1,72,1792]{2,1,0:T(8,128)(2,1)}, u32[]{:S(2)}, u32[]{:S(2)}) collective-permute-start(bf16[1,72,1792]{2,1,0:T(8,128)(2,1)S(1)} %constant_dynamic-slice_fusion.10), channel_id=1, source_target_pairs={{0,2},{2,4},{4,6},{6,0},{1,3},{3,5},{5,7},{7,1},{8,10},{10,12},{12... | collective-permute-start | bytes 774152 | tf_op jit(solution)/shard_map/ppermute | solution.py:624
  39.3 231.1 %all-gather.5.cloned.1.call-start = ((), (), s32[]{:S(2)}) async-start(), calls=%async_computation.3 | async-start | bytes 10948608 | tf_op jit(solution)/shard_map/all_gather | solution.py:690
  41.1 418.8 %reduce-scatter.3.cloned.1.call-start = ((), (), s32[]{:S(2)}) async-start(), calls=%async_computation.4 | async-start | bytes 10948608 | tf_op jit(solution)/shard_map/reduce_scatter | solution.py:959
  42.2 21.5 %collective-permute-start.3 = (bf16[3,72,1792]{2,1,0:T(8,128)(2,1)S(1)}, bf16[3,72,1792]{2,1,0:T(8,128)(2,1)}, u32[]{:S(2)}, u32[]{:S(2)}) collective-permute-start(bf16[3,72,1792]{2,1,0:T(8,128)(2,1)S(1)} %constant_dynamic-update-slice_fusion.refs_1_), channel_id=1, source_target_pairs={{0,16},{8,24},{16,0},{24,8},{1,17},{9,25},{17,1},{25,9},{2,18},{10... | collective-permute-start | bytes 2322440 | tf_op jit(solution)/shard_map/ppermute | solution.py:619
  44.9 26.6 %collective-permute-start.6 = (bf16[4,72,1792]{2,1,0:T(8,128)(2,1)S(1)}, bf16[4,72,1792]{2,1,0:T(8,128)(2,1)S(1)}, u32[]{:S(2)}, u32[]{:S(2)}) collective-permute-start(bf16[4,72,1792]{2,1,0:T(8,128)(2,1)S(1)} %pad_maximum_fusion), channel_id=1, source_target_pairs={{0,1},{1,0},{2,3},{3,2},{4,5},{5,4},{6,7},{7,6},{8,9},{9,8},{10,11... | collective-permute-start | bytes 3096584 | tf_op jit(solution)/shard_map/ppermute | solution.py:619
  46.5 25.6 %collective-permute-start.4 = (bf16[3,72,1792]{2,1,0:T(8,128)(2,1)S(1)}, bf16[3,72,1792]{2,1,0:T(8,128)(2,1)}, u32[]{:S(2)}, u32[]{:S(2)}) collective-permute-start(bf16[3,72,1792]{2,1,0:T(8,128)(2,1)S(1)} %constant_dynamic-update-slice_fusion.refs_1_), channel_id=1, source_target_pairs={{0,8},{8,0},{16,24},{24,16},{1,9},{9,1},{17,25},{25,17},{2,10},{10... | collective-permute-start | bytes 2322440 | tf_op jit(solution)/shard_map/ppermute | solution.py:619
  71.5 48.0 %collective-permute-start.7 = (bf16[4,72,1792]{2,1,0:T(8,128)(2,1)S(1)}, bf16[4,72,1792]{2,1,0:T(8,128)(2,1)S(1)}, u32[]{:S(2)}, u32[]{:S(2)}) collective-permute-start(bf16[4,72,1792]{2,1,0:T(8,128)(2,1)S(1)} %collective-permute-done.6.refs_0_), channel_id=1, source_target_pairs={{0,16},{8,24},{16,0},{24,8},{1,17},{9,25},{17,1},{25,9},{2,18},{10... | collective-permute-start | bytes 3096584 | tf_op jit(solution)/shard_map/ppermute | solution.py:619
  269.1 374.9 %reduce-scatter.5.cloned.1.call-start = ((), (), s32[]{:S(2)}) async-start(), calls=%async_computation.5 | async-start | bytes 14598144 | tf_op jit(solution)/shard_map/reduce_scatter | solution.py:1084
  306.4 152.9 %collective-permute-start.10 = (bf16[3,729,1152]{2,1,0:T(8,128)(2,1)}, bf16[3,729,1152]{2,1,0:T(8,128)(2,1)}, u32[]{:S(2)}, u32[]{:S(2)}) collective-permute-start(bf16[3,729,1152]{2,1,0:T(8,128)(2,1)} %get-tuple-element.193), channel_id=1, source_target_pairs={{0,1},{1,0},{2,3},{3,2},{4,5},{5,4},{6,7},{7,6},{8,9},{9,8},{10,11... | collective-permute-start | bytes 15116552 | tf_op jit(solution)/shard_map/ppermute | solution.py:619
  459.9 39.5 %collective-permute-start.11 = (bf16[1,72,2304]{2,1,0:T(8,128)(2,1)}, bf16[1,72,2304]{2,1,0:T(8,128)(2,1)S(1)}, u32[]{:S(2)}, u32[]{:S(2)}) collective-permute-start(bf16[1,72,2304]{2,1,0:T(8,128)(2,1)} %bitcast.100), channel_id=1, source_target_pairs={{0,16},{8,24},{16,0},{24,8},{1,17},{9,25},{17,1},{25,9},{2,18},{10... | collective-permute-start | bytes 995336 | tf_op jit(solution)/shard_map/ppermute | solution.py:619
  499.4 17.7 %collective-permute-start.12 = (bf16[1,72,2304]{2,1,0:T(8,128)(2,1)S(1)}, bf16[1,72,2304]{2,1,0:T(8,128)(2,1)S(1)}, u32[]{:S(2)}, u32[]{:S(2)}) collective-permute-start(bf16[1,72,2304]{2,1,0:T(8,128)(2,1)S(1)} %bitcast.102), channel_id=1, source_target_pairs={{0,8},{8,0},{16,24},{24,16},{1,9},{9,1},{17,25},{25,17},{2,10},{10... | collective-permute-start | bytes 995336 | tf_op jit(solution)/shard_map/ppermute | solution.py:619
  499.5 17.7 %collective-permute-start.13 = (bf16[1,72,2304]{2,1,0:T(8,128)(2,1)S(1)}, bf16[1,72,2304]{2,1,0:T(8,128)(2,1)S(1)}, u32[]{:S(2)}, u32[]{:S(2)}) collective-permute-start(bf16[1,72,2304]{2,1,0:T(8,128)(2,1)S(1)} %collective-permute-done.11.refs_1_), channel_id=1, source_target_pairs={{0,8},{8,0},{16,24},{24,16},{1,9},{9,1},{17,25},{25,17},{2,10},{10... | collective-permute-start | bytes 995336 | tf_op jit(solution)/shard_map/ppermute | solution.py:619
  524.7 17.0 %collective-permute-start.14 = (bf16[4,2,72,1792]{3,2,0,1:T(8,128)(2,1)}, bf16[4,2,72,1792]{3,2,0,1:T(8,128)(2,1)S(1)}, u32[]{:S(2)}, u32[]{:S(2)}) collective-permute-start(bf16[4,2,72,1792]{3,2,0,1:T(8,128)(2,1)} %copy_bitcast_fusion.1), channel_id=1, source_target_pairs={{0,8},{8,0},{16,24},{24,16},{1,9},{9,1},{17,25},{25,17},{2,10},{10... | collective-permute-start | bytes 6193160 | tf_op jit(solution)/shard_map/ppermute | solution.py:619
  560.9 37.6 %collective-permute-start.15 = (bf16[1,368,1152]{2,1,0:T(8,128)(2,1)}, bf16[1,368,1152]{2,1,0:T(8,128)(2,1)}, u32[]{:S(2)}, u32[]{:S(2)}) collective-permute-start(bf16[1,368,1152]{2,1,0:T(8,128)(2,1)} %get-tuple-element.213), channel_id=1, source_target_pairs={{0,1},{1,0},{2,3},{3,2},{4,5},{5,4},{6,7},{7,6},{8,9},{9,8},{10,11... | collective-permute-start | bytes 2543624 | tf_op jit(solution)/shard_map/ppermute | solution.py:619
  561.6 70.9 %collective-permute-start.18 = (bf16[1,361,1152]{2,1,0:T(8,128)(2,1)}, bf16[1,361,1152]{2,1,0:T(8,128)(2,1)}, u32[]{:S(2)}, u32[]{:S(2)}) collective-permute-start(bf16[1,361,1152]{2,1,0:T(8,128)(2,1)} %get-tuple-element.228), channel_id=1, source_target_pairs={{0,1},{1,0},{2,3},{3,2},{4,5},{5,4},{6,7},{7,6},{8,9},{9,8},{10,11... | collective-permute-start | bytes 2495240 | tf_op jit(solution)/shard_map/ppermute | solution.py:619
  563.0 34.2 %collective-permute-start.16 = (bf16[4,72,1792]{2,1,0:T(8,128)(2,1)S(1)}, bf16[4,72,1792]{2,1,0:T(8,128)(2,1)S(1)}, u32[]{:S(2)}, u32[]{:S(2)}) collective-permute-start(bf16[4,72,1792]{2,1,0:T(8,128)(2,1)S(1)} %dynamic-slice_bitcast_fusion.1), channel_id=1, source_target_pairs={{0,16},{8,24},{16,0},{24,8},{1,17},{9,25},{17,1},{25,9},{2,18},{10... | collective-permute-start | bytes 3096584 | tf_op jit(solution)/shard_map/ppermute | solution.py:619
  598.5 35.9 %collective-permute-start.17 = (bf16[1,368,1152]{2,1,0:T(8,128)(2,1)}, bf16[1,368,1152]{2,1,0:T(8,128)(2,1)S(1)}, u32[]{:S(2)}, u32[]{:S(2)}) collective-permute-start(bf16[1,368,1152]{2,1,0:T(8,128)(2,1)} %get-tuple-element.223), channel_id=1, source_target_pairs={{0,1},{1,0},{2,3},{3,2},{4,5},{5,4},{6,7},{7,6},{8,9},{9,8},{10,11... | collective-permute-start | bytes 2543624 | tf_op jit(solution)/shard_map/ppermute | solution.py:619
  638.2 39.8 %collective-permute-start.24 = (bf16[1,361,1152]{2,1,0:T(8,128)(2,1)}, bf16[1,361,1152]{2,1,0:T(8,128)(2,1)}, u32[]{:S(2)}, u32[]{:S(2)}) collective-permute-start(bf16[1,361,1152]{2,1,0:T(8,128)(2,1)} %get-tuple-element.259), channel_id=1, source_target_pairs={{0,1},{1,0},{2,3},{3,2},{4,5},{5,4},{6,7},{7,6},{8,9},{9,8},{10,11... | collective-permute-start | bytes 2495240 | tf_op jit(solution)/shard_map/ppermute | solution.py:619
  644.8 23.7 %collective-permute-start.21 = (bf16[1,72,1792]{2,1,0:T(8,128)(2,1)}, bf16[1,72,1792]{2,1,0:T(8,128)(2,1)}, u32[]{:S(2)}, u32[]{:S(2)}) collective-permute-start(bf16[1,72,1792]{2,1,0:T(8,128)(2,1)} %get-tuple-element.316), channel_id=1, source_target_pairs={{0,2},{2,4},{4,6},{6,0},{1,3},{3,5},{5,7},{7,1},{8,10},{10,12},{12... | collective-permute-start | bytes 774152 | tf_op jit(solution)/shard_map/ppermute | solution.py:624
  646.5 22.0 %collective-permute-start.23 = (bf16[1,72,1792]{2,1,0:T(8,128)(2,1)S(1)}, bf16[1,72,1792]{2,1,0:T(8,128)(2,1)}, u32[]{:S(2)}, u32[]{:S(2)}) collective-permute-start(bf16[1,72,1792]{2,1,0:T(8,128)(2,1)S(1)} %get-tuple-element.317), channel_id=1, source_target_pairs={{0,6},{2,0},{4,2},{6,4},{1,7},{3,1},{5,3},{7,5},{8,14},{10,8},{12,... | collective-permute-start | bytes 774152 | tf_op jit(solution)/shard_map/ppermute | solution.py:624
  648.6 23.1 %collective-permute-start.22 = (bf16[1,72,1792]{2,1,0:T(8,128)(2,1)S(1)}, bf16[1,72,1792]{2,1,0:T(8,128)(2,1)}, u32[]{:S(2)}, u32[]{:S(2)}) collective-permute-start(bf16[1,72,1792]{2,1,0:T(8,128)(2,1)S(1)} %get-tuple-element.318), channel_id=1, source_target_pairs={{0,4},{2,6},{4,0},{6,2},{1,5},{3,7},{5,1},{7,3},{8,12},{10,14},{12... | collective-permute-start | bytes 774152 | tf_op jit(solution)/shard_map/ppermute | solution.py:624
  652.2 24.3 %collective-permute-start.20 = (bf16[4,72,1792]{2,1,0:T(8,128)(2,1)}, bf16[4,72,1792]{2,1,0:T(8,128)(2,1)}, u32[]{:S(2)}, u32[]{:S(2)}) collective-permute-start(bf16[4,72,1792]{2,1,0:T(8,128)(2,1)} %dynamic-slice_bitcast_fusion), channel_id=1, source_target_pairs={{0,16},{8,24},{16,0},{24,8},{1,17},{9,25},{17,1},{25,9},{2,18},{10... | collective-permute-start | bytes 3096584 | tf_op jit(solution)/shard_map/ppermute | solution.py:619
  678.3 26.4 %collective-permute-start.29 = (bf16[1,368,1152]{2,1,0:T(8,128)(2,1)}, bf16[1,368,1152]{2,1,0:T(8,128)(2,1)S(1)}, u32[]{:S(2)}, u32[]{:S(2)}) collective-permute-start(bf16[1,368,1152]{2,1,0:T(8,128)(2,1)} %get-tuple-element.266), channel_id=1, source_target_pairs={{0,1},{1,0},{2,3},{3,2},{4,5},{5,4},{6,7},{7,6},{8,9},{9,8},{10,11... | collective-permute-start | bytes 2543624 | tf_op jit(solution)/shard_map/ppermute | solution.py:619
  684.0 19.1 %collective-permute-start.26 = (bf16[1,72,1792]{2,1,0:T(8,128)(2,1)S(1)}, bf16[1,72,1792]{2,1,0:T(8,128)(2,1)}, u32[]{:S(2)}, u32[]{:S(2)}) collective-permute-start(bf16[1,72,1792]{2,1,0:T(8,128)(2,1)S(1)} %get-tuple-element.315), channel_id=1, source_target_pairs={{0,4},{2,6},{4,0},{6,2},{1,5},{3,7},{5,1},{7,3},{8,12},{10,14},{12... | collective-permute-start | bytes 774152 | tf_op jit(solution)/shard_map/ppermute | solution.py:624
  708.4 17.2 %collective-permute-start.35 = (f32[112,128]{1,0:T(8,128)S(1)}, f32[112,128]{1,0:T(8,128)S(1)}, u32[]{:S(2)}, u32[]{:S(2)}) collective-permute-start(f32[112,128]{1,0:T(8,128)S(1)} %pad_bitcast_fusion), channel_id=1, source_target_pairs={{0,16},{8,24},{16,0},{24,8},{1,17},{9,25},{17,1},{25,9},{2,18},{10... | collective-permute-start | bytes 172040 | tf_op jit(solution)/shard_map/ppermute | solution.py:731
  709.3 17.8 %collective-permute-start.36 = (f32[112,128]{1,0:T(8,128)S(1)}, f32[112,128]{1,0:T(8,128)S(1)}, u32[]{:S(2)}, u32[]{:S(2)}) collective-permute-start(f32[112,128]{1,0:T(8,128)S(1)} %pad_bitcast_fusion), channel_id=1, source_target_pairs={{0,24},{8,16},{16,8},{24,0},{1,25},{9,17},{17,9},{25,1},{2,26},{10... | collective-permute-start | bytes 172040 | tf_op jit(solution)/shard_map/ppermute | solution.py:731
  709.3 18.3 %collective-permute-start.34 = (f32[112,128]{1,0:T(8,128)S(1)}, f32[112,128]{1,0:T(8,128)S(1)}, u32[]{:S(2)}, u32[]{:S(2)}) collective-permute-start(f32[112,128]{1,0:T(8,128)S(1)} %pad_bitcast_fusion), channel_id=1, source_target_pairs={{0,8},{8,0},{16,24},{24,16},{1,9},{9,1},{17,25},{25,17},{2,10},{10... | collective-permute-start | bytes 172040 | tf_op jit(solution)/shard_map/ppermute | solution.py:731
  710.6 17.1 %collective-permute-start.32 = (bf16[1,72,1792]{2,1,0:T(8,128)(2,1)S(1)}, bf16[1,72,1792]{2,1,0:T(8,128)(2,1)}, u32[]{:S(2)}, u32[]{:S(2)}) collective-permute-start(bf16[1,72,1792]{2,1,0:T(8,128)(2,1)S(1)} %add_convert_fusion.refs_0_), channel_id=1, source_target_pairs={{0,16},{8,24},{16,0},{24,8},{1,17},{9,25},{17,1},{25,9},{2,18},{10... | collective-permute-start | bytes 774152 | tf_op jit(solution)/shard_map/ppermute | solution.py:619
  727.1 21.4 %collective-permute-start.40 = (bf16[1,361,1152]{2,1,0:T(8,128)(2,1)}, bf16[1,361,1152]{2,1,0:T(8,128)(2,1)S(1)}, u32[]{:S(2)}, u32[]{:S(2)}) collective-permute-start(bf16[1,361,1152]{2,1,0:T(8,128)(2,1)} %get-tuple-element.295), channel_id=1, source_target_pairs={{0,1},{1,0},{2,3},{3,2},{4,5},{5,4},{6,7},{7,6},{8,9},{9,8},{10,11... | collective-permute-start | bytes 2495240 | tf_op jit(solution)/shard_map/ppermute | solution.py:619
  (49 other events, 634.7 us)
Sparse Core Ops, SparseCore 0:
  39.5 119.2 all-gather.2
  162.2 85.3 all-gather.4
  269.3 170.0 reduce-scatter.2
  459.5 181.0 reduce-scatter.4

commit v4 on v3

--- a/solution.py
+++ b/solution.py
@@ -719,6 +719,32 @@
     return add_low(*terms)
 
 
+def place_cuts(found, cuts):
+    copy = lax.axis_index("replica")
+    pieces = list(found.values())
+    rows = pieces[0].shape[1]
+
+    def kernel(slots_ref, *refs):
+        for at in range(len(pieces)):
+            values = refs[at][...].astype(jnp.float32)
+            for (start, size), out_ref in zip(cuts, refs[len(pieces) :]):
+                out_ref[pl.ds(slots_ref[at], 1)] = values[:, :, start : start + size]
+
+    def whole(shape):
+        return fixed(shape, lambda i, s: (0, 0, 0))
+
+    shapes = [(len(pieces), rows, size) for _, size in cuts]
+    wholes = call(
+        kernel,
+        "place_cuts",
+        (1,),
+        jnp.stack([copy ^ bits for bits in found]).astype(jnp.int32),
+        [(piece, whole(piece.shape)) for piece in pieces],
+        [(shape, jnp.float32, whole(shape)) for shape in shapes],
+    )
+    return [array.reshape(-1, array.shape[2]) for array in wholes]
+
+
 def place_found(found):
     copy = lax.axis_index("replica")
     whole = place(list(found.values()), [[copy ^ bits] for bits in found], len(found))
@@ -1225,6 +1251,7 @@
     third_sums = third_sums + sums
     in_parts.append(trade_halves(input_grad))
     lower = in_parts[-1][1]
+    out_whole = lay(out_whole, out_parts, 0)
     up_found = join_on({0: up_share[None]}, far_bits)
     near_total = add_low(
         sum_lines(near[0]), *(swap(term, "tensor", rank) for rank, term in zip(ranks[1:], far))
@@ -1233,7 +1260,6 @@
         near_total,
         in_parts,
         up_found,
-        out_parts,
         out_whole,
         input_whole,
         third_sums,
@@ -1246,7 +1272,6 @@
         near_total,
         [*in_parts[:-1], in_parts[-1][:1]],
         up_found,
-        out_parts,
         out_whole,
         input_whole,
         third_sums,
@@ -1257,11 +1282,12 @@
         down_grads,
     )
     in_parts[-1].append(lower)
-    out_whole = lay(out_whole, out_parts, 0)
     for slot in range(last):
         input_whole = lay_halves(input_whole, in_parts[slot], slot)
     near_found = among_replicas(near_total)
-    up_o_grads = place_found(join_on(up_found, far_bit))
+    up_grads, o_grads = place_cuts(
+        join_on(up_found, far_bit), [(0, units), (unit_width + SHIFT, width)]
+    )
 
     def all_ranks(parts, size):
         whole = jnp.zeros((tensor_count * size,), full)
@@ -1289,7 +1315,7 @@
     summed = sum_over(summed, "fsdp")
     summed, in_parts[-1][1] = tie(summed, in_parts[-1][1])
     summed = sum_over(summed, "tensor").reshape(-1)
-    in_grads = place_found(near_found)
+    q_grads, v_grads, k_grads = place_cuts(near_found, [(at * width, width) for at in range(3)])
     input_whole = lay_halves(input_whole, in_parts[-1], last)
     ends, start = [], 0
     for size in sizes:
@@ -1302,16 +1328,16 @@
         input_whole,
         gain_one,
         shift_one,
-        in_grads[:, :width].astype(full),
+        q_grads,
         q_sum,
-        in_grads[:, 2 * width : 3 * width].astype(full),
-        in_grads[:, width : 2 * width].astype(full),
+        k_grads,
+        v_grads,
         v_sum,
-        up_o_grads[:, unit_width + SHIFT : unit_width + SHIFT + width].astype(full).T,
+        o_grads.T,
         o_sum,
         gain_two,
         shift_two,
-        up_o_grads[:, :units].astype(full),
+        up_grads,
         up_sum,
         down_grads[:, :units].astype(full).T,
         down_sum,

time: 766 us -> 751 us (0.980)
  other arithmetic: 34.2 us -> 25 us
  transfers between devices with their start and end apart: 48 -> 48, of which waited for: 13 -> 11; matrix products, arithmetic and copies ran while one was open for 12% -> 12% of each run, Pallas kernels for 71% -> 73%
where the time goes in v4:
time: 751 us; the launch traced here: 746 us
  Pallas kernels  543 us (72%)
  waiting for transfers between devices  50.6 us (7%)
  starting transfers between devices  41.3 us (5%)
  local copies, waits for them, and re-layouts  39.4 us (5%)
  matrix products  31.4 us (4%)
  other arithmetic  25 us (3%)
  between operations  14.8 us (2%)
    pallas_call x26, Pallas kernels, call(): pl.pallas_call(kernel, grid_spec=pltpu.PrefetchScalarGridSpec(num_scalar_...  543 us
    ppermute x28, waiting for transfers between devices, swap(): lax.ppermute(array, axis, [(rank, rank ^ bits) for rank in range(size)])  32.7 us
    dot_general x2, matrix products, matmul(): return jnp.dot(first_op, second_op, preferred_element_type=jnp.float32)  31.4 us
    ppermute x28, starting transfers between devices, swap(): lax.ppermute(array, axis, [(rank, rank ^ bits) for rank in range(size)])  17.3 us
    ppermute x9, starting transfers between devices, turn(): lax.ppermute(array, axis, [(rank, (rank + steps) % size) for rank in rang...  15.9 us
    ppermute x9, waiting for transfers between devices, turn(): lax.ppermute(array, axis, [(rank, (rank + steps) % size) for rank in rang...  15.8 us
  transfers between devices with their start and end apart: 48, of which 11 were waited for; matrix products, arithmetic and copies ran while one was open for 12% of the time, Pallas kernels for 73%

profile of v4, /device:TPU:0, one launch (start us, length us, event | category | flops | bytes accessed | tf_op | source)
XLA Modules:
  0.0 745.9 jit_solution(13837788280629835025)
XLA Ops:
  11.5 5.1 collective-permute-start.2
  25.5 11.4 %first_norm.1 = (bf16[2208,1152]{1,0:T(8,128)(2,1)}, bf16[2208,1152]{1,0:T(8,128)(2,1)}, f32[8,1152]{1,0:T(8,128)}) custom-call(s32[6]{0:T(128)} %pad_add_fusion.scalars_ref, bf16[6,729,1152]{2,1,0:T(8,128)(2,1)} %refs_4_.7, bf16[6,729,1152]{2,1,0:T(8,128)(2,1)} %cot_ref.1, f32[1,1152]{1,0:T(1,128)} %reshape.129.gain_ref.refs_6_, f32[1,1152]{1,0:T(1,128)} %reshape.130.shift_ref), custom_call_target="tpu_custom_call" | custom-call | bytes 20164608 | tf_op jit(solution)/shard_map/first_norm/pallas_call | solution.py:416
  46.5 17.3 %collective-permute-done.3.refs_2_ = bf16[3,72,1792]{2,1,0:T(8,128)(2,1)} collective-permute-done((bf16[3,72,1792]{2,1,0:T(8,128)(2,1)S(1)}, bf16[3,72,1792]{2,1,0:T(8,128)(2,1)}, u32[]{:S(2)}, u32[]{:S(2)}) %collective-permute-start.3) | collective-permute-done | bytes 774176 | tf_op jit(solution)/shard_map/ppermute | solution.py:619
  64.5 7.0 collective-permute-done.6.refs_0_
  72.0 5.1 place.3
  77.1 15.7 %multiply_convert_fusion.1.qvk_ref = bf16[2208,1792]{1,0:T(8,128)(2,1)} fusion(bf16[2208,1152]{1,0:T(8,128)(2,1)} %get-tuple-element.203.left_ref, bf16[1152,1792]{1,0:T(8,128)(2,1)} %bitcast.82, f32[1792]{0:T(1024)S(1)} %fusion.7, f32[1792]{0:T(1024)S(1)} %select_maximum_fusion.1), kind=kOutput, calls=%fused_computation.1 | convolution fusion | flops 9128189952 | bytes 17143808 | tf_op jit(solution)/shard_map/dot_general | solution.py:19
  92.8 26.7 %attention.2 = (bf16[2208,768]{1,0:T(8,128)(2,1)}, bf16[24,736,736]{2,1,0:T(8,128)(2,1)}) custom-call(s32[1]{0:T(128)} %constant.172.clone.1.none_ref.scalars_ref, bf16[2208,1792]{1,0:T(8,128)(2,1)} %multiply_convert_fusion.1.qvk_ref), custom_call_target="tpu_custom_call" | custom-call | flops 13312720896 | bytes 7913472 | tf_op jit(solution)/shard_map/attention/pallas_call | solution.py:416
  123.9 5.1 place.4
  128.9 15.7 %multiply_convert_fusion.qvk_ref = bf16[2208,1792]{1,0:T(8,128)(2,1)} fusion(bf16[2208,1152]{1,0:T(8,128)(2,1)} %get-tuple-element.203.left_ref, bf16[1152,1792]{1,0:T(8,128)(2,1)} %bitcast.86, f32[1792]{0:T(1024)S(1)} %select_maximum_fusion, f32[1792]{0:T(1024)S(1)} %fusion.7), kind=kOutput, calls=%fused_computation | convolution fusion | flops 9128189952 | bytes 17143808 | tf_op jit(solution)/shard_map/dot_general | solution.py:19
  144.7 26.7 %attention.3 = (bf16[2208,768]{1,0:T(8,128)(2,1)}, bf16[24,736,736]{2,1,0:T(8,128)(2,1)}) custom-call(s32[1]{0:T(128)} %constant.172.clone.1.none_ref.scalars_ref, bf16[2208,1792]{1,0:T(8,128)(2,1)} %multiply_convert_fusion.qvk_ref), custom_call_target="tpu_custom_call" | custom-call | flops 13312720896 | bytes 7913472 | tf_op jit(solution)/shard_map/attention/pallas_call | solution.py:416
  171.4 17.7 %middle_norm.1 = (f32[2208,1152]{1,0:T(8,128)}, bf16[2208,1152]{1,0:T(8,128)(2,1)}) custom-call(s32[6]{0:T(128)} %pad_add_fusion.scalars_ref, bf16[2208,768]{1,0:T(8,128)(2,1)} %get-tuple-element.181.refs_0_.right_ref.mixed_ref, bf16[2208,768]{1,0:T(8,128)(2,1)} %get-tuple-element.180.refs_1_.right_ref.mixed_ref, ...), custom_call_target="tpu_custom_call" | custom-call | flops 7813988352 | bytes 45186048 | tf_op jit(solution)/shard_map/middle_norm/pallas_call | solution.py:416
  189.1 48.6 %hidden.1 = (bf16[2208,4608]{1,0:T(8,128)(2,1)}, bf16[2208,4608]{1,0:T(8,128)(2,1)}) custom-call(s32[6]{0:T(128)} %pad_add_fusion.scalars_ref, bf16[2208,1152]{1,0:T(8,128)(2,1)} %get-tuple-element.183.second_ref.left_ref, bf16[2304,3072]{1,0:T(8,128)(2,1)} %all-gather.3.cloned.1.call-done.refs_2_.refs_3_.weight_ref.refs_7_.refs_8_, f32[1,4608]{1,0:T(1,128)} %bitcast.103), custom_call_target="tpu_custom_call" | custom-call | flops 23441965056 | bytes 19261440 | tf_op jit(solution)/shard_map/hidden/pallas_call | solution.py:416
  237.7 31.3 %outer_sum.6 = bf16[2304,2304]{1,0:T(8,128)(2,1)} custom-call(s32[1]{0:T(128)} %constant.172.clone.1.none_ref.scalars_ref, bf16[2208,1152]{1,0:T(8,128)(2,1)} %get-tuple-element.190.left_ref.grad_ref.refs_5_, bf16[2208,4608]{1,0:T(8,128)(2,1)} %get-tuple-element.186.right_ref.refs_0_.refs_1_), custom_call_target="tpu_custom_call" | custom-call | flops 23441965056 | bytes 25436160 | tf_op jit(solution)/shard_map/outer_sum/pallas_call | solution.py:416
  270.3 36.0 %output.1 = (bf16[3,729,1152]{2,1,0:T(8,128)(2,1)}, bf16[6,729,1152]{2,1,0:T(8,128)(2,1)}) custom-call(s32[6]{0:T(128)} %pad_add_fusion.scalars_ref, bf16[2208,4608]{1,0:T(8,128)(2,1)} %get-tuple-element.186.right_ref.refs_0_.refs_1_, bf16[2208,4608]{1,0:T(8,128)(2,1)} %get-tuple-element.186.right_ref.refs_0_.refs_1_, ...), custom_call_target="tpu_custom_call" | custom-call | flops 23441965056 | bytes 72110592 | tf_op jit(solution)/shard_map/output/pallas_call | solution.py:416
  307.8 37.6 %hidden_back.1 = (bf16[2208,4608]{1,0:T(8,128)(2,1)}, f32[8,4608]{1,0:T(8,128)}) custom-call(s32[6]{0:T(128)} %pad_add_fusion.scalars_ref, bf16[2208,1152]{1,0:T(8,128)(2,1)} %get-tuple-element.190.left_ref.grad_ref.refs_5_, bf16[2304,2304]{1,0:T(8,128)(2,1)} %all-gather.5.cloned.1.call-done.refs_2_.refs_3_.weight_ref, ...), custom_call_target="tpu_custom_call" | custom-call | flops 23441965056 | bytes 36052992 | tf_op jit(solution)/shard_map/hidden_back/pallas_call | solution.py:416
  345.4 31.5 %outer_sum.7.refs_0_ = bf16[2304,3072]{1,0:T(8,128)(2,1)} custom-call(s32[1]{0:T(128)} %constant.172.clone.1.none_ref.scalars_ref, bf16[2208,1152]{1,0:T(8,128)(2,1)} %get-tuple-element.183.second_ref.left_ref, bf16[2208,4608]{1,0:T(8,128)(2,1)} %get-tuple-element.193.right_ref.refs_0_.refs_1_), custom_call_target="tpu_custom_call" | custom-call | flops 23441965056 | bytes 25436160 | tf_op jit(solution)/shard_map/outer_sum/pallas_call | solution.py:416
  376.9 62.7 %middle_back.1 = (f32[2208,1152]{1,0:T(8,128)}, bf16[2208,1152]{1,0:T(8,128)(2,1)}, f32[8,1152]{1,0:T(8,128)}, bf16[2208,768]{1,0:T(8,128)(2,1)}, bf16[2208,768]{1,0:T(8,128)(2,1)}) custom-call(s32[6]{0:T(128)} %pad_add_fusion.scalars_ref, bf16[2208,4608]{1,0:T(8,128)(2,1)} %get-tuple-element.193.right_ref.refs_0_.refs_1_, ...), custom_call_target="tpu_custom_call" | custom-call | flops 31255953408 | bytes 112587264 | tf_op jit(solution)/shard_map/middle_back/pallas_call | solution.py:416
  439.6 9.9 %outer_sum.8.refs_0_ = bf16[2304,3072]{1,0:T(8,128)(2,1)} custom-call(s32[6]{0:T(128)} %pad_add_fusion.scalars_ref, bf16[2208,1152]{1,0:T(8,128)(2,1)} %get-tuple-element.194.left_ref, bf16[2208,768]{1,0:T(8,128)(2,1)} %get-tuple-element.181.refs_0_.right_ref.mixed_ref, bf16[2304,3072]{1,0:T(8,128)(2,1)} %outer_sum.7.refs_0_), custom_call_target="tpu_custom_call", output_to_operand_aliasing={{}: (3, {})} | custom-call | flops 3906994176 | bytes 22634496 | tf_op jit(solution)/shard_map/outer_sum/pallas_call | solution.py:416
  449.4 9.8 %outer_sum.9 = bf16[2304,3072]{1,0:T(8,128)(2,1)} custom-call(s32[6]{0:T(128)} %pad_add_fusion.scalars_ref, bf16[2208,1152]{1,0:T(8,128)(2,1)} %get-tuple-element.194.left_ref, bf16[2208,768]{1,0:T(8,128)(2,1)} %get-tuple-element.180.refs_1_.right_ref.mixed_ref, bf16[2304,3072]{1,0:T(8,128)(2,1)} %outer_sum.8.refs_0_), custom_call_target="tpu_custom_call", output_to_operand_aliasing={{}: (3, {})} | custom-call | flops 3906994176 | bytes 22634496 | tf_op jit(solution)/shard_map/outer_sum/pallas_call | solution.py:416
  461.1 38.3 %attention_back.4 = (bf16[2208,1792]{1,0:T(8,128)(2,1)}, f32[3,8,1792]{2,1,0:T(8,128)}) custom-call(s32[1]{0:T(128)} %constant.172.clone.1.none_ref.scalars_ref, bf16[2208,1792]{1,0:T(8,128)(2,1)} %multiply_convert_fusion.qvk_ref, bf16[2208,768]{1,0:T(8,128)(2,1)} %get-tuple-element.180.refs_1_.right_ref.mixed_ref, ...), custom_call_target="tpu_custom_call" | custom-call | flops 26625441792 | bytes 40697856 | tf_op jit(solution)/shard_map/attention_back/pallas_call | solution.py:416
  500.0 17.1 %outer_sum.10 = bf16[1152,1792]{1,0:T(8,128)(2,1)} custom-call(s32[1]{0:T(128)} %constant.172.clone.1.none_ref.scalars_ref, bf16[2208,1152]{1,0:T(8,128)(2,1)} %get-tuple-element.203.left_ref, bf16[2208,1792]{1,0:T(8,128)(2,1)} %get-tuple-element.204.right_ref.refs_1_), custom_call_target="tpu_custom_call" | custom-call | flops 9116319744 | bytes 13000704 | tf_op jit(solution)/shard_map/outer_sum/pallas_call | solution.py:416
  523.5 16.9 %attention_back.5 = (bf16[2208,1792]{1,0:T(8,128)(2,1)}, f32[1,8,1792]{2,1,0:T(8,128)}) custom-call(s32[1]{0:T(128)} %constant.172.clone.1.none_ref.scalars_ref, bf16[2208,1792]{1,0:T(8,128)(2,1)} %multiply_convert_fusion.1.qvk_ref, bf16[2208,768]{1,0:T(8,128)(2,1)} %get-tuple-element.181.refs_0_.right_ref.mixed_ref, ...), custom_call_target="tpu_custom_call" | custom-call | flops 8875147264 | bytes 40697856 | tf_op jit(solution)/shard_map/attention_back/pallas_call | solution.py:416
  543.2 16.9 %first_back.3 = (bf16[1,368,1152]{2,1,0:T(8,128)(2,1)}, bf16[1,361,1152]{2,1,0:T(8,128)(2,1)}, bf16[6,729,1152]{2,1,0:T(8,128)(2,1)}, f32[8,1152]{1,0:T(8,128)}) custom-call(s32[6]{0:T(128)} %pad_add_fusion.scalars_ref, bf16[2208,1792]{1,0:T(8,128)(2,1)} %get-tuple-element.213.refs_0_, bf16[2208,1792]{1,0:T(8,128)(2,1)} %get-tuple-element.204.right_ref.refs_1_, ...), custom_call_target="tpu_custom_call" | custom-call | flops 6077546496 | bytes 44341248 | tf_op jit(solution)/shard_map/first_back/pallas_call | solution.py:416
  562.9 17.2 %attention_back.6 = (bf16[2208,1792]{1,0:T(8,128)(2,1)}, f32[1,8,1792]{2,1,0:T(8,128)}) custom-call(s32[1]{0:T(128)} %constant.172.clone.1.none_ref.scalars_ref, bf16[2208,1792]{1,0:T(8,128)(2,1)} %multiply_convert_fusion.1.qvk_ref, bf16[2208,768]{1,0:T(8,128)(2,1)} %get-tuple-element.181.refs_0_.right_ref.mixed_ref, ...), custom_call_target="tpu_custom_call", output_to_operand_aliasing={{0}: (5, {})} | custom-call | flops 8875147264 | bytes 48611328 | tf_op jit(solution)/shard_map/attention_back/pallas_call | solution.py:416
  580.1 16.4 %first_back.4 = (bf16[1,368,1152]{2,1,0:T(8,128)(2,1)}, bf16[1,361,1152]{2,1,0:T(8,128)(2,1)}, bf16[6,729,1152]{2,1,0:T(8,128)(2,1)}, f32[8,1152]{1,0:T(8,128)}) custom-call(s32[6]{0:T(128)} %pad_add_fusion.scalars_ref, bf16[2208,1792]{1,0:T(8,128)(2,1)} %get-tuple-element.220.refs_0_, ...), custom_call_target="tpu_custom_call", output_to_operand_aliasing={{2}: (8, {})} | custom-call | flops 6077546496 | bytes 54418944 | tf_op jit(solution)/shard_map/first_back/pallas_call | solution.py:416
  598.6 17.0 %attention_back.7 = (bf16[2208,1792]{1,0:T(8,128)(2,1)}, f32[1,8,1792]{2,1,0:T(8,128)}) custom-call(s32[1]{0:T(128)} %constant.172.clone.1.none_ref.scalars_ref, bf16[2208,1792]{1,0:T(8,128)(2,1)} %multiply_convert_fusion.1.qvk_ref, bf16[2208,768]{1,0:T(8,128)(2,1)} %get-tuple-element.181.refs_0_.right_ref.mixed_ref, ...), custom_call_target="tpu_custom_call", output_to_operand_aliasing={{0}: (5, {})} | custom-call | flops 8875147264 | bytes 48611328 | tf_op jit(solution)/shard_map/attention_back/pallas_call | solution.py:416
  615.6 16.7 %outer_sum.11 = bf16[1152,1792]{1,0:T(8,128)(2,1)} custom-call(s32[1]{0:T(128)} %constant.172.clone.1.none_ref.scalars_ref, bf16[2208,1152]{1,0:T(8,128)(2,1)} %get-tuple-element.203.left_ref, bf16[2208,1792]{1,0:T(8,128)(2,1)} %get-tuple-element.241.right_ref.refs_0_), custom_call_target="tpu_custom_call" | custom-call | flops 9116319744 | bytes 13000704 | tf_op jit(solution)/shard_map/outer_sum/pallas_call | solution.py:416
  649.9 16.3 %first_back.5 = (bf16[1,368,1152]{2,1,0:T(8,128)(2,1)}, bf16[1,361,1152]{2,1,0:T(8,128)(2,1)}, bf16[6,729,1152]{2,1,0:T(8,128)(2,1)}, f32[8,1152]{1,0:T(8,128)}) custom-call(s32[6]{0:T(128)} %pad_add_fusion.scalars_ref, bf16[2208,1792]{1,0:T(8,128)(2,1)} %get-tuple-element.241.right_ref.refs_0_, ...), custom_call_target="tpu_custom_call", output_to_operand_aliasing={{2}: (8, {})} | custom-call | flops 6077546496 | bytes 54418944 | tf_op jit(solution)/shard_map/first_back/pallas_call | solution.py:416
  676.5 3.5 collective-permute-start.27
  681.6 5.3 constant_dynamic-update-slice_fusion.9
  688.8 11.1 %collective-permute-done.26 = bf16[1,72,1792]{2,1,0:T(8,128)(2,1)S(1)} collective-permute-done((bf16[1,72,1792]{2,1,0:T(8,128)(2,1)S(1)}, bf16[1,72,1792]{2,1,0:T(8,128)(2,1)S(1)}, u32[]{:S(2)}, u32[]{:S(2)}) %collective-permute-start.26) | collective-permute-done | bytes 258080 | tf_op jit(solution)/shard_map/ppermute | solution.py:624
  726.0 4.0 place_cuts.3
  (241 shorter events, 113.7 us)
Async XLA Ops:
  7.2 164.2 %all-gather.3.cloned.1.call-start = ((), (), s32[]{:S(2)}) async-start(), calls=%async_computation.2 | async-start | bytes 14598144 | tf_op jit(solution)/shard_map/all_gather | solution.py:690
  11.5 25.8 %collective-permute-start.2 = (bf16[1,72,1792]{2,1,0:T(8,128)(2,1)S(1)}, bf16[1,72,1792]{2,1,0:T(8,128)(2,1)S(1)}, u32[]{:S(2)}, u32[]{:S(2)}) collective-permute-start(bf16[1,72,1792]{2,1,0:T(8,128)(2,1)S(1)} %constant_dynamic-slice_fusion.10), channel_id=1, source_target_pairs={{0,6},{2,0},{4,2},{6,4},{1,7},{3,1},{5,3},{7,5},{8,14},{10,8},{12,... | collective-permute-start | bytes 774152 | tf_op jit(solution)/shard_map/ppermute | solution.py:624
  16.6 22.0 %collective-permute-start.1 = (bf16[1,72,1792]{2,1,0:T(8,128)(2,1)S(1)}, bf16[1,72,1792]{2,1,0:T(8,128)(2,1)S(1)}, u32[]{:S(2)}, u32[]{:S(2)}) collective-permute-start(bf16[1,72,1792]{2,1,0:T(8,128)(2,1)S(1)} %constant_dynamic-slice_fusion.10), channel_id=1, source_target_pairs={{0,4},{2,6},{4,0},{6,2},{1,5},{3,7},{5,1},{7,3},{8,12},{10,14},{12... | collective-permute-start | bytes 774152 | tf_op jit(solution)/shard_map/ppermute | solution.py:624
  16.6 22.0 %collective-permute-start = (bf16[1,72,1792]{2,1,0:T(8,128)(2,1)S(1)}, bf16[1,72,1792]{2,1,0:T(8,128)(2,1)}, u32[]{:S(2)}, u32[]{:S(2)}) collective-permute-start(bf16[1,72,1792]{2,1,0:T(8,128)(2,1)S(1)} %constant_dynamic-slice_fusion.10), channel_id=1, source_target_pairs={{0,2},{2,4},{4,6},{6,0},{1,3},{3,5},{5,7},{7,1},{8,10},{10,12},{12... | collective-permute-start | bytes 774152 | tf_op jit(solution)/shard_map/ppermute | solution.py:624
  39.3 230.9 %all-gather.5.cloned.1.call-start = ((), (), s32[]{:S(2)}) async-start(), calls=%async_computation.3 | async-start | bytes 10948608 | tf_op jit(solution)/shard_map/all_gather | solution.py:690
  41.1 418.7 %reduce-scatter.3.cloned.1.call-start = ((), (), s32[]{:S(2)}) async-start(), calls=%async_computation.4 | async-start | bytes 10948608 | tf_op jit(solution)/shard_map/reduce_scatter | solution.py:985
  42.2 21.5 %collective-permute-start.3 = (bf16[3,72,1792]{2,1,0:T(8,128)(2,1)S(1)}, bf16[3,72,1792]{2,1,0:T(8,128)(2,1)}, u32[]{:S(2)}, u32[]{:S(2)}) collective-permute-start(bf16[3,72,1792]{2,1,0:T(8,128)(2,1)S(1)} %constant_dynamic-update-slice_fusion.refs_1_), channel_id=1, source_target_pairs={{0,16},{8,24},{16,0},{24,8},{1,17},{9,25},{17,1},{25,9},{2,18},{10... | collective-permute-start | bytes 2322440 | tf_op jit(solution)/shard_map/ppermute | solution.py:619
  44.9 26.6 %collective-permute-start.6 = (bf16[4,72,1792]{2,1,0:T(8,128)(2,1)S(1)}, bf16[4,72,1792]{2,1,0:T(8,128)(2,1)S(1)}, u32[]{:S(2)}, u32[]{:S(2)}) collective-permute-start(bf16[4,72,1792]{2,1,0:T(8,128)(2,1)S(1)} %pad_maximum_fusion), channel_id=1, source_target_pairs={{0,1},{1,0},{2,3},{3,2},{4,5},{5,4},{6,7},{7,6},{8,9},{9,8},{10,11... | collective-permute-start | bytes 3096584 | tf_op jit(solution)/shard_map/ppermute | solution.py:619
  46.5 25.6 %collective-permute-start.4 = (bf16[3,72,1792]{2,1,0:T(8,128)(2,1)S(1)}, bf16[3,72,1792]{2,1,0:T(8,128)(2,1)}, u32[]{:S(2)}, u32[]{:S(2)}) collective-permute-start(bf16[3,72,1792]{2,1,0:T(8,128)(2,1)S(1)} %constant_dynamic-update-slice_fusion.refs_1_), channel_id=1, source_target_pairs={{0,8},{8,0},{16,24},{24,16},{1,9},{9,1},{17,25},{25,17},{2,10},{10... | collective-permute-start | bytes 2322440 | tf_op jit(solution)/shard_map/ppermute | solution.py:619
  71.5 47.9 %collective-permute-start.7 = (bf16[4,72,1792]{2,1,0:T(8,128)(2,1)S(1)}, bf16[4,72,1792]{2,1,0:T(8,128)(2,1)S(1)}, u32[]{:S(2)}, u32[]{:S(2)}) collective-permute-start(bf16[4,72,1792]{2,1,0:T(8,128)(2,1)S(1)} %collective-permute-done.6.refs_0_), channel_id=1, source_target_pairs={{0,16},{8,24},{16,0},{24,8},{1,17},{9,25},{17,1},{25,9},{2,18},{10... | collective-permute-start | bytes 3096584 | tf_op jit(solution)/shard_map/ppermute | solution.py:619
  269.0 373.7 %reduce-scatter.5.cloned.1.call-start = ((), (), s32[]{:S(2)}) async-start(), calls=%async_computation.5 | async-start | bytes 14598144 | tf_op jit(solution)/shard_map/reduce_scatter | solution.py:1110
  306.3 152.9 %collective-permute-start.10 = (bf16[3,729,1152]{2,1,0:T(8,128)(2,1)}, bf16[3,729,1152]{2,1,0:T(8,128)(2,1)}, u32[]{:S(2)}, u32[]{:S(2)}) collective-permute-start(bf16[3,729,1152]{2,1,0:T(8,128)(2,1)} %get-tuple-element.197), channel_id=1, source_target_pairs={{0,1},{1,0},{2,3},{3,2},{4,5},{5,4},{6,7},{7,6},{8,9},{9,8},{10,11... | collective-permute-start | bytes 15116552 | tf_op jit(solution)/shard_map/ppermute | solution.py:619
  459.9 39.5 %collective-permute-start.11 = (bf16[1,72,2304]{2,1,0:T(8,128)(2,1)}, bf16[1,72,2304]{2,1,0:T(8,128)(2,1)S(1)}, u32[]{:S(2)}, u32[]{:S(2)}) collective-permute-start(bf16[1,72,2304]{2,1,0:T(8,128)(2,1)} %bitcast.100), channel_id=1, source_target_pairs={{0,16},{8,24},{16,0},{24,8},{1,17},{9,25},{17,1},{25,9},{2,18},{10... | collective-permute-start | bytes 995336 | tf_op jit(solution)/shard_map/ppermute | solution.py:619
  499.4 17.7 %collective-permute-start.12 = (bf16[1,72,2304]{2,1,0:T(8,128)(2,1)S(1)}, bf16[1,72,2304]{2,1,0:T(8,128)(2,1)S(1)}, u32[]{:S(2)}, u32[]{:S(2)}) collective-permute-start(bf16[1,72,2304]{2,1,0:T(8,128)(2,1)S(1)} %bitcast.102), channel_id=1, source_target_pairs={{0,8},{8,0},{16,24},{24,16},{1,9},{9,1},{17,25},{25,17},{2,10},{10... | collective-permute-start | bytes 995336 | tf_op jit(solution)/shard_map/ppermute | solution.py:619
  499.5 17.7 %collective-permute-start.13 = (bf16[1,72,2304]{2,1,0:T(8,128)(2,1)S(1)}, bf16[1,72,2304]{2,1,0:T(8,128)(2,1)S(1)}, u32[]{:S(2)}, u32[]{:S(2)}) collective-permute-start(bf16[1,72,2304]{2,1,0:T(8,128)(2,1)S(1)} %collective-permute-done.11.refs_1_), channel_id=1, source_target_pairs={{0,8},{8,0},{16,24},{24,16},{1,9},{9,1},{17,25},{25,17},{2,10},{10... | collective-permute-start | bytes 995336 | tf_op jit(solution)/shard_map/ppermute | solution.py:619
  523.4 17.1 %collective-permute-start.14 = (bf16[4,2,72,1792]{3,2,0,1:T(8,128)(2,1)S(1)}, bf16[4,2,72,1792]{3,2,0,1:T(8,128)(2,1)}, u32[]{:S(2)}, u32[]{:S(2)}) collective-permute-start(bf16[4,2,72,1792]{3,2,0,1:T(8,128)(2,1)S(1)} %copy_bitcast_fusion.1), channel_id=1, source_target_pairs={{0,8},{8,0},{16,24},{24,16},{1,9},{9,1},{17,25},{25,17},{2,10},{10... | collective-permute-start | bytes 6193160 | tf_op jit(solution)/shard_map/ppermute | solution.py:619
  560.0 38.0 %collective-permute-start.15 = (bf16[1,368,1152]{2,1,0:T(8,128)(2,1)}, bf16[1,368,1152]{2,1,0:T(8,128)(2,1)}, u32[]{:S(2)}, u32[]{:S(2)}) collective-permute-start(bf16[1,368,1152]{2,1,0:T(8,128)(2,1)} %get-tuple-element.217), channel_id=1, source_target_pairs={{0,1},{1,0},{2,3},{3,2},{4,5},{5,4},{6,7},{7,6},{8,9},{9,8},{10,11... | collective-permute-start | bytes 2543624 | tf_op jit(solution)/shard_map/ppermute | solution.py:619
  560.8 71.6 %collective-permute-start.18 = (bf16[1,361,1152]{2,1,0:T(8,128)(2,1)}, bf16[1,361,1152]{2,1,0:T(8,128)(2,1)}, u32[]{:S(2)}, u32[]{:S(2)}) collective-permute-start(bf16[1,361,1152]{2,1,0:T(8,128)(2,1)} %get-tuple-element.232), channel_id=1, source_target_pairs={{0,1},{1,0},{2,3},{3,2},{4,5},{5,4},{6,7},{7,6},{8,9},{9,8},{10,11... | collective-permute-start | bytes 2495240 | tf_op jit(solution)/shard_map/ppermute | solution.py:619
  562.2 34.4 %collective-permute-start.16 = (bf16[4,72,1792]{2,1,0:T(8,128)(2,1)S(1)}, bf16[4,72,1792]{2,1,0:T(8,128)(2,1)}, u32[]{:S(2)}, u32[]{:S(2)}) collective-permute-start(bf16[4,72,1792]{2,1,0:T(8,128)(2,1)S(1)} %dynamic-slice_bitcast_fusion.1), channel_id=1, source_target_pairs={{0,16},{8,24},{16,0},{24,8},{1,17},{9,25},{17,1},{25,9},{2,18},{10... | collective-permute-start | bytes 3096584 | tf_op jit(solution)/shard_map/ppermute | solution.py:619
  598.1 35.9 %collective-permute-start.17 = (bf16[1,368,1152]{2,1,0:T(8,128)(2,1)}, bf16[1,368,1152]{2,1,0:T(8,128)(2,1)}, u32[]{:S(2)}, u32[]{:S(2)}) collective-permute-start(bf16[1,368,1152]{2,1,0:T(8,128)(2,1)} %get-tuple-element.227), channel_id=1, source_target_pairs={{0,1},{1,0},{2,3},{3,2},{4,5},{5,4},{6,7},{7,6},{8,9},{9,8},{10,11... | collective-permute-start | bytes 2543624 | tf_op jit(solution)/shard_map/ppermute | solution.py:619
  637.4 38.1 %collective-permute-start.24 = (bf16[1,361,1152]{2,1,0:T(8,128)(2,1)}, bf16[1,361,1152]{2,1,0:T(8,128)(2,1)}, u32[]{:S(2)}, u32[]{:S(2)}) collective-permute-start(bf16[1,361,1152]{2,1,0:T(8,128)(2,1)} %get-tuple-element.263), channel_id=1, source_target_pairs={{0,1},{1,0},{2,3},{3,2},{4,5},{5,4},{6,7},{7,6},{8,9},{9,8},{10,11... | collective-permute-start | bytes 2495240 | tf_op jit(solution)/shard_map/ppermute | solution.py:619
  642.8 23.3 %collective-permute-start.21 = (bf16[1,72,1792]{2,1,0:T(8,128)(2,1)S(1)}, bf16[1,72,1792]{2,1,0:T(8,128)(2,1)}, u32[]{:S(2)}, u32[]{:S(2)}) collective-permute-start(bf16[1,72,1792]{2,1,0:T(8,128)(2,1)S(1)} %get-tuple-element.321), channel_id=1, source_target_pairs={{0,2},{2,4},{4,6},{6,0},{1,3},{3,5},{5,7},{7,1},{8,10},{10,12},{12... | collective-permute-start | bytes 774152 | tf_op jit(solution)/shard_map/ppermute | solution.py:624
  644.3 21.9 %collective-permute-start.23 = (bf16[1,72,1792]{2,1,0:T(8,128)(2,1)S(1)}, bf16[1,72,1792]{2,1,0:T(8,128)(2,1)}, u32[]{:S(2)}, u32[]{:S(2)}) collective-permute-start(bf16[1,72,1792]{2,1,0:T(8,128)(2,1)S(1)} %get-tuple-element.322), channel_id=1, source_target_pairs={{0,6},{2,0},{4,2},{6,4},{1,7},{3,1},{5,3},{7,5},{8,14},{10,8},{12,... | collective-permute-start | bytes 774152 | tf_op jit(solution)/shard_map/ppermute | solution.py:624
  646.7 22.9 %collective-permute-start.22 = (bf16[1,72,1792]{2,1,0:T(8,128)(2,1)S(1)}, bf16[1,72,1792]{2,1,0:T(8,128)(2,1)}, u32[]{:S(2)}, u32[]{:S(2)}) collective-permute-start(bf16[1,72,1792]{2,1,0:T(8,128)(2,1)S(1)} %get-tuple-element.323), channel_id=1, source_target_pairs={{0,4},{2,6},{4,0},{6,2},{1,5},{3,7},{5,1},{7,3},{8,12},{10,14},{12... | collective-permute-start | bytes 774152 | tf_op jit(solution)/shard_map/ppermute | solution.py:624
  649.7 24.3 %collective-permute-start.20 = (bf16[4,72,1792]{2,1,0:T(8,128)(2,1)}, bf16[4,72,1792]{2,1,0:T(8,128)(2,1)}, u32[]{:S(2)}, u32[]{:S(2)}) collective-permute-start(bf16[4,72,1792]{2,1,0:T(8,128)(2,1)} %dynamic-slice_bitcast_fusion), channel_id=1, source_target_pairs={{0,16},{8,24},{16,0},{24,8},{1,17},{9,25},{17,1},{25,9},{2,18},{10... | collective-permute-start | bytes 3096584 | tf_op jit(solution)/shard_map/ppermute | solution.py:619
  676.5 12.2 %collective-permute-start.27 = (bf16[1,72,1792]{2,1,0:T(8,128)(2,1)S(1)}, bf16[1,72,1792]{2,1,0:T(8,128)(2,1)S(1)}, u32[]{:S(2)}, u32[]{:S(2)}) collective-permute-start(bf16[1,72,1792]{2,1,0:T(8,128)(2,1)S(1)} %get-tuple-element.319), channel_id=1, source_target_pairs={{0,6},{2,0},{4,2},{6,4},{1,7},{3,1},{5,3},{7,5},{8,14},{10,8},{12,... | collective-permute-start | bytes 774152 | tf_op jit(solution)/shard_map/ppermute | solution.py:624
  680.0 19.8 %collective-permute-start.26 = (bf16[1,72,1792]{2,1,0:T(8,128)(2,1)S(1)}, bf16[1,72,1792]{2,1,0:T(8,128)(2,1)S(1)}, u32[]{:S(2)}, u32[]{:S(2)}) collective-permute-start(bf16[1,72,1792]{2,1,0:T(8,128)(2,1)S(1)} %get-tuple-element.320), channel_id=1, source_target_pairs={{0,4},{2,6},{4,0},{6,2},{1,5},{3,7},{5,1},{7,3},{8,12},{10,14},{12... | collective-permute-start | bytes 774152 | tf_op jit(solution)/shard_map/ppermute | solution.py:624
  680.0 22.2 %collective-permute-start.29 = (bf16[1,368,1152]{2,1,0:T(8,128)(2,1)S(1)}, bf16[1,368,1152]{2,1,0:T(8,128)(2,1)S(1)}, u32[]{:S(2)}, u32[]{:S(2)}) collective-permute-start(bf16[1,368,1152]{2,1,0:T(8,128)(2,1)S(1)} %copy-done.31), channel_id=1, source_target_pairs={{0,1},{1,0},{2,3},{3,2},{4,5},{5,4},{6,7},{7,6},{8,9},{9,8},{10,11... | collective-permute-start | bytes 2543624 | tf_op jit(solution)/shard_map/ppermute | solution.py:619
  686.9 13.1 %collective-permute-start.30 = (bf16[1,72,3072]{2,1,0:T(8,128)(2,1)S(1)}, bf16[1,72,3072]{2,1,0:T(8,128)(2,1)S(1)}, u32[]{:S(2)}, u32[]{:S(2)}) collective-permute-start(bf16[1,72,3072]{2,1,0:T(8,128)(2,1)S(1)} %bitcast.98), channel_id=1, source_target_pairs={{0,16},{8,24},{16,0},{24,8},{1,17},{9,25},{17,1},{25,9},{2,18},{10... | collective-permute-start | bytes 1327112 | tf_op jit(solution)/shard_map/ppermute | solution.py:619
  687.3 46.1 %collective-permute-start.40 = (bf16[1,361,1152]{2,1,0:T(8,128)(2,1)}, bf16[1,361,1152]{2,1,0:T(8,128)(2,1)S(1)}, u32[]{:S(2)}, u32[]{:S(2)}) collective-permute-start(bf16[1,361,1152]{2,1,0:T(8,128)(2,1)} %get-tuple-element.298), channel_id=1, source_target_pairs={{0,1},{1,0},{2,3},{3,2},{4,5},{5,4},{6,7},{7,6},{8,9},{9,8},{10,11... | collective-permute-start | bytes 2495240 | tf_op jit(solution)/shard_map/ppermute | solution.py:619
  706.3 12.9 %collective-permute-start.34 = (f32[112,128]{1,0:T(8,128)S(1)}, f32[112,128]{1,0:T(8,128)S(1)}, u32[]{:S(2)}, u32[]{:S(2)}) collective-permute-start(f32[112,128]{1,0:T(8,128)S(1)} %pad_bitcast_fusion), channel_id=1, source_target_pairs={{0,8},{8,0},{16,24},{24,16},{1,9},{9,1},{17,25},{25,17},{2,10},{10... | collective-permute-start | bytes 172040 | tf_op jit(solution)/shard_map/ppermute | solution.py:757
  719.7 13.7 %collective-permute-start.39 = (f32[112,128]{1,0:T(8,128)S(1)}, f32[112,128]{1,0:T(8,128)S(1)}, u32[]{:S(2)}, u32[]{:S(2)}) collective-permute-start(f32[112,128]{1,0:T(8,128)S(1)} %add_add_fusion.1), channel_id=1, source_target_pairs={{0,6},{2,4},{4,2},{6,0},{1,7},{3,5},{5,3},{7,1},{8,14},{10,12},{12... | collective-permute-start | bytes 172040 | tf_op jit(solution)/shard_map/ppermute | solution.py:757
  (49 other events, 596.6 us)
Sparse Core Ops, SparseCore 0:
  39.5 119.2 all-gather.2
  162.2 85.3 all-gather.4
  269.1 170.0 reduce-scatter.2
  459.4 181.2 reduce-scatter.4

commit v5 on v4

--- a/solution.py
+++ b/solution.py
@@ -1252,6 +1252,8 @@
     in_parts.append(trade_halves(input_grad))
     lower = in_parts[-1][1]
     out_whole = lay(out_whole, out_parts, 0)
+    for slot in range(last - 1):
+        input_whole = lay_halves(input_whole, in_parts[slot], slot)
     up_found = join_on({0: up_share[None]}, far_bits)
     near_total = add_low(
         sum_lines(near[0]), *(swap(term, "tensor", rank) for rank, term in zip(ranks[1:], far))
@@ -1282,7 +1284,7 @@
         down_grads,
     )
     in_parts[-1].append(lower)
-    for slot in range(last):
+    for slot in range(max(last - 1, 0), last):
         input_whole = lay_halves(input_whole, in_parts[slot], slot)
     near_found = among_replicas(near_total)
     up_grads, o_grads = place_cuts(

time: 751 us -> 750 us (level)
  transfers between devices with their start and end apart: 48 -> 48, of which waited for: 11 -> 13; matrix products, arithmetic and copies ran while one was open for 12% -> 12% of each run, Pallas kernels for 73% -> 73%
where the time goes in v5:
time: 750 us; the launch traced here: 745 us
  Pallas kernels  543 us (72%)
  waiting for transfers between devices  50.7 us (7%)
  starting transfers between devices  41.2 us (5%)
  local copies, waits for them, and re-layouts  39.2 us (5%)
  matrix products  31.4 us (4%)
  other arithmetic  25 us (3%)
  between operations  14.7 us (2%)
    pallas_call x26, Pallas kernels, call(): pl.pallas_call(kernel, grid_spec=pltpu.PrefetchScalarGridSpec(num_scalar_...  543 us
    ppermute x28, waiting for transfers between devices, swap(): lax.ppermute(array, axis, [(rank, rank ^ bits) for rank in range(size)])  36.5 us
    dot_general x2, matrix products, matmul(): return jnp.dot(first_op, second_op, preferred_element_type=jnp.float32)  31.4 us
    ppermute x28, starting transfers between devices, swap(): lax.ppermute(array, axis, [(rank, rank ^ bits) for rank in range(size)])  17.2 us
    ppermute x9, starting transfers between devices, turn(): lax.ppermute(array, axis, [(rank, (rank + steps) % size) for rank in rang...  16 us
  transfers between devices with their start and end apart: 48, of which 13 were waited for; matrix products, arithmetic and copies ran while one was open for 12% of the time, Pallas kernels for 73%

profile of v5, /device:TPU:0, one launch (start us, length us, event | category | flops | bytes accessed | tf_op | source)
XLA Modules:
  0.0 745.4 jit_solution(6755105319560320067)
XLA Ops:
  11.5 5.1 collective-permute-start.2
  25.5 11.4 %first_norm.1 = (bf16[2208,1152]{1,0:T(8,128)(2,1)}, bf16[2208,1152]{1,0:T(8,128)(2,1)}, f32[8,1152]{1,0:T(8,128)}) custom-call(s32[6]{0:T(128)} %pad_add_fusion.scalars_ref, bf16[6,729,1152]{2,1,0:T(8,128)(2,1)} %refs_4_.7, bf16[6,729,1152]{2,1,0:T(8,128)(2,1)} %cot_ref.1, f32[1,1152]{1,0:T(1,128)} %reshape.129.gain_ref.refs_6_, f32[1,1152]{1,0:T(1,128)} %reshape.130.shift_ref), custom_call_target="tpu_custom_call" | custom-call | bytes 20164608 | tf_op jit(solution)/shard_map/first_norm/pallas_call | solution.py:416
  46.5 17.3 %collective-permute-done.3.refs_2_ = bf16[3,72,1792]{2,1,0:T(8,128)(2,1)} collective-permute-done((bf16[3,72,1792]{2,1,0:T(8,128)(2,1)S(1)}, bf16[3,72,1792]{2,1,0:T(8,128)(2,1)}, u32[]{:S(2)}, u32[]{:S(2)}) %collective-permute-start.3) | collective-permute-done | bytes 774176 | tf_op jit(solution)/shard_map/ppermute | solution.py:619
  64.5 7.0 collective-permute-done.6.refs_0_
  72.0 5.1 place.3
  77.1 15.7 %multiply_convert_fusion.1.qvk_ref = bf16[2208,1792]{1,0:T(8,128)(2,1)} fusion(bf16[2208,1152]{1,0:T(8,128)(2,1)} %get-tuple-element.201.left_ref, bf16[1152,1792]{1,0:T(8,128)(2,1)} %bitcast.82, f32[1792]{0:T(1024)S(1)} %fusion.7, f32[1792]{0:T(1024)S(1)} %select_maximum_fusion.1), kind=kOutput, calls=%fused_computation.1 | convolution fusion | flops 9128189952 | bytes 17143808 | tf_op jit(solution)/shard_map/dot_general | solution.py:19
  92.8 26.7 %attention.2 = (bf16[2208,768]{1,0:T(8,128)(2,1)}, bf16[24,736,736]{2,1,0:T(8,128)(2,1)}) custom-call(s32[1]{0:T(128)} %constant.172.clone.1.none_ref.scalars_ref, bf16[2208,1792]{1,0:T(8,128)(2,1)} %multiply_convert_fusion.1.qvk_ref), custom_call_target="tpu_custom_call" | custom-call | flops 13312720896 | bytes 7913472 | tf_op jit(solution)/shard_map/attention/pallas_call | solution.py:416
  123.9 5.1 place.4
  128.9 15.7 %multiply_convert_fusion.qvk_ref = bf16[2208,1792]{1,0:T(8,128)(2,1)} fusion(bf16[2208,1152]{1,0:T(8,128)(2,1)} %get-tuple-element.201.left_ref, bf16[1152,1792]{1,0:T(8,128)(2,1)} %bitcast.86, f32[1792]{0:T(1024)S(1)} %select_maximum_fusion, f32[1792]{0:T(1024)S(1)} %fusion.7), kind=kOutput, calls=%fused_computation | convolution fusion | flops 9128189952 | bytes 17143808 | tf_op jit(solution)/shard_map/dot_general | solution.py:19
  144.7 26.7 %attention.3 = (bf16[2208,768]{1,0:T(8,128)(2,1)}, bf16[24,736,736]{2,1,0:T(8,128)(2,1)}) custom-call(s32[1]{0:T(128)} %constant.172.clone.1.none_ref.scalars_ref, bf16[2208,1792]{1,0:T(8,128)(2,1)} %multiply_convert_fusion.qvk_ref), custom_call_target="tpu_custom_call" | custom-call | flops 13312720896 | bytes 7913472 | tf_op jit(solution)/shard_map/attention/pallas_call | solution.py:416
  171.4 17.7 %middle_norm.1 = (f32[2208,1152]{1,0:T(8,128)}, bf16[2208,1152]{1,0:T(8,128)(2,1)}) custom-call(s32[6]{0:T(128)} %pad_add_fusion.scalars_ref, bf16[2208,768]{1,0:T(8,128)(2,1)} %get-tuple-element.179.refs_0_.right_ref.mixed_ref, bf16[2208,768]{1,0:T(8,128)(2,1)} %get-tuple-element.178.refs_1_.right_ref.mixed_ref, ...), custom_call_target="tpu_custom_call" | custom-call | flops 7813988352 | bytes 45186048 | tf_op jit(solution)/shard_map/middle_norm/pallas_call | solution.py:416
  189.1 48.6 %hidden.1 = (bf16[2208,4608]{1,0:T(8,128)(2,1)}, bf16[2208,4608]{1,0:T(8,128)(2,1)}) custom-call(s32[6]{0:T(128)} %pad_add_fusion.scalars_ref, bf16[2208,1152]{1,0:T(8,128)(2,1)} %get-tuple-element.181.second_ref.left_ref, bf16[2304,3072]{1,0:T(8,128)(2,1)} %all-gather.3.cloned.1.call-done.refs_2_.refs_3_.weight_ref.refs_7_.refs_8_, f32[1,4608]{1,0:T(1,128)} %bitcast.103), custom_call_target="tpu_custom_call" | custom-call | flops 23441965056 | bytes 19261440 | tf_op jit(solution)/shard_map/hidden/pallas_call | solution.py:416
  237.7 31.3 %outer_sum.6 = bf16[2304,2304]{1,0:T(8,128)(2,1)} custom-call(s32[1]{0:T(128)} %constant.172.clone.1.none_ref.scalars_ref, bf16[2208,1152]{1,0:T(8,128)(2,1)} %get-tuple-element.188.left_ref.grad_ref.refs_5_, bf16[2208,4608]{1,0:T(8,128)(2,1)} %get-tuple-element.184.right_ref.refs_0_.refs_1_), custom_call_target="tpu_custom_call" | custom-call | flops 23441965056 | bytes 25436160 | tf_op jit(solution)/shard_map/outer_sum/pallas_call | solution.py:416
  270.3 36.0 %output.1 = (bf16[3,729,1152]{2,1,0:T(8,128)(2,1)}, bf16[6,729,1152]{2,1,0:T(8,128)(2,1)}) custom-call(s32[6]{0:T(128)} %pad_add_fusion.scalars_ref, bf16[2208,4608]{1,0:T(8,128)(2,1)} %get-tuple-element.184.right_ref.refs_0_.refs_1_, bf16[2208,4608]{1,0:T(8,128)(2,1)} %get-tuple-element.184.right_ref.refs_0_.refs_1_, ...), custom_call_target="tpu_custom_call" | custom-call | flops 23441965056 | bytes 72110592 | tf_op jit(solution)/shard_map/output/pallas_call | solution.py:416
  307.8 37.5 %hidden_back.1 = (bf16[2208,4608]{1,0:T(8,128)(2,1)}, f32[8,4608]{1,0:T(8,128)}) custom-call(s32[6]{0:T(128)} %pad_add_fusion.scalars_ref, bf16[2208,1152]{1,0:T(8,128)(2,1)} %get-tuple-element.188.left_ref.grad_ref.refs_5_, bf16[2304,2304]{1,0:T(8,128)(2,1)} %all-gather.5.cloned.1.call-done.refs_2_.refs_3_.weight_ref, ...), custom_call_target="tpu_custom_call" | custom-call | flops 23441965056 | bytes 36052992 | tf_op jit(solution)/shard_map/hidden_back/pallas_call | solution.py:416
  345.3 31.5 %outer_sum.7.refs_0_ = bf16[2304,3072]{1,0:T(8,128)(2,1)} custom-call(s32[1]{0:T(128)} %constant.172.clone.1.none_ref.scalars_ref, bf16[2208,1152]{1,0:T(8,128)(2,1)} %get-tuple-element.181.second_ref.left_ref, bf16[2208,4608]{1,0:T(8,128)(2,1)} %get-tuple-element.191.right_ref.refs_0_.refs_1_), custom_call_target="tpu_custom_call" | custom-call | flops 23441965056 | bytes 25436160 | tf_op jit(solution)/shard_map/outer_sum/pallas_call | solution.py:416
  376.8 62.7 %middle_back.1 = (f32[2208,1152]{1,0:T(8,128)}, bf16[2208,1152]{1,0:T(8,128)(2,1)}, f32[8,1152]{1,0:T(8,128)}, bf16[2208,768]{1,0:T(8,128)(2,1)}, bf16[2208,768]{1,0:T(8,128)(2,1)}) custom-call(s32[6]{0:T(128)} %pad_add_fusion.scalars_ref, bf16[2208,4608]{1,0:T(8,128)(2,1)} %get-tuple-element.191.right_ref.refs_0_.refs_1_, ...), custom_call_target="tpu_custom_call" | custom-call | flops 31255953408 | bytes 112587264 | tf_op jit(solution)/shard_map/middle_back/pallas_call | solution.py:416
  439.5 9.9 %outer_sum.8.refs_0_ = bf16[2304,3072]{1,0:T(8,128)(2,1)} custom-call(s32[6]{0:T(128)} %pad_add_fusion.scalars_ref, bf16[2208,1152]{1,0:T(8,128)(2,1)} %get-tuple-element.192.left_ref, bf16[2208,768]{1,0:T(8,128)(2,1)} %get-tuple-element.179.refs_0_.right_ref.mixed_ref, bf16[2304,3072]{1,0:T(8,128)(2,1)} %outer_sum.7.refs_0_), custom_call_target="tpu_custom_call", output_to_operand_aliasing={{}: (3, {})} | custom-call | flops 3906994176 | bytes 22634496 | tf_op jit(solution)/shard_map/outer_sum/pallas_call | solution.py:416
  449.4 9.8 %outer_sum.9 = bf16[2304,3072]{1,0:T(8,128)(2,1)} custom-call(s32[6]{0:T(128)} %pad_add_fusion.scalars_ref, bf16[2208,1152]{1,0:T(8,128)(2,1)} %get-tuple-element.192.left_ref, bf16[2208,768]{1,0:T(8,128)(2,1)} %get-tuple-element.178.refs_1_.right_ref.mixed_ref, bf16[2304,3072]{1,0:T(8,128)(2,1)} %outer_sum.8.refs_0_), custom_call_target="tpu_custom_call", output_to_operand_aliasing={{}: (3, {})} | custom-call | flops 3906994176 | bytes 22634496 | tf_op jit(solution)/shard_map/outer_sum/pallas_call | solution.py:416
  461.0 38.2 %attention_back.4 = (bf16[2208,1792]{1,0:T(8,128)(2,1)}, f32[3,8,1792]{2,1,0:T(8,128)}) custom-call(s32[1]{0:T(128)} %constant.172.clone.1.none_ref.scalars_ref, bf16[2208,1792]{1,0:T(8,128)(2,1)} %multiply_convert_fusion.qvk_ref, bf16[2208,768]{1,0:T(8,128)(2,1)} %get-tuple-element.178.refs_1_.right_ref.mixed_ref, ...), custom_call_target="tpu_custom_call" | custom-call | flops 26625441792 | bytes 40697856 | tf_op jit(solution)/shard_map/attention_back/pallas_call | solution.py:416
  499.9 17.1 %outer_sum.10 = bf16[1152,1792]{1,0:T(8,128)(2,1)} custom-call(s32[1]{0:T(128)} %constant.172.clone.1.none_ref.scalars_ref, bf16[2208,1152]{1,0:T(8,128)(2,1)} %get-tuple-element.201.left_ref, bf16[2208,1792]{1,0:T(8,128)(2,1)} %get-tuple-element.202.right_ref.refs_1_), custom_call_target="tpu_custom_call" | custom-call | flops 9116319744 | bytes 13000704 | tf_op jit(solution)/shard_map/outer_sum/pallas_call | solution.py:416
  523.4 16.9 %attention_back.5 = (bf16[2208,1792]{1,0:T(8,128)(2,1)}, f32[1,8,1792]{2,1,0:T(8,128)}) custom-call(s32[1]{0:T(128)} %constant.172.clone.1.none_ref.scalars_ref, bf16[2208,1792]{1,0:T(8,128)(2,1)} %multiply_convert_fusion.1.qvk_ref, bf16[2208,768]{1,0:T(8,128)(2,1)} %get-tuple-element.179.refs_0_.right_ref.mixed_ref, ...), custom_call_target="tpu_custom_call" | custom-call | flops 8875147264 | bytes 40697856 | tf_op jit(solution)/shard_map/attention_back/pallas_call | solution.py:416
  543.1 16.8 %first_back.3 = (bf16[1,368,1152]{2,1,0:T(8,128)(2,1)}, bf16[1,361,1152]{2,1,0:T(8,128)(2,1)}, bf16[6,729,1152]{2,1,0:T(8,128)(2,1)}, f32[8,1152]{1,0:T(8,128)}) custom-call(s32[6]{0:T(128)} %pad_add_fusion.scalars_ref, bf16[2208,1792]{1,0:T(8,128)(2,1)} %get-tuple-element.211.refs_0_, bf16[2208,1792]{1,0:T(8,128)(2,1)} %get-tuple-element.202.right_ref.refs_1_, ...), custom_call_target="tpu_custom_call" | custom-call | flops 6077546496 | bytes 44341248 | tf_op jit(solution)/shard_map/first_back/pallas_call | solution.py:416
  562.8 17.2 %attention_back.6 = (bf16[2208,1792]{1,0:T(8,128)(2,1)}, f32[1,8,1792]{2,1,0:T(8,128)}) custom-call(s32[1]{0:T(128)} %constant.172.clone.1.none_ref.scalars_ref, bf16[2208,1792]{1,0:T(8,128)(2,1)} %multiply_convert_fusion.1.qvk_ref, bf16[2208,768]{1,0:T(8,128)(2,1)} %get-tuple-element.179.refs_0_.right_ref.mixed_ref, ...), custom_call_target="tpu_custom_call", output_to_operand_aliasing={{0}: (5, {})} | custom-call | flops 8875147264 | bytes 48611328 | tf_op jit(solution)/shard_map/attention_back/pallas_call | solution.py:416
  580.0 16.4 %first_back.4 = (bf16[1,368,1152]{2,1,0:T(8,128)(2,1)}, bf16[1,361,1152]{2,1,0:T(8,128)(2,1)}, bf16[6,729,1152]{2,1,0:T(8,128)(2,1)}, f32[8,1152]{1,0:T(8,128)}) custom-call(s32[6]{0:T(128)} %pad_add_fusion.scalars_ref, bf16[2208,1792]{1,0:T(8,128)(2,1)} %get-tuple-element.218.refs_0_, ...), custom_call_target="tpu_custom_call", output_to_operand_aliasing={{2}: (8, {})} | custom-call | flops 6077546496 | bytes 54418944 | tf_op jit(solution)/shard_map/first_back/pallas_call | solution.py:416
  598.6 17.0 %attention_back.7 = (bf16[2208,1792]{1,0:T(8,128)(2,1)}, f32[1,8,1792]{2,1,0:T(8,128)}) custom-call(s32[1]{0:T(128)} %constant.172.clone.1.none_ref.scalars_ref, bf16[2208,1792]{1,0:T(8,128)(2,1)} %multiply_convert_fusion.1.qvk_ref, bf16[2208,768]{1,0:T(8,128)(2,1)} %get-tuple-element.179.refs_0_.right_ref.mixed_ref, ...), custom_call_target="tpu_custom_call", output_to_operand_aliasing={{0}: (5, {})} | custom-call | flops 8875147264 | bytes 48611328 | tf_op jit(solution)/shard_map/attention_back/pallas_call | solution.py:416
  615.6 16.7 %outer_sum.11 = bf16[1152,1792]{1,0:T(8,128)(2,1)} custom-call(s32[1]{0:T(128)} %constant.172.clone.1.none_ref.scalars_ref, bf16[2208,1152]{1,0:T(8,128)(2,1)} %get-tuple-element.201.left_ref, bf16[2208,1792]{1,0:T(8,128)(2,1)} %get-tuple-element.239.right_ref.refs_0_), custom_call_target="tpu_custom_call" | custom-call | flops 9116319744 | bytes 13000704 | tf_op jit(solution)/shard_map/outer_sum/pallas_call | solution.py:416
  649.9 16.3 %first_back.5 = (bf16[1,368,1152]{2,1,0:T(8,128)(2,1)}, bf16[1,361,1152]{2,1,0:T(8,128)(2,1)}, bf16[6,729,1152]{2,1,0:T(8,128)(2,1)}, f32[8,1152]{1,0:T(8,128)}) custom-call(s32[6]{0:T(128)} %pad_add_fusion.scalars_ref, bf16[2208,1792]{1,0:T(8,128)(2,1)} %get-tuple-element.239.right_ref.refs_0_, ...), custom_call_target="tpu_custom_call", output_to_operand_aliasing={{2}: (8, {})} | custom-call | flops 6077546496 | bytes 54418944 | tf_op jit(solution)/shard_map/first_back/pallas_call | solution.py:416
  681.7 5.1 constant_dynamic-update-slice_fusion.9
  692.5 7.5 collective-permute-done.26
  712.6 4.0 collective-permute-done.32.refs_2_
  725.5 4.0 place_cuts.3
  (241 shorter events, 116.8 us)
Async XLA Ops:
  7.2 164.2 %all-gather.3.cloned.1.call-start = ((), (), s32[]{:S(2)}) async-start(), calls=%async_computation.2 | async-start | bytes 14598144 | tf_op jit(solution)/shard_map/all_gather | solution.py:690
  11.5 25.8 %collective-permute-start.2 = (bf16[1,72,1792]{2,1,0:T(8,128)(2,1)S(1)}, bf16[1,72,1792]{2,1,0:T(8,128)(2,1)S(1)}, u32[]{:S(2)}, u32[]{:S(2)}) collective-permute-start(bf16[1,72,1792]{2,1,0:T(8,128)(2,1)S(1)} %constant_dynamic-slice_fusion.10), channel_id=1, source_target_pairs={{0,6},{2,0},{4,2},{6,4},{1,7},{3,1},{5,3},{7,5},{8,14},{10,8},{12,... | collective-permute-start | bytes 774152 | tf_op jit(solution)/shard_map/ppermute | solution.py:624
  16.6 22.0 %collective-permute-start.1 = (bf16[1,72,1792]{2,1,0:T(8,128)(2,1)S(1)}, bf16[1,72,1792]{2,1,0:T(8,128)(2,1)S(1)}, u32[]{:S(2)}, u32[]{:S(2)}) collective-permute-start(bf16[1,72,1792]{2,1,0:T(8,128)(2,1)S(1)} %constant_dynamic-slice_fusion.10), channel_id=1, source_target_pairs={{0,4},{2,6},{4,0},{6,2},{1,5},{3,7},{5,1},{7,3},{8,12},{10,14},{12... | collective-permute-start | bytes 774152 | tf_op jit(solution)/shard_map/ppermute | solution.py:624
  16.6 22.0 %collective-permute-start = (bf16[1,72,1792]{2,1,0:T(8,128)(2,1)S(1)}, bf16[1,72,1792]{2,1,0:T(8,128)(2,1)}, u32[]{:S(2)}, u32[]{:S(2)}) collective-permute-start(bf16[1,72,1792]{2,1,0:T(8,128)(2,1)S(1)} %constant_dynamic-slice_fusion.10), channel_id=1, source_target_pairs={{0,2},{2,4},{4,6},{6,0},{1,3},{3,5},{5,7},{7,1},{8,10},{10,12},{12... | collective-permute-start | bytes 774152 | tf_op jit(solution)/shard_map/ppermute | solution.py:624
  39.3 230.9 %all-gather.5.cloned.1.call-start = ((), (), s32[]{:S(2)}) async-start(), calls=%async_computation.3 | async-start | bytes 10948608 | tf_op jit(solution)/shard_map/all_gather | solution.py:690
  41.1 418.7 %reduce-scatter.3.cloned.1.call-start = ((), (), s32[]{:S(2)}) async-start(), calls=%async_computation.4 | async-start | bytes 10948608 | tf_op jit(solution)/shard_map/reduce_scatter | solution.py:985
  42.2 21.5 %collective-permute-start.3 = (bf16[3,72,1792]{2,1,0:T(8,128)(2,1)S(1)}, bf16[3,72,1792]{2,1,0:T(8,128)(2,1)}, u32[]{:S(2)}, u32[]{:S(2)}) collective-permute-start(bf16[3,72,1792]{2,1,0:T(8,128)(2,1)S(1)} %constant_dynamic-update-slice_fusion.refs_1_), channel_id=1, source_target_pairs={{0,16},{8,24},{16,0},{24,8},{1,17},{9,25},{17,1},{25,9},{2,18},{10... | collective-permute-start | bytes 2322440 | tf_op jit(solution)/shard_map/ppermute | solution.py:619
  44.9 26.6 %collective-permute-start.6 = (bf16[4,72,1792]{2,1,0:T(8,128)(2,1)S(1)}, bf16[4,72,1792]{2,1,0:T(8,128)(2,1)S(1)}, u32[]{:S(2)}, u32[]{:S(2)}) collective-permute-start(bf16[4,72,1792]{2,1,0:T(8,128)(2,1)S(1)} %pad_maximum_fusion), channel_id=1, source_target_pairs={{0,1},{1,0},{2,3},{3,2},{4,5},{5,4},{6,7},{7,6},{8,9},{9,8},{10,11... | collective-permute-start | bytes 3096584 | tf_op jit(solution)/shard_map/ppermute | solution.py:619
  46.5 25.6 %collective-permute-start.4 = (bf16[3,72,1792]{2,1,0:T(8,128)(2,1)S(1)}, bf16[3,72,1792]{2,1,0:T(8,128)(2,1)}, u32[]{:S(2)}, u32[]{:S(2)}) collective-permute-start(bf16[3,72,1792]{2,1,0:T(8,128)(2,1)S(1)} %constant_dynamic-update-slice_fusion.refs_1_), channel_id=1, source_target_pairs={{0,8},{8,0},{16,24},{24,16},{1,9},{9,1},{17,25},{25,17},{2,10},{10... | collective-permute-start | bytes 2322440 | tf_op jit(solution)/shard_map/ppermute | solution.py:619
  71.5 47.9 %collective-permute-start.7 = (bf16[4,72,1792]{2,1,0:T(8,128)(2,1)S(1)}, bf16[4,72,1792]{2,1,0:T(8,128)(2,1)S(1)}, u32[]{:S(2)}, u32[]{:S(2)}) collective-permute-start(bf16[4,72,1792]{2,1,0:T(8,128)(2,1)S(1)} %collective-permute-done.6.refs_0_), channel_id=1, source_target_pairs={{0,16},{8,24},{16,0},{24,8},{1,17},{9,25},{17,1},{25,9},{2,18},{10... | collective-permute-start | bytes 3096584 | tf_op jit(solution)/shard_map/ppermute | solution.py:619
  269.0 373.6 %reduce-scatter.5.cloned.1.call-start = ((), (), s32[]{:S(2)}) async-start(), calls=%async_computation.5 | async-start | bytes 14598144 | tf_op jit(solution)/shard_map/reduce_scatter | solution.py:1110
  306.3 152.9 %collective-permute-start.10 = (bf16[3,729,1152]{2,1,0:T(8,128)(2,1)}, bf16[3,729,1152]{2,1,0:T(8,128)(2,1)}, u32[]{:S(2)}, u32[]{:S(2)}) collective-permute-start(bf16[3,729,1152]{2,1,0:T(8,128)(2,1)} %get-tuple-element.195), channel_id=1, source_target_pairs={{0,1},{1,0},{2,3},{3,2},{4,5},{5,4},{6,7},{7,6},{8,9},{9,8},{10,11... | collective-permute-start | bytes 15116552 | tf_op jit(solution)/shard_map/ppermute | solution.py:619
  459.8 39.4 %collective-permute-start.11 = (bf16[1,72,2304]{2,1,0:T(8,128)(2,1)}, bf16[1,72,2304]{2,1,0:T(8,128)(2,1)S(1)}, u32[]{:S(2)}, u32[]{:S(2)}) collective-permute-start(bf16[1,72,2304]{2,1,0:T(8,128)(2,1)} %bitcast.100), channel_id=1, source_target_pairs={{0,16},{8,24},{16,0},{24,8},{1,17},{9,25},{17,1},{25,9},{2,18},{10... | collective-permute-start | bytes 995336 | tf_op jit(solution)/shard_map/ppermute | solution.py:619
  499.3 17.7 %collective-permute-start.12 = (bf16[1,72,2304]{2,1,0:T(8,128)(2,1)S(1)}, bf16[1,72,2304]{2,1,0:T(8,128)(2,1)S(1)}, u32[]{:S(2)}, u32[]{:S(2)}) collective-permute-start(bf16[1,72,2304]{2,1,0:T(8,128)(2,1)S(1)} %bitcast.102), channel_id=1, source_target_pairs={{0,8},{8,0},{16,24},{24,16},{1,9},{9,1},{17,25},{25,17},{2,10},{10... | collective-permute-start | bytes 995336 | tf_op jit(solution)/shard_map/ppermute | solution.py:619
  499.4 17.7 %collective-permute-start.13 = (bf16[1,72,2304]{2,1,0:T(8,128)(2,1)S(1)}, bf16[1,72,2304]{2,1,0:T(8,128)(2,1)S(1)}, u32[]{:S(2)}, u32[]{:S(2)}) collective-permute-start(bf16[1,72,2304]{2,1,0:T(8,128)(2,1)S(1)} %collective-permute-done.11.refs_1_), channel_id=1, source_target_pairs={{0,8},{8,0},{16,24},{24,16},{1,9},{9,1},{17,25},{25,17},{2,10},{10... | collective-permute-start | bytes 995336 | tf_op jit(solution)/shard_map/ppermute | solution.py:619
  523.3 17.1 %collective-permute-start.14 = (bf16[4,2,72,1792]{3,2,0,1:T(8,128)(2,1)S(1)}, bf16[4,2,72,1792]{3,2,0,1:T(8,128)(2,1)}, u32[]{:S(2)}, u32[]{:S(2)}) collective-permute-start(bf16[4,2,72,1792]{3,2,0,1:T(8,128)(2,1)S(1)} %copy_bitcast_fusion.1), channel_id=1, source_target_pairs={{0,8},{8,0},{16,24},{24,16},{1,9},{9,1},{17,25},{25,17},{2,10},{10... | collective-permute-start | bytes 6193160 | tf_op jit(solution)/shard_map/ppermute | solution.py:619
  559.9 38.1 %collective-permute-start.15 = (bf16[1,368,1152]{2,1,0:T(8,128)(2,1)}, bf16[1,368,1152]{2,1,0:T(8,128)(2,1)}, u32[]{:S(2)}, u32[]{:S(2)}) collective-permute-start(bf16[1,368,1152]{2,1,0:T(8,128)(2,1)} %get-tuple-element.215), channel_id=1, source_target_pairs={{0,1},{1,0},{2,3},{3,2},{4,5},{5,4},{6,7},{7,6},{8,9},{9,8},{10,11... | collective-permute-start | bytes 2543624 | tf_op jit(solution)/shard_map/ppermute | solution.py:619
  560.9 71.5 %collective-permute-start.18 = (bf16[1,361,1152]{2,1,0:T(8,128)(2,1)}, bf16[1,361,1152]{2,1,0:T(8,128)(2,1)}, u32[]{:S(2)}, u32[]{:S(2)}) collective-permute-start(bf16[1,361,1152]{2,1,0:T(8,128)(2,1)} %get-tuple-element.230), channel_id=1, source_target_pairs={{0,1},{1,0},{2,3},{3,2},{4,5},{5,4},{6,7},{7,6},{8,9},{9,8},{10,11... | collective-permute-start | bytes 2495240 | tf_op jit(solution)/shard_map/ppermute | solution.py:619
  562.1 34.4 %collective-permute-start.16 = (bf16[4,72,1792]{2,1,0:T(8,128)(2,1)S(1)}, bf16[4,72,1792]{2,1,0:T(8,128)(2,1)}, u32[]{:S(2)}, u32[]{:S(2)}) collective-permute-start(bf16[4,72,1792]{2,1,0:T(8,128)(2,1)S(1)} %dynamic-slice_bitcast_fusion.1), channel_id=1, source_target_pairs={{0,16},{8,24},{16,0},{24,8},{1,17},{9,25},{17,1},{25,9},{2,18},{10... | collective-permute-start | bytes 3096584 | tf_op jit(solution)/shard_map/ppermute | solution.py:619
  598.0 35.9 %collective-permute-start.17 = (bf16[1,368,1152]{2,1,0:T(8,128)(2,1)}, bf16[1,368,1152]{2,1,0:T(8,128)(2,1)}, u32[]{:S(2)}, u32[]{:S(2)}) collective-permute-start(bf16[1,368,1152]{2,1,0:T(8,128)(2,1)} %get-tuple-element.225), channel_id=1, source_target_pairs={{0,1},{1,0},{2,3},{3,2},{4,5},{5,4},{6,7},{7,6},{8,9},{9,8},{10,11... | collective-permute-start | bytes 2543624 | tf_op jit(solution)/shard_map/ppermute | solution.py:619
  637.4 38.2 %collective-permute-start.24 = (bf16[1,361,1152]{2,1,0:T(8,128)(2,1)}, bf16[1,361,1152]{2,1,0:T(8,128)(2,1)}, u32[]{:S(2)}, u32[]{:S(2)}) collective-permute-start(bf16[1,361,1152]{2,1,0:T(8,128)(2,1)} %get-tuple-element.261), channel_id=1, source_target_pairs={{0,1},{1,0},{2,3},{3,2},{4,5},{5,4},{6,7},{7,6},{8,9},{9,8},{10,11... | collective-permute-start | bytes 2495240 | tf_op jit(solution)/shard_map/ppermute | solution.py:619
  642.7 23.4 %collective-permute-start.21 = (bf16[1,72,1792]{2,1,0:T(8,128)(2,1)S(1)}, bf16[1,72,1792]{2,1,0:T(8,128)(2,1)}, u32[]{:S(2)}, u32[]{:S(2)}) collective-permute-start(bf16[1,72,1792]{2,1,0:T(8,128)(2,1)S(1)} %get-tuple-element.317), channel_id=1, source_target_pairs={{0,2},{2,4},{4,6},{6,0},{1,3},{3,5},{5,7},{7,1},{8,10},{10,12},{12... | collective-permute-start | bytes 774152 | tf_op jit(solution)/shard_map/ppermute | solution.py:624
  644.3 21.9 %collective-permute-start.23 = (bf16[1,72,1792]{2,1,0:T(8,128)(2,1)S(1)}, bf16[1,72,1792]{2,1,0:T(8,128)(2,1)}, u32[]{:S(2)}, u32[]{:S(2)}) collective-permute-start(bf16[1,72,1792]{2,1,0:T(8,128)(2,1)S(1)} %get-tuple-element.318), channel_id=1, source_target_pairs={{0,6},{2,0},{4,2},{6,4},{1,7},{3,1},{5,3},{7,5},{8,14},{10,8},{12,... | collective-permute-start | bytes 774152 | tf_op jit(solution)/shard_map/ppermute | solution.py:624
  646.6 22.9 %collective-permute-start.22 = (bf16[1,72,1792]{2,1,0:T(8,128)(2,1)S(1)}, bf16[1,72,1792]{2,1,0:T(8,128)(2,1)}, u32[]{:S(2)}, u32[]{:S(2)}) collective-permute-start(bf16[1,72,1792]{2,1,0:T(8,128)(2,1)S(1)} %get-tuple-element.319), channel_id=1, source_target_pairs={{0,4},{2,6},{4,0},{6,2},{1,5},{3,7},{5,1},{7,3},{8,12},{10,14},{12... | collective-permute-start | bytes 774152 | tf_op jit(solution)/shard_map/ppermute | solution.py:624
  649.8 24.3 %collective-permute-start.20 = (bf16[4,72,1792]{2,1,0:T(8,128)(2,1)}, bf16[4,72,1792]{2,1,0:T(8,128)(2,1)}, u32[]{:S(2)}, u32[]{:S(2)}) collective-permute-start(bf16[4,72,1792]{2,1,0:T(8,128)(2,1)} %dynamic-slice_bitcast_fusion), channel_id=1, source_target_pairs={{0,16},{8,24},{16,0},{24,8},{1,17},{9,25},{17,1},{25,9},{2,18},{10... | collective-permute-start | bytes 3096584 | tf_op jit(solution)/shard_map/ppermute | solution.py:619
  675.6 15.6 %collective-permute-start.28 = (bf16[1,72,1792]{2,1,0:T(8,128)(2,1)S(1)}, bf16[1,72,1792]{2,1,0:T(8,128)(2,1)S(1)}, u32[]{:S(2)}, u32[]{:S(2)}) collective-permute-start(bf16[1,72,1792]{2,1,0:T(8,128)(2,1)S(1)} %add_convert_fusion.2), channel_id=1, source_target_pairs={{0,1},{1,0},{2,3},{3,2},{4,5},{5,4},{6,7},{7,6},{8,9},{9,8},{10,11... | collective-permute-start | bytes 774152 | tf_op jit(solution)/shard_map/ppermute | solution.py:619
  676.2 15.4 %collective-permute-start.25 = (bf16[1,72,1792]{2,1,0:T(8,128)(2,1)S(1)}, bf16[1,72,1792]{2,1,0:T(8,128)(2,1)S(1)}, u32[]{:S(2)}, u32[]{:S(2)}) collective-permute-start(bf16[1,72,1792]{2,1,0:T(8,128)(2,1)S(1)} %get-tuple-element.314), channel_id=1, source_target_pairs={{0,2},{2,4},{4,6},{6,0},{1,3},{3,5},{5,7},{7,1},{8,10},{10,12},{12... | collective-permute-start | bytes 774152 | tf_op jit(solution)/shard_map/ppermute | solution.py:624
  676.6 15.9 %collective-permute-start.27 = (bf16[1,72,1792]{2,1,0:T(8,128)(2,1)S(1)}, bf16[1,72,1792]{2,1,0:T(8,128)(2,1)S(1)}, u32[]{:S(2)}, u32[]{:S(2)}) collective-permute-start(bf16[1,72,1792]{2,1,0:T(8,128)(2,1)S(1)} %get-tuple-element.315), channel_id=1, source_target_pairs={{0,6},{2,0},{4,2},{6,4},{1,7},{3,1},{5,3},{7,5},{8,14},{10,8},{12,... | collective-permute-start | bytes 774152 | tf_op jit(solution)/shard_map/ppermute | solution.py:624
  680.0 19.9 %collective-permute-start.26 = (bf16[1,72,1792]{2,1,0:T(8,128)(2,1)S(1)}, bf16[1,72,1792]{2,1,0:T(8,128)(2,1)S(1)}, u32[]{:S(2)}, u32[]{:S(2)}) collective-permute-start(bf16[1,72,1792]{2,1,0:T(8,128)(2,1)S(1)} %get-tuple-element.316), channel_id=1, source_target_pairs={{0,4},{2,6},{4,0},{6,2},{1,5},{3,7},{5,1},{7,3},{8,12},{10,14},{12... | collective-permute-start | bytes 774152 | tf_op jit(solution)/shard_map/ppermute | solution.py:624
  680.0 22.1 %collective-permute-start.29 = (bf16[1,368,1152]{2,1,0:T(8,128)(2,1)S(1)}, bf16[1,368,1152]{2,1,0:T(8,128)(2,1)S(1)}, u32[]{:S(2)}, u32[]{:S(2)}) collective-permute-start(bf16[1,368,1152]{2,1,0:T(8,128)(2,1)S(1)} %copy-done.31), channel_id=1, source_target_pairs={{0,1},{1,0},{2,3},{3,2},{4,5},{5,4},{6,7},{7,6},{8,9},{9,8},{10,11... | collective-permute-start | bytes 2543624 | tf_op jit(solution)/shard_map/ppermute | solution.py:619
  691.6 41.4 %collective-permute-start.40 = (bf16[1,361,1152]{2,1,0:T(8,128)(2,1)}, bf16[1,361,1152]{2,1,0:T(8,128)(2,1)S(1)}, u32[]{:S(2)}, u32[]{:S(2)}) collective-permute-start(bf16[1,361,1152]{2,1,0:T(8,128)(2,1)} %get-tuple-element.294), channel_id=1, source_target_pairs={{0,1},{1,0},{2,3},{3,2},{4,5},{5,4},{6,7},{7,6},{8,9},{9,8},{10,11... | collective-permute-start | bytes 2495240 | tf_op jit(solution)/shard_map/ppermute | solution.py:619
  719.3 13.7 %collective-permute-start.39 = (f32[112,128]{1,0:T(8,128)S(1)}, f32[112,128]{1,0:T(8,128)S(1)}, u32[]{:S(2)}, u32[]{:S(2)}) collective-permute-start(f32[112,128]{1,0:T(8,128)S(1)} %add_add_fusion.1), channel_id=1, source_target_pairs={{0,6},{2,4},{4,2},{6,0},{1,7},{3,5},{5,3},{7,1},{8,14},{10,12},{12... | collective-permute-start | bytes 172040 | tf_op jit(solution)/shard_map/ppermute | solution.py:757
  (49 other events, 606.4 us)
Sparse Core Ops, SparseCore 0:
  39.5 119.2 all-gather.2
  162.2 84.9 all-gather.4
  269.1 169.9 reduce-scatter.2
  459.3 181.3 reduce-scatter.4
